TPU v7x, 512 devices: a whole 4x8x8 slice. The times are simulated.
512 devices in a mesh: row: 16 (over x, z_lo), col: 32 (over y, z_hi, core).
Axes of the slice: x: 4, y: 8, z: 8 (z_hi: 2, z_lo: 4; z = z_hi * 4 + z_lo), core: 2. Of those that a mesh axis runs over, the one named last changes fastest.
Arguments:
- out_grads: bfloat16 [896, 8192], P('row', 'col'), may hold values from -6 to 6
- inputs: bfloat16 [896, 8192], P('col', 'row'), may hold values from -6 to 6
- basis_out: bfloat16 [8192, 8192], P('col', 'row'), may hold values from -0.0625 to 0.0625
- basis_in: bfloat16 [8192, 8192], P('row', 'col'), may hold values from -0.0625 to 0.0625
- eig_out: float32 [8192], P('row'), may hold values from 0.05 to 5
- eig_in: float32 [8192], P('col'), may hold values from 0.05 to 5
- pair_order: int32 [896], replicated, may hold values from 0 to 895, each once
- length_bucket: int32 [896], replicated, may hold values from 0 to 7
Outputs:
- ihvp: float32 [128, 8192], P('col', 'row')
All inputs are finite; a program needn't handle non-finite values.
Results may differ from a plain program's by a relative error of at most 0.0044.
Values may be sent and summed in bfloat16 or wider, within the bound.
No kernel may reach another device: no remote copies, remote signals or barrier semaphores. Data moves between devices by JAX's collectives and lax.ppermute only.
A program may use at most 64 MiB of HBM per device.

v0:
```python
import jax
import jax.numpy as jnp
from jax import lax
from jax.sharding import PartitionSpec as P

OUT = 128


DAMPING = 0.1


def shards(out_grads, inputs, basis_out, basis_in, eig_out, eig_in, pair_order, length_bucket):
    pair_total = pair_order.shape[0]
    positions = (
        jnp.zeros((pair_total,), jnp.int32)
        .at[pair_order]
        .set(jnp.arange(pair_total, dtype=jnp.int32))
    )
    pair_signs = jnp.where(positions % 2 == 0, 1.0, -1.0).astype(jnp.float32)
    weights = pair_signs / jnp.sqrt((1.0 + length_bucket.astype(jnp.float32)) * pair_total)
    partial_out = jnp.dot(
        lax.all_gather(out_grads, "row", axis=0, tiled=True),
        basis_out,
        preferred_element_type=jnp.float32,
    )
    share_rows = pair_total // lax.axis_size("col")
    share_start = lax.axis_index("col") * share_rows
    share_weights = lax.dynamic_slice_in_dim(weights, share_start, share_rows, 0)
    summed_share = lax.psum_scatter(partial_out, "col", scatter_dimension=0, tiled=True)
    rot_share = (summed_share * share_weights[:, None]).astype(jnp.bfloat16)
    rot_out = lax.all_gather(rot_share, "col", axis=0, tiled=True)
    partial_in = jnp.dot(
        lax.all_gather(inputs, "col", axis=0, tiled=True),
        basis_in,
        preferred_element_type=jnp.float32,
    )
    rot_in = lax.psum(partial_in, "row").astype(jnp.bfloat16)
    middle = lax.dot_general(
        rot_out, rot_in, (((0,), (0,)), ((), ())), preferred_element_type=jnp.float32
    )
    scaled = (middle / (eig_out[:, None] * eig_in[None, :] + DAMPING)).astype(jnp.bfloat16)
    slab_block = OUT // lax.axis_size("col")
    chosen = basis_out[:slab_block]
    partial_left = jnp.dot(
        lax.all_gather(chosen, "col", axis=0, tiled=True),
        scaled,
        preferred_element_type=jnp.float32,
    )
    left_part = lax.psum_scatter(partial_left, "row", scatter_dimension=0, tiled=True).astype(
        jnp.bfloat16
    )
    final_terms = lax.dot_general(
        lax.all_gather(left_part, "row", axis=0, tiled=True),
        basis_in,
        (((1,), (1,)), ((), ())),
        preferred_element_type=jnp.float32,
    )
    return lax.psum_scatter(final_terms, "col", scatter_dimension=0, tiled=True)


def solution(mesh):
    return jax.shard_map(
        shards,
        mesh=mesh,
        in_specs=(
            P("row", "col"),
            P("col", "row"),
            P("col", "row"),
            P("row", "col"),
            P("row"),
            P("col"),
            P(),
            P(),
        ),
        out_specs=P("col", "row"),
        check_vma=False,
    )
```

profile of v0, /device:TPU:1, one launch (start us, length us, event | category | flops | bytes accessed | tf_op | source)
XLA Modules:
  0.0 911.3 jit_solution(4887998539403810276)
XLA Ops:
  6.5 42.7 %all_gather.15 = bf16[896,256]{1,0:T(8,128)(2,1)S(1)} all-gather(bf16[56,256]{1,0:T(8,128)(2,1)} %param.8), channel_id=1, replica_groups=mesh['row'=16,'col'=32] {'row'}, dimensions={0}, use_global_device_ids=true | all-gather | bytes 487424 | tf_op jit(solution)/shard_map/all_gather | solution.py:22
  49.3 1.4 fusion.19
  50.6 107.2 %fusion = f32[32,512]{1,0:T(8,128)S(1)} fusion(f32[896,512]{1,0:T(8,128)S(1)} %fusion.19), kind=kCustom, calls=%all-reduce-scatter | all-reduce-scatter fusion | flops 524289 | bytes 1902592
  157.9 6.5 collective-permute-start
  164.4 1.3 collective-permute-start.1
  165.7 1.3 collective-permute-start.2
  167.0 1.9 collective-permute-start.3
  168.9 0.7 slice_bitcast_fusion
  169.6 67.3 %all-gather.1 = bf16[32,28,512]{2,1,0:T(8,128)(2,1)S(1)} all-gather(bf16[1,28,512]{2,1,0:T(8,128)(2,1)S(1)} %bitcast.20), channel_id=1, replica_groups=mesh['row'=16,'col'=32] {'col'}, dimensions={0}, use_global_device_ids=true | all-gather | bytes 946176 | tf_op jit(solution)/shard_map/all_gather | solution.py:33
  236.9 0.2 reshape.15
  237.1 0.0 copy-start.4
  237.2 0.4 fusion.20
  237.6 83.5 %all-reduce.7 = bf16[896,256]{1,0:T(8,128)(2,1)S(1)} all-reduce(f32[896,256]{1,0:T(8,128)S(1)} %fusion.20), channel_id=1, replica_groups=mesh['row'=16,'col'=32] {'row'}, use_global_device_ids=true, to_apply=%region_2.3 | all-reduce | flops 229376 | bytes 1376256 | tf_op jit(solution)/shard_map/psum | solution.py:37
  321.1 5.3 scatter_custom_fusion
  326.4 60.4 %all-gather.2 = bf16[32,4,512]{2,1,0:T(4,128)(2,1)S(1)} all-gather(bf16[1,4,512]{2,1,0:T(4,128)(2,1)S(1)} %slice_bitcast_fusion), channel_id=1, replica_groups=mesh['row'=16,'col'=32] {'col'}, dimensions={0}, use_global_device_ids=true | all-gather | bytes 135168 | tf_op jit(solution)/shard_map/all_gather | solution.py:45
  386.8 0.1 dynamic_slice.3
  386.9 0.6 fusion.18
  388.2 0.6 concatenate
  388.8 0.1 fusion.12
  388.9 53.0 %all-gather = bf16[32,28,512]{2,1,0:T(8,128)(2,1)S(1)} all-gather(bf16[1,28,512]{2,1,0:T(8,128)(2,1)S(1)} %fusion.12), channel_id=1, replica_groups=mesh['row'=16,'col'=32] {'col'}, dimensions={0}, use_global_device_ids=true | all-gather | bytes 946176 | tf_op jit(solution)/shard_map/all_gather | solution.py:31
  441.9 0.2 reshape.13
  442.1 0.7 fusion.3
  442.8 0.8 copy.11
  443.6 0.0 reduce-scatter.6.cloned.1.call-update
  443.6 0.0 all-reduce.6.cloned.1.call-start
  443.7 67.7 %reduce-scatter.6.cloned.1.call-done = f32[8,256]{1,0:T(8,128)} async-done(((f32[128,256]{1,0:T(8,128)}), f32[8,256]{1,0:T(8,128)}) %reduce-scatter.6.cloned.1.call-update) | async-done | bytes 8208 | tf_op jit(solution)/shard_map/reduce_scatter | solution.py:49
  511.4 0.7 convert_element_type.19
  512.1 30.6 %all_gather.19 = bf16[128,256]{1,0:T(8,128)(2,1)S(1)} all-gather(bf16[8,256]{1,0:T(8,128)(2,1)S(1)} %convert_element_type.19), channel_id=1, replica_groups=mesh['row'=16,'col'=32] {'row'}, dimensions={0}, use_global_device_ids=true | all-gather | bytes 69632 | tf_op jit(solution)/shard_map/all_gather | solution.py:53
  542.7 0.9 fusion.21
  543.6 0.0 all-reduce.6.cloned.1.call-update
  544.3 358.8 %all-reduce.6.cloned.1.call-done = f32[128,512]{1,0:T(8,128)} async-done(((f32[128,512]{1,0:T(8,128)}), f32[128,512]{1,0:T(8,128)}) %all-reduce.6.cloned.1.call-update) | async-done | bytes 262160
  903.1 1.3 constant_dynamic-slice_fusion
  (23 shorter events, 0.1 us)
Async XLA Ops:
  6.5 230.6 %copy-start = (bf16[512,256]{1,0:T(8,128)(2,1)S(1)}, bf16[512,256]{1,0:T(8,128)(2,1)}, u32[]{:S(2)}) copy-start(bf16[512,256]{1,0:T(8,128)(2,1)} %param.11) | copy-start | bytes 786436
  6.5 504.8 %reduce-scatter.6.cloned.1.call-start = ((), (), s32[]{:S(2)}) async-start(), calls=%async_computation.1 | async-start | bytes 139264 | tf_op jit(solution)/shard_map/reduce_scatter | solution.py:49
  49.3 120.3 %copy-start.3 = (s32[896]{0:T(1024)S(1)}, s32[896]{0:T(1024)}, u32[]{:S(2)}) copy-start(s32[896]{0:T(1024)} %param.14) | copy-start | bytes 10756
  49.3 120.3 %copy-start.1 = (bf16[28,512]{1,0:T(8,128)(2,1)S(1)}, bf16[28,512]{1,0:T(8,128)(2,1)}, u32[]{:S(2)}) copy-start(bf16[28,512]{1,0:T(8,128)(2,1)} %param.9) | copy-start | bytes 86020
  157.9 230.3 %collective-permute-start = (f32[32,512]{1,0:T(8,128)S(1)}, f32[32,512]{1,0:T(8,128)S(1)}, u32[]{:S(2)}, u32[]{:S(2)}) collective-permute-start(f32[32,512]{1,0:T(8,128)S(1)} %fusion), channel_id=1, source_target_pairs={{0,1},{1,2},{2,3},{3,4},{4,5},{5,6},{6,7},{7,8},{8,9},{9,10},{10,1... | collective-permute-start | bytes 196616
  164.4 223.8 %collective-permute-start.1 = (f32[32,512]{1,0:T(8,128)S(1)}, f32[32,512]{1,0:T(8,128)S(1)}, u32[]{:S(2)}, u32[]{:S(2)}) collective-permute-start(f32[32,512]{1,0:T(8,128)S(1)} %fusion), channel_id=1, source_target_pairs={{0,2},{1,3},{2,4},{3,5},{4,6},{5,7},{6,8},{7,9},{8,10},{9,11},{10,... | collective-permute-start | bytes 196616
  165.7 222.5 %collective-permute-start.2 = (f32[32,512]{1,0:T(8,128)S(1)}, f32[32,512]{1,0:T(8,128)S(1)}, u32[]{:S(2)}, u32[]{:S(2)}) collective-permute-start(f32[32,512]{1,0:T(8,128)S(1)} %fusion), channel_id=1, source_target_pairs={{0,3},{1,4},{2,5},{3,6},{4,7},{5,8},{6,9},{7,10},{8,11},{9,12},{10... | collective-permute-start | bytes 196616
  167.0 221.1 %collective-permute-start.3 = (f32[28,512]{1,0:T(8,128)S(1)}, f32[28,512]{1,0:T(8,128)S(1)}, u32[]{:S(2)}, u32[]{:S(2)}) collective-permute-start(f32[28,512]{1,0:T(8,128)S(1)} %slice.4), channel_id=1, source_target_pairs={{0,4},{1,5},{2,6},{3,7},{4,8},{5,9},{6,10},{7,11},{8,12},{9,13},{1... | collective-permute-start | bytes 172040
  237.1 89.3 %copy-start.2 = (s32[896]{0:T(1024)S(1)}, s32[896]{0:T(1024)}, u32[]{:S(2)}) copy-start(s32[896]{0:T(1024)} %param.15) | copy-start | bytes 10756
  237.1 149.8 %copy-start.4 = (u32[512]{0:T(512)S(1)}, u32[512]{0:T(512)}, u32[]{:S(2)}) copy-start(u32[512]{0:T(512)} %constant.39) | copy-start | bytes 6148
  388.1 54.0 %copy-start.5 = (f32[512]{0:T(512)S(1)}, f32[512]{0:T(512)}, u32[]{:S(2)}) copy-start(f32[512]{0:T(512)} %param.12) | copy-start | bytes 6148
  388.1 54.0 %copy-start.6 = (f32[256]{0:T(256)S(1)}, f32[256]{0:T(256)}, u32[]{:S(2)}) copy-start(f32[256]{0:T(256)} %param.13) | copy-start | bytes 3076
  443.6 459.5 %all-reduce.6.cloned.1.call-start = ((), (), s32[]{:S(2)}) async-start(), calls=%async_computation.2 | async-start | bytes 524288
Sparse Core Ops, SparseCore 0:
  443.8 67.5 reduce-scatter.5
  543.8 359.2 all-reduce.5
where the time goes:
time: 912 us; the launch traced here: 911 us
  blocking collectives  445 us (49%)
  waiting for transfers between devices  427 us (47%)
  between operations  14.9 us (2%)
  starting transfers between devices  11 us (1%)
  local copies, waits for them, and re-layouts  9.76 us (1%)
    unnamed x7, waiting for transfers between devices  359 us
    unnamed x1, blocking collectives  107 us
    psum x1, blocking collectives, shards(): rot_in = lax.psum(partial_in, 'row').astype(jnp.bfloat16)  83.5 us
    reduce_scatter x1, waiting for transfers between devices, shards(): lax.psum_scatter(partial_left, 'row', scatter_dimension=0, tiled=True)  67.7 us
    all_gather x1, blocking collectives, shards(): lax.all_gather(inputs, 'col', axis=0, tiled=True)  67.3 us
    all_gather x1, blocking collectives, shards(): lax.all_gather(chosen, 'col', axis=0, tiled=True)  60.4 us
    all_gather x1, blocking collectives, shards(): rot_out = lax.all_gather(rot_share, 'col', axis=0, tiled=True)  53 us
    all_gather x1, blocking collectives, shards(): lax.all_gather(out_grads, 'row', axis=0, tiled=True)  42.7 us
  transfers between devices with their start and end apart: 6, of which 2 were waited for; matrix products, arithmetic and copies ran while one was open for 1% of the time, Pallas kernels for 0%

commit v1 on v0

v1 whole, which is shorter than its diff:
```python
import jax
import jax.numpy as jnp
from jax import lax
from jax.sharding import Mesh, PartitionSpec as P

DAMPING = 0.1
PAD = 32
ROW = ("x", "zl")
COL = ("y", "zh")
BF = jnp.bfloat16
F32 = jnp.float32


def dot(a, b, contract):
    return lax.dot_general(a, b, (contract, ((), ())), preferred_element_type=F32)


def gather(block, axes):
    size = lax.axis_size(axes)
    copies = jnp.broadcast_to(block[None], (size, *block.shape))
    return lax.all_to_all(copies, axes, 0, 0, tiled=True)


def scatter_sum(terms, axes):
    size = lax.axis_size(axes)
    parts = terms.astype(BF).reshape(size, -1, terms.shape[-1])
    return jnp.sum(lax.all_to_all(parts, axes, 0, 0, tiled=True).astype(F32), axis=0)


def shards(out_grads, inputs, basis_out, basis_in, eig_out, eig_in, pair_order, length_bucket):
    tokens = pair_order.shape[0]
    share = inputs.shape[0]
    blocks = tokens // (2 * share)
    slab_rows = PAD - share
    core = lax.axis_index("core")
    zh = lax.axis_index("zh")

    row = lax.broadcasted_iota(jnp.int32, (blocks, PAD), 1)
    token = (2 * lax.broadcasted_iota(jnp.int32, (blocks, PAD), 0) + core) * share + row
    token = jnp.where(row < share, token, -1).reshape(1, blocks * PAD)
    hit = pair_order[:, None] == token
    place = lax.broadcasted_iota(jnp.int32, (tokens, 1), 0)
    sign = jnp.sum(jnp.where(hit, jnp.where(place % 2 == 0, 1.0, -1.0), 0.0), axis=0)
    own_bucket = jnp.sum(
        jnp.where(lax.broadcasted_iota(jnp.int32, (tokens, 1), 0) == token, length_bucket[:, None], 0), axis=0
    )
    weights = sign / jnp.sqrt((1.0 + own_bucket.astype(F32)) * tokens)

    in_rows = jnp.concatenate([inputs, basis_out[:slab_rows]], axis=0)
    in_far = lax.ppermute(in_rows, "zh", [(0, 1), (1, 0)])
    grads = lax.all_to_all(out_grads, "core", 0, 1, tiled=True)
    grads = jnp.pad(grads, ((0, slab_rows), (0, 0)))
    basis_out2 = lax.all_gather(basis_out, "core", axis=0, tiled=True)
    basis_in2 = lax.all_gather(basis_in, "core", axis=0)
    eig_in2 = lax.all_gather(eig_in, "core", axis=0, tiled=True)

    grads_all = gather(grads, ROW).reshape(-1, grads.shape[1])
    part_out = dot(basis_out2, grads_all, ((0,), (1,)))

    in_pair = jnp.stack([jnp.where(zh == 0, in_rows, in_far), jnp.where(zh == 0, in_far, in_rows)])
    in_all = gather(in_pair, "y").reshape(blocks, PAD, -1)
    slab = in_all[:, share:].reshape(blocks * slab_rows, -1)
    in_all = in_all.reshape(blocks * PAD, -1)
    part_in = jnp.concatenate([dot(basis_in2[k], in_all, ((0,), (1,))) for k in range(2)])

    sum_out = scatter_sum(part_out, "y")
    sum_out = sum_out + lax.ppermute(sum_out, "zh", [(0, 1), (1, 0)])
    rot_in = scatter_sum(part_in, ROW).astype(BF)
    rot_out = (sum_out * weights).astype(BF)
    rot_out = gather(rot_out, "y").reshape(-1, blocks * PAD)
    rot_in = gather(rot_in, ROW).reshape(-1, blocks * PAD)
    rot_out = lax.all_gather(rot_out, "core", axis=0)
    rot_in = lax.all_gather(rot_in, "core", axis=0)
    middle = sum(dot(rot_out[k], rot_in[k], ((1,), (1,))) for k in range(2))
    scaled = (middle / (eig_out[:, None] * eig_in2[None, :] + DAMPING)).astype(BF)

    left = dot(slab, scaled, ((1,), (0,)))
    for axis in ROW:
        left = jnp.sum(gather(left.astype(BF), axis).astype(F32), axis=0)
    left = left.astype(BF)
    half = basis_in.shape[1]
    final = sum(
        dot(left[:, k * half : (k + 1) * half], basis_in2[k], ((1,), (1,))) for k in range(2)
    )
    return scatter_sum(final, COL)


def solution(mesh):
    fine = Mesh(mesh.devices.reshape(4, 4, 8, 2, 2), ("x", "zl", "y", "zh", "core"))
    row, col = ROW, (*COL, "core")
    return jax.shard_map(
        shards,
        mesh=fine,
        in_specs=(P(row, col), P(col, row), P(col, row), P(row, col), P(row), P(col), P(), P()),
        out_specs=P(col, row),
        check_vma=False,
    )
```

time: 912 us -> 230 us (0.25)
  blocking collectives: 445 us -> 69.9 us
  waiting for transfers between devices: 427 us -> 82.5 us
  starting transfers between devices: 11 us -> 44.3 us
    unnamed x7 -> x2, waiting for transfers between devices: 359 us -> 0.03 us
    all_gather x5 -> x3, blocking collectives: 254 us -> 10.7 us  [the longest x1 5 us: shards(): eig_in2 = lax.all_gather(eig_in, 'core', axis=0, tiled=True)]
    unnamed x1 -> x0, blocking collectives: 107 us -> none
    psum x1 -> x0, blocking collectives: 83.5 us -> none  [shards(): rot_in = lax.psum(partial_in, 'row').astype(jnp.bfloat16)]
    all_to_all x0 -> x6, waiting for transfers between devices: none -> 75.2 us  [the longest x3 47.9 us: gather(): return lax.all_to_all(copies, axes, 0, 0, tiled=True)]
    reduce_scatter x1 -> x0, waiting for transfers between devices: 67.7 us -> none  [shards(): lax.psum_scatter(partial_left, 'row', scatter_dimension=0, tiled=True)]
    all_to_all x0 -> x4, blocking collectives: none -> 59.2 us  [the longest x3 37.7 us: gather(): return lax.all_to_all(copies, axes, 0, 0, tiled=True)]
    all_to_all x0 -> x6, starting transfers between devices: none -> 30.8 us  [the longest x3 19.1 us: gather(): return lax.all_to_all(copies, axes, 0, 0, tiled=True)]
  transfers between devices with their start and end apart: 6 -> 10, of which waited for: 2 -> 7; matrix products, arithmetic and copies ran while one was open for 1% -> 2% of each run, Pallas kernels for 0% -> 0%
where the time goes in v1:
time: 230 us; the launch traced here: 226 us
  waiting for transfers between devices  82.5 us (36%)
  blocking collectives  69.9 us (30%)
  starting transfers between devices  44.3 us (19%)
  between operations  13.7 us (6%)
  local copies, waits for them, and re-layouts  5.79 us (3%)
  matrix products  5.71 us (2%)
  other arithmetic  4.01 us (2%)
    all_to_all x3, waiting for transfers between devices, gather(): return lax.all_to_all(copies, axes, 0, 0, tiled=True)  47.9 us
    all_to_all x3, blocking collectives, gather(): return lax.all_to_all(copies, axes, 0, 0, tiled=True)  37.7 us
    all_to_all x2, waiting for transfers between devices, scatter_sum(): lax.all_to_all(parts, axes, 0, 0, tiled=True).astype(F32)  27 us
    all_to_all x1, blocking collectives, scatter_sum(): lax.all_to_all(parts, axes, 0, 0, tiled=True).astype(F32)  21.5 us
    all_to_all x3, starting transfers between devices, gather(): return lax.all_to_all(copies, axes, 0, 0, tiled=True)  19.1 us
    ppermute x1, starting transfers between devices, shards(): in_far = lax.ppermute(in_rows, 'zh', [(0, 1), (1, 0)])  11.5 us
    all_to_all x2, starting transfers between devices, scatter_sum(): lax.all_to_all(parts, axes, 0, 0, tiled=True).astype(F32)  7.49 us
    all_gather x1, waiting for transfers between devices, shards(): rot_out = lax.all_gather(rot_out, 'core', axis=0)  7.25 us
  transfers between devices with their start and end apart: 10, of which 7 were waited for; matrix products, arithmetic and copies ran while one was open for 2% of the time, Pallas kernels for 0%

profile of v1, /device:TPU:1, one launch (start us, length us, event | category | flops | bytes accessed | tf_op | source)
XLA Modules:
  0.0 225.9 jit_solution(3682693902234508102)
XLA Ops:
  7.2 0.8 pad_maximum_fusion.2
  8.0 11.5 %collective-permute-start = (bf16[32,512]{1,0:T(8,128)(2,1)S(1)}, bf16[32,512]{1,0:T(8,128)(2,1)S(1)}, u32[]{:S(2)}, u32[]{:S(2)}) collective-permute-start(bf16[32,512]{1,0:T(8,128)(2,1)S(1)} %pad_maximum_fusion.2), channel_id=1, source_target_pairs={{0,2},{2,0},{1,3},{3,1},{4,6},{6,4},{5,7},{7,5},{8,10},{10,8},{9,1... | collective-permute-start | bytes 98312 | tf_op jit(solution)/shard_map/ppermute | solution.py:50
  19.5 1.4 all_to_all.42
  20.8 4.2 %all-to-all-start.1 = ((bf16[2,28,256]{2,1,0:T(8,128)(2,1)}), bf16[2,28,256]{2,1,0:T(8,128)(2,1)S(1)}, u32[]{:S(2)}, u32[]{:S(2)}) async-start(bf16[2,28,256]{2,1,0:T(8,128)(2,1)} %all_to_all.42), calls=%async_computation.1 | async-start | bytes 65536 | tf_op jit(solution)/shard_map/all_to_all | solution.py:51
  25.0 0.8 select_bitcast_fusion.1
  26.1 0.9 broadcast_in_dim.48
  26.9 6.8 %all-to-all-start = ((bf16[8,2,32,512]{3,2,1,0:T(8,128)(2,1)}), bf16[8,2,32,512]{3,2,1,0:T(8,128)(2,1)S(1)}, u32[]{:S(2)}, u32[]{:S(2)}) async-start(bf16[8,2,32,512]{3,2,1,0:T(8,128)(2,1)} %broadcast_in_dim.48), calls=%async_computation | async-start | bytes 1048576 | tf_op jit(solution)/shard_map/all_to_all | solution.py:21
  33.9 17.8 %all-to-all-done = bf16[8,2,32,512]{3,2,1,0:T(8,128)(2,1)S(1)} async-done(((bf16[8,2,32,512]{3,2,1,0:T(8,128)(2,1)}), bf16[8,2,32,512]{3,2,1,0:T(8,128)(2,1)S(1)}, u32[]{:S(2)}, u32[]{:S(2)}) %all-to-all-start) | async-done | bytes 524320 | tf_op jit(solution)/shard_map/all_to_all | solution.py:21
  51.7 0.9 broadcast_in_dim.49
  52.6 6.9 %all-to-all-start.2 = ((bf16[16,32,512]{2,1,0:T(8,128)(2,1)}), bf16[16,32,512]{2,1,0:T(8,128)(2,1)S(1)}, u32[]{:S(2)}, u32[]{:S(2)}) async-start(bf16[16,32,512]{2,1,0:T(8,128)(2,1)} %broadcast_in_dim.49), calls=%async_computation.2 | async-start | bytes 1048576 | tf_op jit(solution)/shard_map/all_to_all | solution.py:21
  59.4 2.6 %all-gather = bf16[1024,256]{1,0:T(8,128)(2,1)S(1)} all-gather(bf16[512,256]{1,0:T(8,128)(2,1)S(1)} %copy-done.2), channel_id=2, replica_groups=mesh['x'=4,'zl'=4,'y'=8,'zh'=2,'core'=2] {'core'}, dimensions={0}, use_global_device_ids=true | all-gather | bytes 786432 | tf_op jit(solution)/shard_map/all_gather | solution.py:54
  62.7 0.8 pad_maximum_fusion
  63.6 11.6 %all-to-all-done.2 = bf16[16,32,512]{2,1,0:T(8,128)(2,1)S(1)} async-done(((bf16[16,32,512]{2,1,0:T(8,128)(2,1)}), bf16[16,32,512]{2,1,0:T(8,128)(2,1)S(1)}, u32[]{:S(2)}, u32[]{:S(2)}) %all-to-all-start.2) | async-done | bytes 524320 | tf_op jit(solution)/shard_map/all_to_all | solution.py:21
  75.2 4.0 %all-to-all-start.5 = ((bf16[16,32,512]{2,1,0:T(8,128)(2,1)}), bf16[16,32,512]{2,1,0:T(8,128)(2,1)S(1)}, u32[]{:S(2)}, u32[]{:S(2)}) async-start(bf16[16,32,512]{2,1,0:T(8,128)(2,1)} %bitcast.12), calls=%async_computation.5 | async-start | bytes 1048576 | tf_op jit(solution)/shard_map/all_to_all | solution.py:27
  79.2 3.1 %all_gather.18 = bf16[512,512]{1,0:T(8,128)(2,1)S(1)} all-gather(bf16[256,512]{1,0:T(8,128)(2,1)S(1)} %copy-done.1), channel_id=1, replica_groups=mesh['x'=4,'zl'=4,'y'=8,'zh'=2,'core'=2] {'core'}, dimensions={0}, use_global_device_ids=true | all-gather | bytes 786432 | tf_op jit(solution)/shard_map/all_gather | solution.py:53
  82.3 1.3 convolution_convert_fusion
  83.6 11.3 %all-to-all-done.5 = bf16[16,32,512]{2,1,0:T(8,128)(2,1)S(1)} async-done(((bf16[16,32,512]{2,1,0:T(8,128)(2,1)}), bf16[16,32,512]{2,1,0:T(8,128)(2,1)S(1)}, u32[]{:S(2)}, u32[]{:S(2)}) %all-to-all-start.5) | async-done | bytes 524320 | tf_op jit(solution)/shard_map/all_to_all | solution.py:27
  94.9 3.5 %all-to-all-start.3 = ((bf16[8,64,512]{2,1,0:T(8,128)(2,1)}), bf16[8,64,512]{2,1,0:T(8,128)(2,1)S(1)}, u32[]{:S(2)}, u32[]{:S(2)}) async-start(bf16[8,64,512]{2,1,0:T(8,128)(2,1)} %bitcast.6), calls=%async_computation.3 | async-start | bytes 1048576 | tf_op jit(solution)/shard_map/all_to_all | solution.py:27
  98.5 15.7 %all-to-all-done.3 = bf16[8,64,512]{2,1,0:T(8,128)(2,1)S(1)} async-done(((bf16[8,64,512]{2,1,0:T(8,128)(2,1)}), bf16[8,64,512]{2,1,0:T(8,128)(2,1)S(1)}, u32[]{:S(2)}, u32[]{:S(2)}) %all-to-all-start.3) | async-done | bytes 524320 | tf_op jit(solution)/shard_map/all_to_all | solution.py:27
  114.2 0.9 broadcast_in_dim.87
  115.1 5.4 %all-to-all-start.6 = ((bf16[16,32,512]{2,1,0:T(8,128)(2,1)}), bf16[16,32,512]{2,1,0:T(8,128)(2,1)S(1)}, u32[]{:S(2)}, u32[]{:S(2)}) async-start(bf16[16,32,512]{2,1,0:T(8,128)(2,1)} %broadcast_in_dim.87), calls=%async_computation.6 | async-start | bytes 1048576 | tf_op jit(solution)/shard_map/all_to_all | solution.py:21
  121.5 1.9 collective-permute-start.1
  123.4 18.5 %all-to-all-done.6 = bf16[16,32,512]{2,1,0:T(8,128)(2,1)S(1)} async-done(((bf16[16,32,512]{2,1,0:T(8,128)(2,1)}), bf16[16,32,512]{2,1,0:T(8,128)(2,1)S(1)}, u32[]{:S(2)}, u32[]{:S(2)}) %all-to-all-start.6) | async-done | bytes 524320 | tf_op jit(solution)/shard_map/all_to_all | solution.py:21
  141.9 0.8 copy-done
  142.9 18.0 %all_to_all.64 = bf16[8,64,512]{2,1,0:T(8,128)(2,1)} all-to-all(bf16[8,64,512]{2,1,0:T(8,128)(2,1)S(1)} %broadcast_in_dim.86), channel_id=1, replica_groups=mesh['x'=4,'zl'=4,'y'=8,'zh'=2,'core'=2] {'y'}, dimensions={0} | all-to-all | bytes 1048576 | tf_op jit(solution)/shard_map/all_to_all | solution.py:21
  160.9 5.0 %all-gather.1 = f32[2,1,256]{2,1,0:T(1,128)S(1)} all-gather(f32[1,1,256]{2,1,0:T(1,128)S(1)} %bitcast.52), channel_id=1, replica_groups=mesh['x'=4,'zl'=4,'y'=8,'zh'=2,'core'=2] {'core'}, dimensions={0}, use_global_device_ids=true | all-gather | bytes 3072 | tf_op jit(solution)/shard_map/all_gather | solution.py:55
  166.0 7.3 %all-gather.5.cloned.1.call-done = bf16[2,512,512]{2,1,0:T(8,128)(2,1)} async-done(((bf16[1,512,512]{2,1,0:T(8,128)(2,1)}), bf16[2,512,512]{2,1,0:T(8,128)(2,1)}) %all-gather.5.cloned.1.call-update) | async-done | bytes 1048592 | tf_op jit(solution)/shard_map/all_gather | solution.py:72
  173.3 1.7 fusion.9
  175.0 1.7 fusion.5
  176.7 9.1 %all_to_all.65 = bf16[4,64,512]{2,1,0:T(8,128)(2,1)S(1)} all-to-all(bf16[4,64,512]{2,1,0:T(8,128)(2,1)S(1)} %broadcast_in_dim.88), channel_id=1, replica_groups=mesh['x'=4,'zl'=4,'y'=8,'zh'=2,'core'=2] {'x'}, dimensions={0} | all-to-all | bytes 524288 | tf_op jit(solution)/shard_map/all_to_all | solution.py:21
  185.8 10.7 %all_to_all.66 = bf16[4,64,512]{2,1,0:T(8,128)(2,1)S(1)} all-to-all(bf16[4,64,512]{2,1,0:T(8,128)(2,1)S(1)} %broadcast_in_dim.89), channel_id=1, replica_groups=mesh['x'=4,'zl'=4,'y'=8,'zh'=2,'core'=2] {'zl'}, dimensions={0} | all-to-all | bytes 524288 | tf_op jit(solution)/shard_map/all_to_all | solution.py:21
  196.9 21.5 %all_to_all.67 = bf16[16,4,512]{2,1,0:T(4,128)(2,1)S(1)} all-to-all(bf16[16,4,512]{2,1,0:T(4,128)(2,1)S(1)} %reshape.93), channel_id=1, replica_groups=mesh['x'=4,'zl'=4,'y'=8,'zh'=2,'core'=2] {'y','zh'}, dimensions={0} | all-to-all | bytes 131072 | tf_op jit(solution)/shard_map/all_to_all | solution.py:27
  (53 shorter events, 4.2 us)
Async XLA Ops:
  8.0 17.0 %collective-permute-start = (bf16[32,512]{1,0:T(8,128)(2,1)S(1)}, bf16[32,512]{1,0:T(8,128)(2,1)S(1)}, u32[]{:S(2)}, u32[]{:S(2)}) collective-permute-start(bf16[32,512]{1,0:T(8,128)(2,1)S(1)} %pad_maximum_fusion.2), channel_id=1, source_target_pairs={{0,2},{2,0},{1,3},{3,1},{4,6},{6,4},{5,7},{7,5},{8,10},{10,8},{9,1... | collective-permute-start | bytes 98312 | tf_op jit(solution)/shard_map/ppermute | solution.py:50
  20.8 5.2 %all-to-all-start.1 = ((bf16[2,28,256]{2,1,0:T(8,128)(2,1)}), bf16[2,28,256]{2,1,0:T(8,128)(2,1)S(1)}, u32[]{:S(2)}, u32[]{:S(2)}) async-start(bf16[2,28,256]{2,1,0:T(8,128)(2,1)} %all_to_all.42), calls=%async_computation.1 | async-start | bytes 65536 | tf_op jit(solution)/shard_map/all_to_all | solution.py:51
  26.9 24.8 %all-to-all-start = ((bf16[8,2,32,512]{3,2,1,0:T(8,128)(2,1)}), bf16[8,2,32,512]{3,2,1,0:T(8,128)(2,1)S(1)}, u32[]{:S(2)}, u32[]{:S(2)}) async-start(bf16[8,2,32,512]{3,2,1,0:T(8,128)(2,1)} %broadcast_in_dim.48), calls=%async_computation | async-start | bytes 1048576 | tf_op jit(solution)/shard_map/all_to_all | solution.py:21
  33.8 25.7 %copy-start.2 = (bf16[512,256]{1,0:T(8,128)(2,1)S(1)}, bf16[512,256]{1,0:T(8,128)(2,1)}, u32[]{:S(2)}) copy-start(bf16[512,256]{1,0:T(8,128)(2,1)} %param.11) | copy-start | bytes 786436
  52.6 22.6 %all-to-all-start.2 = ((bf16[16,32,512]{2,1,0:T(8,128)(2,1)}), bf16[16,32,512]{2,1,0:T(8,128)(2,1)S(1)}, u32[]{:S(2)}, u32[]{:S(2)}) async-start(bf16[16,32,512]{2,1,0:T(8,128)(2,1)} %broadcast_in_dim.49), calls=%async_computation.2 | async-start | bytes 1048576 | tf_op jit(solution)/shard_map/all_to_all | solution.py:21
  62.7 16.5 %copy-start.1 = (bf16[256,512]{1,0:T(8,128)(2,1)S(1)}, bf16[256,512]{1,0:T(8,128)(2,1)}, u32[]{:S(2)}) copy-start(bf16[256,512]{1,0:T(8,128)(2,1)} %param.10) | copy-start | bytes 786436
  75.2 19.7 %all-to-all-start.5 = ((bf16[16,32,512]{2,1,0:T(8,128)(2,1)}), bf16[16,32,512]{2,1,0:T(8,128)(2,1)S(1)}, u32[]{:S(2)}, u32[]{:S(2)}) async-start(bf16[16,32,512]{2,1,0:T(8,128)(2,1)} %bitcast.12), calls=%async_computation.5 | async-start | bytes 1048576 | tf_op jit(solution)/shard_map/all_to_all | solution.py:27
  94.9 19.4 %all-to-all-start.3 = ((bf16[8,64,512]{2,1,0:T(8,128)(2,1)}), bf16[8,64,512]{2,1,0:T(8,128)(2,1)S(1)}, u32[]{:S(2)}, u32[]{:S(2)}) async-start(bf16[8,64,512]{2,1,0:T(8,128)(2,1)} %bitcast.6), calls=%async_computation.3 | async-start | bytes 1048576 | tf_op jit(solution)/shard_map/all_to_all | solution.py:27
  98.4 22.4 %copy-start.5 = (s32[896]{0:T(1024)S(1)}, s32[896]{0:T(1024)}, u32[]{:S(2)}) copy-start(s32[896]{0:T(1024)} %param.15) | copy-start | bytes 10756
  98.4 22.7 %copy-start.4 = (s32[896]{0:T(1024)S(1)}, s32[896]{0:T(1024)}, u32[]{:S(2)}) copy-start(s32[896]{0:T(1024)} %param.14) | copy-start | bytes 10756
  115.1 26.8 %all-to-all-start.6 = ((bf16[16,32,512]{2,1,0:T(8,128)(2,1)}), bf16[16,32,512]{2,1,0:T(8,128)(2,1)S(1)}, u32[]{:S(2)}, u32[]{:S(2)}) async-start(bf16[16,32,512]{2,1,0:T(8,128)(2,1)} %broadcast_in_dim.87), calls=%async_computation.6 | async-start | bytes 1048576 | tf_op jit(solution)/shard_map/all_to_all | solution.py:21
  120.5 45.5 %all-gather.7.cloned.1.call-start = ((), (), s32[]{:S(2)}) async-start(), calls=%async_computation.11 | async-start | bytes 1572864 | tf_op jit(solution)/shard_map/all_gather | solution.py:73
  121.5 21.3 %collective-permute-start.1 = (f32[64,512]{1,0:T(8,128)S(1)}, f32[64,512]{1,0:T(8,128)S(1)}, u32[]{:S(2)}, u32[]{:S(2)}) collective-permute-start(f32[64,512]{1,0:T(8,128)S(1)} %convert_reduce_fusion), channel_id=1, source_target_pairs={{0,2},{2,0},{1,3},{3,1},{4,6},{6,4},{5,7},{7,5},{8,10},{10,8},{9,1... | collective-permute-start | bytes 393224 | tf_op jit(solution)/shard_map/ppermute | solution.py:67
  141.9 0.8 copy-start
  142.7 30.6 %all-gather.5.cloned.1.call-start = ((), (), s32[]{:S(2)}) async-start(), calls=%async_computation.10 | async-start | bytes 1572864 | tf_op jit(solution)/shard_map/all_gather | solution.py:72
  142.8 18.1 %copy-start.6 = (f32[256]{0:T(256)S(1)}, f32[256]{0:T(256)}, u32[]{:S(2)}) copy-start(f32[256]{0:T(256)} %param.13) | copy-start | bytes 3076
  166.0 9.0 %copy-start.7 = (f32[512]{0:T(512)S(1)}, f32[512]{0:T(512)}, u32[]{:S(2)}) copy-start(f32[512]{0:T(512)} %param.12) | copy-start | bytes 6148
  166.0 8.9 %copy-start.3 = (bf16[2,512,512]{2,1,0:T(8,128)(2,1)S(1)}, bf16[2,512,512]{2,1,0:T(8,128)(2,1)}, u32[]{:S(2)}) copy-start(bf16[2,512,512]{2,1,0:T(8,128)(2,1)} %all-gather.7.cloned.1.call-done) | copy-start | bytes 3145732
Sparse Core Ops, SparseCore 0:
  142.9 9.3 all-gather.6
  161.0 12.2 all-gather.4

commit v2 on v1

v2 whole, which is shorter than its diff:
```python
import jax
import jax.numpy as jnp
import numpy as np
from jax import lax
from jax.sharding import Mesh, PartitionSpec as P

DAMPING = 0.1
PAD = 32
AXES = ("x", "zl", "y", "zh", "core")
SIZES = (4, 4, 8, 2, 2)
BF = jnp.bfloat16
F32 = jnp.float32
SWAP = [(0, 1), (1, 0)]

INDEX = np.arange(512).reshape(16, 16, 2)
ROWS = [INDEX[:, q, :].T.tolist() for q in range(16)]
COLS = [INDEX[r, :, :].T.tolist() for r in range(16)]
ROW_COL = [g[0] for g in ROWS] + [g[1] for g in COLS]
COL_ROW = [g[0] for g in COLS] + [g[1] for g in ROWS]


def dot(a, b, contract):
    return lax.dot_general(a, b, (contract, ((), ())), preferred_element_type=F32)


def exchange(parts, groups):
    return lax.all_to_all(parts, AXES, 0, 0, axis_index_groups=groups, tiled=True)


def copies(block, n):
    return jnp.broadcast_to(block[None], (n, *block.shape))


def shards(out_grads, inputs, basis_out, basis_in, eig_out, eig_in, pair_order, length_bucket):
    tokens, share = pair_order.shape[0], inputs.shape[0]
    n, extra, half = 16, PAD - share, basis_in.shape[1]
    first = lax.axis_index("core") == 0

    row = lax.broadcasted_iota(jnp.int32, (2 * n, PAD), 1)
    token = lax.broadcasted_iota(jnp.int32, (2 * n, PAD), 0) * share + row
    token = jnp.where(row < share, token, -1).reshape(1, 2 * n * PAD)
    place = lax.broadcasted_iota(jnp.int32, (tokens, 1), 0)
    parity = jnp.where(place % 2 == 0, 1.0, -1.0)
    sign = jnp.sum(jnp.where(pair_order[:, None] == token, parity, 0.0), axis=0)
    bucket = jnp.sum(jnp.where(place == token, length_bucket[:, None], 0), axis=0)
    weights = sign / jnp.sqrt((1.0 + bucket.astype(F32)) * tokens)
    weights = jnp.where(first, weights, 1.0)

    in_rows = jnp.concatenate([inputs, basis_out[:extra]], axis=0)
    grads = jnp.pad(out_grads.reshape(2, share, half), ((0, 0), (0, extra), (0, 0)))
    grads = jnp.concatenate([grads[0], grads[1]], axis=1)
    far = lax.ppermute(jnp.where(first, in_rows, grads), "core", SWAP)
    blocks = jnp.stack(
        [
            jnp.where(
                first,
                jnp.concatenate([s[:, k * half : (k + 1) * half] for s in (grads, far)], axis=1),
                (far, in_rows)[k],
            )
            for k in range(2)
        ]
    )
    rows = exchange(copies(blocks.reshape(2 * PAD, -1), n), ROW_COL)
    rows = rows.reshape(2 * n * PAD, -1)

    out_far = lax.ppermute(basis_out, "core", SWAP)
    in_far = lax.ppermute(basis_in, "core", SWAP)
    eig_far = lax.ppermute(eig_in, "core", SWAP)
    basis_in2 = jnp.where(
        first, jnp.concatenate([basis_in, in_far], axis=1), jnp.concatenate([in_far, basis_in], axis=1)
    )
    eig_in2 = jnp.where(first, jnp.concatenate([eig_in, eig_far]), jnp.concatenate([eig_far, eig_in]))
    basis = jnp.where(first, jnp.concatenate([basis_out, out_far], axis=0), basis_in2)

    part = dot(basis, rows, ((0,), (1,))).astype(BF)
    part = exchange(part.reshape(n, -1, part.shape[1]), COL_ROW)
    rot = (jnp.sum(part.astype(F32), axis=0) * weights).astype(BF)
    rot = exchange(copies(rot, n), COL_ROW).reshape(-1, rot.shape[1])

    slabs = rows.reshape(n, 2, PAD, -1)[:, :, share:]
    slabs = [slabs[:, k].reshape(n * extra, -1) for k in range(2)]
    slab = jnp.where(first, lax.ppermute(slabs[0], "core", SWAP), slabs[1])

    middle = dot(rot, lax.ppermute(rot, "core", SWAP), ((1,), (1,)))
    down, across = jnp.where(first, eig_out, eig_in2), jnp.where(first, eig_in2, eig_out)
    scaled = (middle / (down[:, None] * across[None, :] + DAMPING)).astype(BF)
    left = jnp.where(first, dot(slab, scaled, ((1,), (0,))), dot(slab, scaled, ((1,), (1,))))

    left = jnp.sum(lax.all_to_all(copies(left.astype(BF), 4), "x", 0, 0, tiled=True).astype(F32), axis=0)
    left = jnp.sum(lax.all_to_all(copies(left, 4), "zl", 0, 0, tiled=True), axis=0).astype(BF)
    final = dot(left, basis_in2, ((1,), (1,)))
    final = lax.all_to_all(final.reshape(n, -1, final.shape[1]), ("y", "zh"), 0, 0, tiled=True)
    return jnp.sum(final, axis=0)


def solution(mesh):
    fine = Mesh(mesh.devices.reshape(SIZES), AXES)
    row, col = AXES[:2], AXES[2:]
    return jax.shard_map(
        shards,
        mesh=fine,
        in_specs=(P(row, col), P(col, row), P(col, row), P(row, col), P(row), P(col), P(), P()),
        out_specs=P(col, row),
        check_vma=False,
    )
```

time: 230 us -> 171 us (0.74)
  waiting for transfers between devices: 82.5 us -> 40.8 us
  between operations: 13.7 us -> 0.31 us
  starting transfers between devices: 44.3 us -> 53.3 us
  blocking collectives: 69.9 us -> 64.8 us
  local copies, waits for them, and re-layouts: 5.79 us -> 3 us
  matrix products: 5.71 us -> 3.28 us
    all_to_all x6 -> x2, waiting for transfers between devices: 75.2 us -> 37.5 us  [exchange(): lax.all_to_all(parts, AXES, 0, 0, axis_index_groups=groups, tiled=True)]
    ppermute x2 -> x6, starting transfers between devices: 13.4 us -> 37.8 us  [the longest x1 20.7 us: shards(): middle = dot(rot, lax.ppermute(rot, 'core', SWAP), ((1,), (1,)))]
    all_to_all x6 -> x2, starting transfers between devices: 30.8 us -> 15.5 us  [exchange(): lax.all_to_all(parts, AXES, 0, 0, axis_index_groups=groups, tiled=True)]
    all_gather x3 -> x0, blocking collectives: 10.7 us -> none  [the longest x1 5 us: shards(): eig_in2 = lax.all_gather(eig_in, 'core', axis=0, tiled=True)]
    all_gather x2 -> x0, waiting for transfers between devices: 7.27 us -> none  [the longest x1 7.25 us: shards(): rot_out = lax.all_gather(rot_out, 'core', axis=0)]
    all_to_all x4, blocking collectives: 59.2 us -> 64.8 us  [the longest x1 20.8 us: exchange(): lax.all_to_all(parts, AXES, 0, 0, axis_index_groups=groups, tiled=True)]
    ppermute x2 -> x6, waiting for transfers between devices: 0.01 us -> 3.36 us  [the longest x1 1.13 us: shards(): in_far = lax.ppermute(basis_in, 'core', SWAP)]
    dot_general x7 -> x5, matrix products: 5.71 us -> 3.28 us  [dot(): lax.dot_general(a, b, (contract, ((), ())), preferred_element_type=F32)]
  transfers between devices with their start and end apart: 10 -> 8, of which waited for: 7 -> 6; matrix products, arithmetic and copies ran while one was open for 2% -> 1% of each run, Pallas kernels for 0% -> 0%
where the time goes in v2:
time: 171 us; the launch traced here: 169 us
  blocking collectives  64.8 us (38%)
  starting transfers between devices  53.3 us (31%)
  waiting for transfers between devices  40.8 us (24%)
  other arithmetic  3.49 us (2%)
  matrix products  3.28 us (2%)
  local copies, waits for them, and re-layouts  3 us (2%)
    all_to_all x2, waiting for transfers between devices, exchange(): lax.all_to_all(parts, AXES, 0, 0, axis_index_groups=groups, tiled=True)  37.5 us
    all_to_all x1, blocking collectives, exchange(): lax.all_to_all(parts, AXES, 0, 0, axis_index_groups=groups, tiled=True)  20.8 us
    ppermute x1, starting transfers between devices, shards(): middle = dot(rot, lax.ppermute(rot, 'core', SWAP), ((1,), (1,)))  20.7 us
    all_to_all x1, blocking collectives, shards(): lax.all_to_all(final.reshape(n, -1, final.shape[1]), ('y', 'zh'), 0, 0, t...  19.1 us
    all_to_all x1, blocking collectives, shards(): lax.all_to_all(copies(left, 4), 'zl', 0, 0, tiled=True)  16 us
    all_to_all x2, starting transfers between devices, exchange(): lax.all_to_all(parts, AXES, 0, 0, axis_index_groups=groups, tiled=True)  15.5 us
    all_to_all x1, blocking collectives, shards(): lax.all_to_all(copies(left.astype(BF), 4), 'x', 0, 0, tiled=True)  9.02 us
    ppermute x1, starting transfers between devices, shards(): far = lax.ppermute(jnp.where(first, in_rows, grads), 'core', SWAP)  8.79 us
  transfers between devices with their start and end apart: 8, of which 6 were waited for; matrix products, arithmetic and copies ran while one was open for 1% of the time, Pallas kernels for 0%

profile of v2, /device:TPU:1, one launch (start us, length us, event | category | flops | bytes accessed | tf_op | source)
XLA Modules:
  0.0 169.1 jit_solution(11986711568248628339)
XLA Ops:
  0.0 0.7 slice_bitcast_fusion.1
  0.7 0.8 reshape.146
  1.5 0.8 fusion.9
  2.3 8.8 %collective-permute-start = (bf16[32,512]{1,0:T(8,128)(2,1)S(1)}, bf16[32,512]{1,0:T(8,128)(2,1)S(1)}, u32[]{:S(2)}, u32[]{:S(2)}) collective-permute-start(bf16[32,512]{1,0:T(8,128)(2,1)S(1)} %fusion.9), channel_id=1, source_target_pairs={{0,1},{1,0},{2,3},{3,2},{4,5},{5,4},{6,7},{7,6},{8,9},{9,8},{10,11... | collective-permute-start | bytes 98312 | tf_op jit(solution)/shard_map/ppermute | solution.py:52
  11.1 0.8 collective-permute-done
  11.9 0.8 maximum_select_fusion.5
  12.7 1.1 broadcast_in_dim.69
  13.8 10.1 %all-to-all-start = ((bf16[16,64,512]{2,1,0:T(8,128)(2,1)}), bf16[16,64,512]{2,1,0:T(8,128)(2,1)S(1)}, u32[]{:S(2)}, u32[]{:S(2)}) async-start(bf16[16,64,512]{2,1,0:T(8,128)(2,1)} %broadcast_in_dim.69), calls=%async_computation | async-start | bytes 2097152 | tf_op jit(solution)/shard_map/all_to_all | solution.py:27
  23.9 1.9 %collective-permute-start.2 = (bf16[256,512]{1,0:T(8,128)(2,1)S(1)}, bf16[256,512]{1,0:T(8,128)(2,1)S(1)}, u32[]{:S(2)}, u32[]{:S(2)}) collective-permute-start(bf16[256,512]{1,0:T(8,128)(2,1)S(1)} %copy-done.4), channel_id=1, source_target_pairs={{0,1},{1,0},{2,3},{3,2},{4,5},{5,4},{6,7},{7,6},{8,9},{9,8},{10,11... | collective-permute-start | bytes 786440 | tf_op jit(solution)/shard_map/ppermute | solution.py:66
  25.9 2.4 %collective-permute-start.3 = (bf16[512,256]{1,0:T(8,128)(2,1)S(1)}, bf16[512,256]{1,0:T(8,128)(2,1)S(1)}, u32[]{:S(2)}, u32[]{:S(2)}) collective-permute-start(bf16[512,256]{1,0:T(8,128)(2,1)S(1)} %copy-done.5), channel_id=1, source_target_pairs={{0,1},{1,0},{2,3},{3,2},{4,5},{5,4},{6,7},{7,6},{8,9},{9,8},{10,11... | collective-permute-start | bytes 786440 | tf_op jit(solution)/shard_map/ppermute | solution.py:67
  28.3 1.1 collective-permute-done.3
  29.4 18.5 %all-to-all-done = bf16[16,64,512]{2,1,0:T(8,128)(2,1)S(1)} async-done(((bf16[16,64,512]{2,1,0:T(8,128)(2,1)}), bf16[16,64,512]{2,1,0:T(8,128)(2,1)S(1)}, u32[]{:S(2)}, u32[]{:S(2)}) %all-to-all-start) | async-done | bytes 1048608 | tf_op jit(solution)/shard_map/all_to_all | solution.py:27
  47.9 1.7 %convolution_convert_fusion = bf16[512,1024]{1,0:T(8,128)(2,1)} fusion(bf16[1024,512]{1,0:T(8,128)(2,1)S(1)} %bitcast.22, bf16[256,512]{1,0:T(8,128)(2,1)S(1)} %collective-permute-done.2, bf16[256,512]{1,0:T(8,128)(2,1)S(1)} %copy-done.4, pred[]{:T(512)S(6)} %eq.40, bf16[512,256]{1,0:T(8,128)(2,1)S(1)} %collective-permute-done.3, ...), kind=kOutput, calls=%fused_computation.4 | convolution fusion | flops 541065216 | bytes 3145729 | tf_op jit(solution)/shard_map/dot_general | solution.py:23
  49.7 5.4 %all-to-all-start.1 = ((bf16[16,32,1024]{2,1,0:T(8,128)(2,1)}), bf16[16,32,1024]{2,1,0:T(8,128)(2,1)S(1)}, u32[]{:S(2)}, u32[]{:S(2)}) async-start(bf16[16,32,1024]{2,1,0:T(8,128)(2,1)} %bitcast.9), calls=%async_computation.1 | async-start | bytes 2097152 | tf_op jit(solution)/shard_map/all_to_all | solution.py:27
  55.2 0.5 select_reduce_fusion
  55.7 0.4 select_reduce_fusion.1
  56.2 19.0 %all-to-all-done.1 = bf16[16,32,1024]{2,1,0:T(8,128)(2,1)S(1)} async-done(((bf16[16,32,1024]{2,1,0:T(8,128)(2,1)}), bf16[16,32,1024]{2,1,0:T(8,128)(2,1)S(1)}, u32[]{:S(2)}, u32[]{:S(2)}) %all-to-all-start.1) | async-done | bytes 1048608 | tf_op jit(solution)/shard_map/all_to_all | solution.py:27
  75.2 0.2 convert_reduce_fusion
  75.5 20.8 %all_to_all.30 = bf16[16,32,1024]{2,1,0:T(8,128)(2,1)S(1)} all-to-all(bf16[16,32,1024]{2,1,0:T(8,128)(2,1)S(1)} %broadcast_in_dim.77), channel_id=1, replica_groups={{0,2,4,6,8,10,12,14,16,18,20,22,24,26,28,30},{32,34,36,38,40,42,44,46,4..., dimensions={0} | all-to-all | bytes 2097152 | tf_op jit(solution)/shard_map/all_to_all | solution.py:27
  96.4 20.7 %collective-permute-start.4 = (bf16[512,1024]{1,0:T(8,128)(2,1)S(1)}, bf16[512,1024]{1,0:T(8,128)(2,1)S(1)}, u32[]{:S(2)}, u32[]{:S(2)}) collective-permute-start(bf16[512,1024]{1,0:T(8,128)(2,1)S(1)} %bitcast.24), channel_id=1, source_target_pairs={{0,1},{1,0},{2,3},{3,2},{4,5},{5,4},{6,7},{7,6},{8,9},{9,8},{10,11... | collective-permute-start | bytes 3145736 | tf_op jit(solution)/shard_map/ppermute | solution.py:84
  117.1 1.9 %collective-permute-start.5 = (f32[256]{0:T(256)S(1)}, f32[256]{0:T(256)S(1)}, u32[]{:S(2)}, u32[]{:S(2)}) collective-permute-start(f32[256]{0:T(256)S(1)} %copy-done.3), channel_id=1, source_target_pairs={{0,1},{1,0},{2,3},{3,2},{4,5},{5,4},{6,7},{7,6},{8,9},{9,8},{10,11... | collective-permute-start | bytes 3080 | tf_op jit(solution)/shard_map/ppermute | solution.py:68
  119.0 1.1 collective-permute-done.5
  120.3 2.1 %collective-permute-start.1 = (bf16[64,512]{1,0:T(8,128)(2,1)S(1)}, bf16[64,512]{1,0:T(8,128)(2,1)S(1)}, u32[]{:S(2)}, u32[]{:S(2)}) collective-permute-start(bf16[64,512]{1,0:T(8,128)(2,1)S(1)} %reshape_squeeze.6), channel_id=1, source_target_pairs={{0,1},{1,0},{2,3},{3,2},{4,5},{5,4},{6,7},{7,6},{8,9},{9,8},{10,11... | collective-permute-start | bytes 196616 | tf_op jit(solution)/shard_map/ppermute | solution.py:82
  122.4 0.7 fusion
  123.1 0.3 collective-permute-done.1
  123.4 0.3 fusion.10
  123.7 0.2 fusion.1
  123.9 9.0 %all_to_all.31 = bf16[4,64,512]{2,1,0:T(8,128)(2,1)S(1)} all-to-all(bf16[4,64,512]{2,1,0:T(8,128)(2,1)S(1)} %broadcast_in_dim.78), channel_id=1, replica_groups=mesh['x'=4,'zl'=4,'y'=8,'zh'=2,'core'=2] {'x'}, dimensions={0} | all-to-all | bytes 524288 | tf_op jit(solution)/shard_map/all_to_all | solution.py:89
  133.1 16.0 %all_to_all.32 = f32[4,64,512]{2,1,0:T(8,128)S(1)} all-to-all(f32[4,64,512]{2,1,0:T(8,128)S(1)} %broadcast_in_dim.79), channel_id=1, replica_groups=mesh['x'=4,'zl'=4,'y'=8,'zh'=2,'core'=2] {'zl'}, dimensions={0} | all-to-all | bytes 1048576 | tf_op jit(solution)/shard_map/all_to_all | solution.py:90
  149.1 0.3 fusion.5
  149.4 19.1 %all_to_all.33 = f32[16,4,512]{2,1,0:T(4,128)S(1)} all-to-all(f32[16,4,512]{2,1,0:T(4,128)S(1)} %reshape.150), channel_id=1, replica_groups=mesh['x'=4,'zl'=4,'y'=8,'zh'=2,'core'=2] {'y','zh'}, dimensions={0} | all-to-all | bytes 262144 | tf_op jit(solution)/shard_map/all_to_all | solution.py:92
  168.5 0.6 reduce_sum.59
  (39 shorter events, 0.7 us)
Async XLA Ops:
  2.3 9.6 %collective-permute-start = (bf16[32,512]{1,0:T(8,128)(2,1)S(1)}, bf16[32,512]{1,0:T(8,128)(2,1)S(1)}, u32[]{:S(2)}, u32[]{:S(2)}) collective-permute-start(bf16[32,512]{1,0:T(8,128)(2,1)S(1)} %fusion.9), channel_id=1, source_target_pairs={{0,1},{1,0},{2,3},{3,2},{4,5},{5,4},{6,7},{7,6},{8,9},{9,8},{10,11... | collective-permute-start | bytes 98312 | tf_op jit(solution)/shard_map/ppermute | solution.py:52
  13.8 10.1 %copy-start.4 = (bf16[256,512]{1,0:T(8,128)(2,1)S(1)}, bf16[256,512]{1,0:T(8,128)(2,1)}, u32[]{:S(2)}) copy-start(bf16[256,512]{1,0:T(8,128)(2,1)} %param.10) | copy-start | bytes 786436
  13.8 12.1 %copy-start.5 = (bf16[512,256]{1,0:T(8,128)(2,1)S(1)}, bf16[512,256]{1,0:T(8,128)(2,1)}, u32[]{:S(2)}) copy-start(bf16[512,256]{1,0:T(8,128)(2,1)} %param.11) | copy-start | bytes 786436
  13.8 34.1 %all-to-all-start = ((bf16[16,64,512]{2,1,0:T(8,128)(2,1)}), bf16[16,64,512]{2,1,0:T(8,128)(2,1)S(1)}, u32[]{:S(2)}, u32[]{:S(2)}) async-start(bf16[16,64,512]{2,1,0:T(8,128)(2,1)} %broadcast_in_dim.69), calls=%async_computation | async-start | bytes 2097152 | tf_op jit(solution)/shard_map/all_to_all | solution.py:27
  23.9 4.4 %collective-permute-start.2 = (bf16[256,512]{1,0:T(8,128)(2,1)S(1)}, bf16[256,512]{1,0:T(8,128)(2,1)S(1)}, u32[]{:S(2)}, u32[]{:S(2)}) collective-permute-start(bf16[256,512]{1,0:T(8,128)(2,1)S(1)} %copy-done.4), channel_id=1, source_target_pairs={{0,1},{1,0},{2,3},{3,2},{4,5},{5,4},{6,7},{7,6},{8,9},{9,8},{10,11... | collective-permute-start | bytes 786440 | tf_op jit(solution)/shard_map/ppermute | solution.py:66
  25.9 3.6 %collective-permute-start.3 = (bf16[512,256]{1,0:T(8,128)(2,1)S(1)}, bf16[512,256]{1,0:T(8,128)(2,1)S(1)}, u32[]{:S(2)}, u32[]{:S(2)}) collective-permute-start(bf16[512,256]{1,0:T(8,128)(2,1)S(1)} %copy-done.5), channel_id=1, source_target_pairs={{0,1},{1,0},{2,3},{3,2},{4,5},{5,4},{6,7},{7,6},{8,9},{9,8},{10,11... | collective-permute-start | bytes 786440 | tf_op jit(solution)/shard_map/ppermute | solution.py:67
  29.4 20.2 %copy-start.6 = (bf16[512,256]{1,0:T(8,128)(2,1)}, bf16[512,256]{1,0:T(8,128)(2,1)S(1)}, u32[]{:S(2)}) copy-start(bf16[512,256]{1,0:T(8,128)(2,1)S(1)} %collective-permute-done.3) | copy-start | bytes 786436
  49.6 5.6 %copy-start = (s32[896]{0:T(1024)S(1)}, s32[896]{0:T(1024)}, u32[]{:S(2)}) copy-start(s32[896]{0:T(1024)} %param.15) | copy-start | bytes 10756
  49.7 6.0 %copy-start.1 = (s32[896]{0:T(1024)S(1)}, s32[896]{0:T(1024)}, u32[]{:S(2)}) copy-start(s32[896]{0:T(1024)} %param.14) | copy-start | bytes 10756
  49.7 25.5 %all-to-all-start.1 = ((bf16[16,32,1024]{2,1,0:T(8,128)(2,1)}), bf16[16,32,1024]{2,1,0:T(8,128)(2,1)S(1)}, u32[]{:S(2)}, u32[]{:S(2)}) async-start(bf16[16,32,1024]{2,1,0:T(8,128)(2,1)} %bitcast.9), calls=%async_computation.1 | async-start | bytes 2097152 | tf_op jit(solution)/shard_map/all_to_all | solution.py:27
  75.5 41.6 %copy-start.3 = (f32[256]{0:T(256)S(1)}, f32[256]{0:T(256)}, u32[]{:S(2)}) copy-start(f32[256]{0:T(256)} %param.13) | copy-start | bytes 3076
  75.5 44.6 %copy-start.2 = (f32[512]{0:T(512)S(1)}, f32[512]{0:T(512)}, u32[]{:S(2)}) copy-start(f32[512]{0:T(512)} %param.12) | copy-start | bytes 6148
  96.4 26.0 %collective-permute-start.4 = (bf16[512,1024]{1,0:T(8,128)(2,1)S(1)}, bf16[512,1024]{1,0:T(8,128)(2,1)S(1)}, u32[]{:S(2)}, u32[]{:S(2)}) collective-permute-start(bf16[512,1024]{1,0:T(8,128)(2,1)S(1)} %bitcast.24), channel_id=1, source_target_pairs={{0,1},{1,0},{2,3},{3,2},{4,5},{5,4},{6,7},{7,6},{8,9},{9,8},{10,11... | collective-permute-start | bytes 3145736 | tf_op jit(solution)/shard_map/ppermute | solution.py:84
  117.1 3.0 %collective-permute-start.5 = (f32[256]{0:T(256)S(1)}, f32[256]{0:T(256)S(1)}, u32[]{:S(2)}, u32[]{:S(2)}) collective-permute-start(f32[256]{0:T(256)S(1)} %copy-done.3), channel_id=1, source_target_pairs={{0,1},{1,0},{2,3},{3,2},{4,5},{5,4},{6,7},{7,6},{8,9},{9,8},{10,11... | collective-permute-start | bytes 3080 | tf_op jit(solution)/shard_map/ppermute | solution.py:68
  120.3 3.1 %collective-permute-start.1 = (bf16[64,512]{1,0:T(8,128)(2,1)S(1)}, bf16[64,512]{1,0:T(8,128)(2,1)S(1)}, u32[]{:S(2)}, u32[]{:S(2)}) collective-permute-start(bf16[64,512]{1,0:T(8,128)(2,1)S(1)} %reshape_squeeze.6), channel_id=1, source_target_pairs={{0,1},{1,0},{2,3},{3,2},{4,5},{5,4},{6,7},{7,6},{8,9},{9,8},{10,11... | collective-permute-start | bytes 196616 | tf_op jit(solution)/shard_map/ppermute | solution.py:82
  133.0 16.1 %copy-start.7 = (bf16[512,256]{1,0:T(8,128)(2,1)S(1)}, bf16[512,256]{1,0:T(8,128)(2,1)}, u32[]{:S(2)}) copy-start(bf16[512,256]{1,0:T(8,128)(2,1)} %copy-done.6) | copy-start | bytes 786436

commit v3 on v2

v3 whole, which is shorter than its diff:
```python
import jax
import jax.numpy as jnp
import numpy as np
from jax import lax
from jax.sharding import Mesh, PartitionSpec as P

DAMPING = 0.1
AXES = ("x", "zl", "y", "zh", "core")
SIZES = (4, 4, 8, 2, 2)
BF = jnp.bfloat16
F32 = jnp.float32
SWAP = [(0, 1), (1, 0)]

INDEX = np.arange(512).reshape(4, 2, 2, 8, 2, 2)


def lists(order, size):
    return INDEX.transpose(order).reshape(2, -1, size).tolist()


NEAR_PAIR, NEAR_EIGHT = lists((5, 0, 1, 3, 4, 2), 2), lists((5, 2, 3, 4, 0, 1), 8)
SKIP_PAIR, SKIP_EIGHT = lists((5, 0, 2, 3, 4, 1), 2), lists((5, 1, 3, 4, 0, 2), 8)
COL_PAIR, COL_EIGHT = lists((5, 0, 1, 2, 3, 4), 2), lists((5, 0, 1, 2, 4, 3), 8)
PAIR_IN = [(g[i], g[1 - i]) for g in NEAR_PAIR[0] + COL_PAIR[1] for i in range(2)]
PAIR_MID = [(g[i], g[1 - i]) for g in COL_PAIR[0] + SKIP_PAIR[1] for i in range(2)]
EIGHT_IN = NEAR_EIGHT[0] + COL_EIGHT[1]
EIGHT_MID = COL_EIGHT[0] + SKIP_EIGHT[1]


def dot(a, b, contract):
    return lax.dot_general(a, b, (contract, ((), ())), preferred_element_type=F32)


def exchange(parts, groups):
    return lax.all_to_all(parts, AXES, 0, 0, axis_index_groups=groups, tiled=True)


def copies(block, n):
    return jnp.broadcast_to(block[None], (n, *block.shape))


def three(value):
    out = []
    for _ in range(3):
        out.append(lax.reduce_precision(value, 8, 7))
        value = value - out[-1]
    return [v.astype(BF) for v in out]


def shards(out_grads, inputs, basis_out, basis_in, eig_out, eig_in, pair_order, length_bucket):
    tokens, share, block = pair_order.shape[0], inputs.shape[0], out_grads.shape[0]
    half = basis_in.shape[1]
    extra = 32 - share
    n = 16
    first = lax.axis_index("core") == 0
    zh, zl = lax.axis_index("zh"), lax.axis_index("zl")

    slab_own = basis_out[:extra]
    eig3 = jnp.concatenate([*three(eig_in), jnp.zeros((half,), BF)]).reshape(2, 2 * half)
    eig3 = jnp.pad(eig3, ((0, 6), (0, 0)))
    grads = jnp.pad(out_grads, ((0, 64 - block), (0, 0)))
    send = jnp.where(
        first,
        jnp.concatenate([inputs, slab_own, eig3], axis=0),
        jnp.concatenate([jnp.concatenate([grads[:32], grads[32:]], axis=1), eig3], axis=0),
    )
    far = lax.ppermute(send, "core", SWAP)
    far_grads = jnp.concatenate([far[:32, :half], far[:32, half:]], axis=0)
    rows = jnp.where(
        first,
        jnp.concatenate([grads, far_grads], axis=1),
        jnp.concatenate([far[:share], inputs, far[share:32], slab_own], axis=0),
    )
    eig_far = far[32:34].reshape(4, half).astype(F32)
    eig_far = eig_far[0] + eig_far[1] + eig_far[2]
    eig_in2 = jnp.where(first, jnp.concatenate([eig_in, eig_far]), jnp.concatenate([eig_far, eig_in]))

    rows_far = lax.ppermute(rows, AXES, PAIR_IN)
    out_far = lax.ppermute(basis_out, "core", SWAP)
    in_far = lax.ppermute(basis_in, "core", SWAP)
    basis_in2 = jnp.where(
        first, jnp.concatenate([basis_in, in_far], axis=1), jnp.concatenate([in_far, basis_in], axis=1)
    )
    basis = jnp.where(first, jnp.concatenate([basis_out, out_far], axis=0), basis_in2)
    low = jnp.where(first, zl % 2, zh) == 0
    rows = jnp.stack([jnp.where(low, rows, rows_far), jnp.where(low, rows_far, rows)])

    place = lax.broadcasted_iota(jnp.int32, (tokens, 1), 0)
    token = lax.broadcasted_iota(jnp.int32, (1, tokens), 1)
    parity = jnp.where(place % 2 == 0, 1.0, -1.0)
    sign = jnp.sum(jnp.where(pair_order[:, None] == token, parity, 0.0), axis=0)
    weights = sign / jnp.sqrt((1.0 + length_bucket.astype(F32)) * tokens)
    weights = jnp.where(first, weights, 1.0)

    rows, basis, basis_in2, weights, eig_in2 = lax.optimization_barrier(
        (rows, basis, basis_in2, weights, eig_in2)
    )
    rows = exchange(copies(rows, 8), EIGHT_IN).reshape(n, 64, -1)

    slab0 = rows[:, block : block + extra].reshape(n * extra, -1)
    slab1 = rows[:, block + extra :].reshape(n * extra, -1)
    part = dot(basis, rows[:, :block].reshape(tokens, -1), ((0,), (1,))).astype(BF)
    part = exchange(part.reshape(8, -1, tokens), EIGHT_MID)
    total = jnp.sum(part.astype(F32), axis=0)
    total_far = lax.ppermute(total.astype(BF), AXES, PAIR_MID)
    slab = jnp.where(first, lax.ppermute(slab0, "core", SWAP), slab1)
    rot = ((total + total_far.astype(F32)) * weights).astype(BF)
    rot, slab = lax.optimization_barrier((rot, slab))
    rot = exchange(copies(rot, 8), EIGHT_MID).reshape(-1, tokens)

    middle = dot(rot, lax.ppermute(rot, "core", SWAP), ((1,), (1,)))
    down, across = jnp.where(first, eig_out, eig_in2), jnp.where(first, eig_in2, eig_out)
    scaled = (middle / (down[:, None] * across[None, :] + DAMPING)).astype(BF)
    left = jnp.where(first, dot(slab, scaled, ((1,), (0,))), dot(slab, scaled, ((1,), (1,))))

    left = lax.all_to_all(left.reshape(n, -1, left.shape[1]), ("x", "zl"), 0, 0, tiled=True)
    left = jnp.sum(left, axis=0).astype(BF)
    left = lax.all_to_all(copies(left, n), ("x", "zl"), 0, 0, tiled=True)
    left = left.reshape(-1, left.shape[2])
    final = dot(left, basis_in2, ((1,), (1,)))
    final = lax.all_to_all(final.reshape(n, -1, final.shape[1]), ("y", "zh"), 0, 0, tiled=True)
    return jnp.sum(final, axis=0)


def solution(mesh):
    fine = Mesh(mesh.devices.reshape(SIZES), AXES)
    row, col = AXES[:2], AXES[2:]
    return jax.shard_map(
        shards,
        mesh=fine,
        in_specs=(P(row, col), P(col, row), P(col, row), P(row, col), P(row), P(col), P(), P()),
        out_specs=P(col, row),
        check_vma=False,
    )
```

time: 171 us -> 155 us (0.906)
  waiting for transfers between devices: 40.8 us -> 16.3 us
  blocking collectives: 64.8 us -> 75.1 us
  starting transfers between devices: 53.3 us -> 48.9 us
  other arithmetic: 3.49 us -> 5.95 us
    all_to_all x2 -> x1, waiting for transfers between devices: 37.5 us -> 7.66 us  [exchange(): lax.all_to_all(parts, AXES, 0, 0, axis_index_groups=groups, tiled=True)]
    all_to_all x1 -> x2, blocking collectives: 20.8 us -> 35.6 us  [exchange(): lax.all_to_all(parts, AXES, 0, 0, axis_index_groups=groups, tiled=True)]
    all_to_all x2 -> x1, starting transfers between devices: 15.5 us -> 4.86 us  [exchange(): lax.all_to_all(parts, AXES, 0, 0, axis_index_groups=groups, tiled=True)]
    ppermute x1, starting transfers between devices: 1.92 us -> 8.91 us  [shards(): out_far = lax.ppermute(basis_out, 'core', SWAP)]
    all_to_all x2, blocking collectives: 25 us -> 20.5 us  [the longest x1 10.7 us: shards(): left = lax.all_to_all(copies(left, n), ('x', 'zl'), 0, 0, tiled=True)]
    ppermute x3 -> x4, waiting for transfers between devices: 2.22 us -> 6.58 us  [the longest x1 3.37 us: shards(): total_far = lax.ppermute(total.astype(BF), AXES, PAIR_MID)]
    ppermute x1, waiting for transfers between devices: 0.01 us -> 2.05 us  [shards(): middle = dot(rot, lax.ppermute(rot, 'core', SWAP), ((1,), (1,)))]
    ppermute x3 -> x4, starting transfers between devices: 12.8 us -> 13.4 us  [the longest x1 5.26 us: shards(): rows_far = lax.ppermute(rows, AXES, PAIR_IN)]
  transfers between devices with their start and end apart: 8 -> 8, of which waited for: 6 -> 4; matrix products, arithmetic and copies ran while one was open for 1% -> 5% of each run, Pallas kernels for 0% -> 0%
where the time goes in v3:
time: 155 us; the launch traced here: 153 us
  blocking collectives  75.1 us (48%)
  starting transfers between devices  48.9 us (32%)
  waiting for transfers between devices  16.3 us (11%)
  other arithmetic  5.95 us (4%)
  matrix products  3.21 us (2%)
  local copies, waits for them, and re-layouts  2.78 us (2%)
    all_to_all x2, blocking collectives, exchange(): lax.all_to_all(parts, AXES, 0, 0, axis_index_groups=groups, tiled=True)  35.6 us
    ppermute x1, starting transfers between devices, shards(): middle = dot(rot, lax.ppermute(rot, 'core', SWAP), ((1,), (1,)))  19.3 us
    all_to_all x1, blocking collectives, shards(): lax.all_to_all(final.reshape(n, -1, final.shape[1]), ('y', 'zh'), 0, 0, t...  19.1 us
    all_to_all x1, blocking collectives, shards(): left = lax.all_to_all(copies(left, n), ('x', 'zl'), 0, 0, tiled=True)  10.7 us
    all_to_all x1, blocking collectives, shards(): lax.all_to_all(left.reshape(n, -1, left.shape[1]), ('x', 'zl'), 0, 0, til...  9.83 us
    ppermute x1, starting transfers between devices, shards(): out_far = lax.ppermute(basis_out, 'core', SWAP)  8.91 us
    all_to_all x1, waiting for transfers between devices, exchange(): lax.all_to_all(parts, AXES, 0, 0, axis_index_groups=groups, tiled=True)  7.66 us
    ppermute x1, starting transfers between devices, shards(): rows_far = lax.ppermute(rows, AXES, PAIR_IN)  5.26 us
  transfers between devices with their start and end apart: 8, of which 4 were waited for; matrix products, arithmetic and copies ran while one was open for 5% of the time, Pallas kernels for 0%

profile of v3, /device:TPU:1, one launch (start us, length us, event | category | flops | bytes accessed | tf_op | source)
XLA Modules:
  0.0 152.6 jit_solution(6981018761559442745)
XLA Ops:
  0.0 8.9 %collective-permute-start.2 = (bf16[256,512]{1,0:T(8,128)(2,1)}, bf16[256,512]{1,0:T(8,128)(2,1)S(1)}, u32[]{:S(2)}, u32[]{:S(2)}) collective-permute-start(bf16[256,512]{1,0:T(8,128)(2,1)} %param.10), channel_id=1, source_target_pairs={{0,1},{1,0},{2,3},{3,2},{4,5},{5,4},{6,7},{7,6},{8,9},{9,8},{10,11... | collective-permute-start | bytes 786440 | tf_op jit(solution)/shard_map/ppermute | solution.py:79
  8.9 0.7 slice.43
  9.6 0.7 reduce-precision_convert_fusion.1
  10.3 0.7 fusion.17
  11.1 0.8 fusion.7
  11.8 1.9 %collective-permute-start = (bf16[40,512]{1,0:T(8,128)(2,1)S(1)}, bf16[40,512]{1,0:T(8,128)(2,1)S(1)}, u32[]{:S(2)}, u32[]{:S(2)}) collective-permute-start(bf16[40,512]{1,0:T(8,128)(2,1)S(1)} %fusion.7), channel_id=1, source_target_pairs={{0,1},{1,0},{2,3},{3,2},{4,5},{5,4},{6,7},{7,6},{8,9},{9,8},{10,11... | collective-permute-start | bytes 122888 | tf_op jit(solution)/shard_map/ppermute | solution.py:67
  13.8 2.4 %collective-permute-start.3 = (bf16[512,256]{1,0:T(8,128)(2,1)}, bf16[512,256]{1,0:T(8,128)(2,1)S(1)}, u32[]{:S(2)}, u32[]{:S(2)}) collective-permute-start(bf16[512,256]{1,0:T(8,128)(2,1)} %param.11), channel_id=1, source_target_pairs={{0,1},{1,0},{2,3},{3,2},{4,5},{5,4},{6,7},{7,6},{8,9},{9,8},{10,11... | collective-permute-start | bytes 786440 | tf_op jit(solution)/shard_map/ppermute | solution.py:80
  16.2 1.1 select_reduce_fusion
  17.3 0.7 multiply_select_fusion
  18.0 0.8 pad.8
  18.8 0.8 maximum_select_fusion.2
  19.6 5.3 %collective-permute-start.1 = (bf16[64,512]{1,0:T(8,128)(2,1)S(1)}, bf16[64,512]{1,0:T(8,128)(2,1)S(1)}, u32[]{:S(2)}, u32[]{:S(2)}) collective-permute-start(bf16[64,512]{1,0:T(8,128)(2,1)S(1)} %maximum_select_fusion.2), channel_id=1, source_target_pairs={{0,32},{32,0},{2,34},{34,2},{4,36},{36,4},{6,38},{38,6},{8,40},{40... | collective-permute-start | bytes 196616 | tf_op jit(solution)/shard_map/ppermute | solution.py:78
  24.9 0.8 maximum_select_fusion.3
  25.7 3.2 %collective-permute-done.1 = bf16[64,512]{1,0:T(8,128)(2,1)S(1)} collective-permute-done((bf16[64,512]{1,0:T(8,128)(2,1)S(1)}, bf16[64,512]{1,0:T(8,128)(2,1)S(1)}, u32[]{:S(2)}, u32[]{:S(2)}) %collective-permute-start.1) | collective-permute-done | bytes 65568 | tf_op jit(solution)/shard_map/ppermute | solution.py:78
  29.3 22.1 %all_to_all.30 = bf16[8,2,64,512]{3,2,1,0:T(8,128)(2,1)S(1)} all-to-all(bf16[8,2,64,512]{3,2,1,0:T(8,128)(2,1)S(1)} %broadcast_in_dim.52), channel_id=1, replica_groups={{0,64,128,192,256,320,384,448},{2,66,130,194,258,322,386,450},{4,68,132..., dimensions={0} | all-to-all | bytes 2097152 | tf_op jit(solution)/shard_map/all_to_all | solution.py:35
  51.5 1.7 %convolution_convert_fusion = bf16[512,896]{1,0:T(8,128)(2,1)} fusion(bf16[512,512]{1,0:T(8,128)(2,1)S(1)} %get-tuple-element.12, bf16[896,512]{1,0:T(8,128)(2,1)S(1)} %bitcast.24), kind=kOutput, calls=%fused_computation.3 | convolution fusion | flops 470220800 | bytes 2359296 | tf_op jit(solution)/shard_map/dot_general | solution.py:31
  53.2 4.9 %all-to-all-start.1 = ((bf16[8,64,896]{2,1,0:T(8,128)(2,1)}), bf16[8,64,896]{2,1,0:T(8,128)(2,1)S(1)}, u32[]{:S(2)}, u32[]{:S(2)}) async-start(bf16[8,64,896]{2,1,0:T(8,128)(2,1)} %bitcast.5), calls=%async_computation.1 | async-start | bytes 1835008 | tf_op jit(solution)/shard_map/all_to_all | solution.py:35
  58.1 1.9 %collective-permute-start.5 = (bf16[64,512]{1,0:T(8,128)(2,1)S(1)}, bf16[64,512]{1,0:T(8,128)(2,1)S(1)}, u32[]{:S(2)}, u32[]{:S(2)}) collective-permute-start(bf16[64,512]{1,0:T(8,128)(2,1)S(1)} %reshape.65), channel_id=1, source_target_pairs={{0,1},{1,0},{2,3},{3,2},{4,5},{5,4},{6,7},{7,6},{8,9},{9,8},{10,11... | collective-permute-start | bytes 196616 | tf_op jit(solution)/shard_map/ppermute | solution.py:106
  60.0 7.7 %all-to-all-done.1 = bf16[8,64,896]{2,1,0:T(8,128)(2,1)S(1)} async-done(((bf16[8,64,896]{2,1,0:T(8,128)(2,1)}), bf16[8,64,896]{2,1,0:T(8,128)(2,1)S(1)}, u32[]{:S(2)}, u32[]{:S(2)}) %all-to-all-start.1) | async-done | bytes 917536 | tf_op jit(solution)/shard_map/all_to_all | solution.py:35
  67.9 4.3 %collective-permute-start.4 = (bf16[64,896]{1,0:T(8,128)(2,1)S(1)}, bf16[64,896]{1,0:T(8,128)(2,1)S(1)}, u32[]{:S(2)}, u32[]{:S(2)}) collective-permute-start(bf16[64,896]{1,0:T(8,128)(2,1)S(1)} %convert_element_type.55), channel_id=1, source_target_pairs={{0,2},{2,0},{4,6},{6,4},{8,10},{10,8},{12,14},{14,12},{16,18},{18,... | collective-permute-start | bytes 344072 | tf_op jit(solution)/shard_map/ppermute | solution.py:105
  72.2 3.4 %collective-permute-done.4 = bf16[64,896]{1,0:T(8,128)(2,1)S(1)} collective-permute-done((bf16[64,896]{1,0:T(8,128)(2,1)S(1)}, bf16[64,896]{1,0:T(8,128)(2,1)S(1)}, u32[]{:S(2)}, u32[]{:S(2)}) %collective-permute-start.4) | collective-permute-done | bytes 114720 | tf_op jit(solution)/shard_map/ppermute | solution.py:105
  75.7 13.5 %all_to_all.31 = bf16[8,64,896]{2,1,0:T(8,128)(2,1)S(1)} all-to-all(bf16[8,64,896]{2,1,0:T(8,128)(2,1)S(1)} %broadcast_in_dim.53), channel_id=1, replica_groups={{0,4,8,12,16,20,24,28},{2,6,10,14,18,22,26,30},{32,36,40,44,48,52,56,60..., dimensions={0} | all-to-all | bytes 1835008 | tf_op jit(solution)/shard_map/all_to_all | solution.py:35
  89.2 19.3 %collective-permute-start.6 = (bf16[512,896]{1,0:T(8,128)(2,1)S(1)}, bf16[512,896]{1,0:T(8,128)(2,1)S(1)}, u32[]{:S(2)}, u32[]{:S(2)}) collective-permute-start(bf16[512,896]{1,0:T(8,128)(2,1)S(1)} %bitcast.22), channel_id=1, source_target_pairs={{0,1},{1,0},{2,3},{3,2},{4,5},{5,4},{6,7},{7,6},{8,9},{9,8},{10,11... | collective-permute-start | bytes 2752520 | tf_op jit(solution)/shard_map/ppermute | solution.py:111
  108.6 2.1 %collective-permute-done.6 = bf16[512,896]{1,0:T(8,128)(2,1)S(1)} collective-permute-done((bf16[512,896]{1,0:T(8,128)(2,1)S(1)}, bf16[512,896]{1,0:T(8,128)(2,1)S(1)}, u32[]{:S(2)}, u32[]{:S(2)}) %collective-permute-start.6) | collective-permute-done | bytes 917536 | tf_op jit(solution)/shard_map/ppermute | solution.py:111
  110.6 0.7 fusion
  111.4 0.3 fusion.18
  111.6 0.2 convolution_select_fusion
  111.9 9.8 %all_to_all.32 = f32[16,4,512]{2,1,0:T(4,128)S(1)} all-to-all(f32[16,4,512]{2,1,0:T(4,128)S(1)} %reshape.68), channel_id=1, replica_groups=mesh['x'=4,'zl'=4,'y'=8,'zh'=2,'core'=2] {'x','zl'}, dimensions={0} | all-to-all | bytes 262144 | tf_op jit(solution)/shard_map/all_to_all | solution.py:116
  121.8 10.7 %all_to_all.33 = bf16[16,4,512]{2,1,0:T(4,128)(2,1)S(1)} all-to-all(bf16[16,4,512]{2,1,0:T(4,128)(2,1)S(1)} %broadcast_in_dim.54), channel_id=1, replica_groups=mesh['x'=4,'zl'=4,'y'=8,'zh'=2,'core'=2] {'x','zl'}, dimensions={0} | all-to-all | bytes 131072 | tf_op jit(solution)/shard_map/all_to_all | solution.py:118
  132.5 0.3 fusion.1
  132.9 19.1 %all_to_all.34 = f32[16,4,512]{2,1,0:T(4,128)S(1)} all-to-all(f32[16,4,512]{2,1,0:T(4,128)S(1)} %copy.12), channel_id=1, replica_groups=mesh['x'=4,'zl'=4,'y'=8,'zh'=2,'core'=2] {'y','zh'}, dimensions={0} | all-to-all | bytes 262144 | tf_op jit(solution)/shard_map/all_to_all | solution.py:121
  151.9 0.6 reduce_sum.39
  (38 shorter events, 1.1 us)
Async XLA Ops:
  0.0 29.0 %copy-start = (bf16[256,512]{1,0:T(8,128)(2,1)S(1)}, bf16[256,512]{1,0:T(8,128)(2,1)}, u32[]{:S(2)}) copy-start(bf16[256,512]{1,0:T(8,128)(2,1)} %param.10) | copy-start | bytes 786436
  0.0 29.0 %copy-start.1 = (bf16[512,256]{1,0:T(8,128)(2,1)S(1)}, bf16[512,256]{1,0:T(8,128)(2,1)}, u32[]{:S(2)}) copy-start(bf16[512,256]{1,0:T(8,128)(2,1)} %param.11) | copy-start | bytes 786436
  0.0 28.9 %collective-permute-start.2 = (bf16[256,512]{1,0:T(8,128)(2,1)}, bf16[256,512]{1,0:T(8,128)(2,1)S(1)}, u32[]{:S(2)}, u32[]{:S(2)}) collective-permute-start(bf16[256,512]{1,0:T(8,128)(2,1)} %param.10), channel_id=1, source_target_pairs={{0,1},{1,0},{2,3},{3,2},{4,5},{5,4},{6,7},{7,6},{8,9},{9,8},{10,11... | collective-permute-start | bytes 786440 | tf_op jit(solution)/shard_map/ppermute | solution.py:79
  11.8 6.9 %collective-permute-start = (bf16[40,512]{1,0:T(8,128)(2,1)S(1)}, bf16[40,512]{1,0:T(8,128)(2,1)S(1)}, u32[]{:S(2)}, u32[]{:S(2)}) collective-permute-start(bf16[40,512]{1,0:T(8,128)(2,1)S(1)} %fusion.7), channel_id=1, source_target_pairs={{0,1},{1,0},{2,3},{3,2},{4,5},{5,4},{6,7},{7,6},{8,9},{9,8},{10,11... | collective-permute-start | bytes 122888 | tf_op jit(solution)/shard_map/ppermute | solution.py:67
  13.8 15.2 %collective-permute-start.3 = (bf16[512,256]{1,0:T(8,128)(2,1)}, bf16[512,256]{1,0:T(8,128)(2,1)S(1)}, u32[]{:S(2)}, u32[]{:S(2)}) collective-permute-start(bf16[512,256]{1,0:T(8,128)(2,1)} %param.11), channel_id=1, source_target_pairs={{0,1},{1,0},{2,3},{3,2},{4,5},{5,4},{6,7},{7,6},{8,9},{9,8},{10,11... | collective-permute-start | bytes 786440 | tf_op jit(solution)/shard_map/ppermute | solution.py:80
  19.6 9.3 %collective-permute-start.1 = (bf16[64,512]{1,0:T(8,128)(2,1)S(1)}, bf16[64,512]{1,0:T(8,128)(2,1)S(1)}, u32[]{:S(2)}, u32[]{:S(2)}) collective-permute-start(bf16[64,512]{1,0:T(8,128)(2,1)S(1)} %maximum_select_fusion.2), channel_id=1, source_target_pairs={{0,32},{32,0},{2,34},{34,2},{4,36},{36,4},{6,38},{38,6},{8,40},{40... | collective-permute-start | bytes 196616 | tf_op jit(solution)/shard_map/ppermute | solution.py:78
  53.2 14.5 %all-to-all-start.1 = ((bf16[8,64,896]{2,1,0:T(8,128)(2,1)}), bf16[8,64,896]{2,1,0:T(8,128)(2,1)S(1)}, u32[]{:S(2)}, u32[]{:S(2)}) async-start(bf16[8,64,896]{2,1,0:T(8,128)(2,1)} %bitcast.5), calls=%async_computation.1 | async-start | bytes 1835008 | tf_op jit(solution)/shard_map/all_to_all | solution.py:35
  58.1 14.1 %collective-permute-start.5 = (bf16[64,512]{1,0:T(8,128)(2,1)S(1)}, bf16[64,512]{1,0:T(8,128)(2,1)S(1)}, u32[]{:S(2)}, u32[]{:S(2)}) collective-permute-start(bf16[64,512]{1,0:T(8,128)(2,1)S(1)} %reshape.65), channel_id=1, source_target_pairs={{0,1},{1,0},{2,3},{3,2},{4,5},{5,4},{6,7},{7,6},{8,9},{9,8},{10,11... | collective-permute-start | bytes 196616 | tf_op jit(solution)/shard_map/ppermute | solution.py:106
  67.9 7.7 %collective-permute-start.4 = (bf16[64,896]{1,0:T(8,128)(2,1)S(1)}, bf16[64,896]{1,0:T(8,128)(2,1)S(1)}, u32[]{:S(2)}, u32[]{:S(2)}) collective-permute-start(bf16[64,896]{1,0:T(8,128)(2,1)S(1)} %convert_element_type.55), channel_id=1, source_target_pairs={{0,2},{2,0},{4,6},{6,4},{8,10},{10,8},{12,14},{14,12},{16,18},{18,... | collective-permute-start | bytes 344072 | tf_op jit(solution)/shard_map/ppermute | solution.py:105
  75.7 32.8 %copy-start.2 = (f32[512]{0:T(512)S(1)}, f32[512]{0:T(512)}, u32[]{:S(2)}) copy-start(f32[512]{0:T(512)} %param.12) | copy-start | bytes 6148
  89.2 21.4 %collective-permute-start.6 = (bf16[512,896]{1,0:T(8,128)(2,1)S(1)}, bf16[512,896]{1,0:T(8,128)(2,1)S(1)}, u32[]{:S(2)}, u32[]{:S(2)}) collective-permute-start(bf16[512,896]{1,0:T(8,128)(2,1)S(1)} %bitcast.22), channel_id=1, source_target_pairs={{0,1},{1,0},{2,3},{3,2},{4,5},{5,4},{6,7},{7,6},{8,9},{9,8},{10,11... | collective-permute-start | bytes 2752520 | tf_op jit(solution)/shard_map/ppermute | solution.py:111

commit v4 on v3

v4 whole, which is shorter than its diff:
```python
import jax
import jax.numpy as jnp
import numpy as np
from jax import lax
from jax.sharding import Mesh, PartitionSpec as P

DAMPING = 0.1
AXES = ("x", "zl", "y", "zh", "core")
SIZES = (4, 4, 8, 2, 2)
BF = jnp.bfloat16
F32 = jnp.float32
SWAP = [(0, 1), (1, 0)]

INDEX = np.arange(512).reshape(4, 2, 2, 8, 2, 2)


def lists(order, size):
    return INDEX.transpose(order).reshape(2, -1, size).tolist()


ROW_PAIR, ROW_EIGHT = lists((5, 0, 2, 3, 4, 1), 2), lists((5, 1, 3, 4, 0, 2), 8)
COL_PAIR, COL_EIGHT = lists((5, 0, 1, 2, 3, 4), 2), lists((5, 0, 1, 2, 4, 3), 8)
COL_ALL = lists((5, 0, 1, 2, 4, 3), 16)
EIGHT_IN = ROW_EIGHT[0] + COL_EIGHT[1]
EIGHT_MID = COL_EIGHT[0] + ROW_EIGHT[1]
PAIR_IN = [(g[i], g[1 - i]) for g in ROW_PAIR[0] + COL_PAIR[1] for i in range(2)]
PAIR_MID = [(g[i], g[1 - i]) for g in COL_PAIR[0] + ROW_PAIR[1] for i in range(2)]
CROSS = [(g[i], g[1 - i] + 1) for g in COL_PAIR[0] for i in range(2)]
CROSS += [(g[i], g[1 - i] - 1) for g in ROW_PAIR[1] for i in range(2)]


def dot(a, b, contract):
    return lax.dot_general(a, b, (contract, ((), ())), preferred_element_type=F32)


def exchange(parts, groups):
    return lax.all_to_all(parts, AXES, 0, 0, axis_index_groups=groups, tiled=True)


def copies(block, n):
    return jnp.broadcast_to(block[None], (n, *block.shape))


def shards(out_grads, inputs, basis_out, basis_in, eig_out, eig_in, pair_order, length_bucket):
    tokens, share, block = pair_order.shape[0], inputs.shape[0], out_grads.shape[0]
    half = basis_in.shape[1]
    extra = 32 - share
    n = 16
    first = lax.axis_index("core") == 0
    zh, zl = lax.axis_index("zh"), lax.axis_index("zl")

    acts = jnp.concatenate([inputs, basis_out[:extra]], axis=0)
    grads = jnp.pad(out_grads, ((0, 64 - block), (0, 0)))
    grads = jnp.concatenate([grads[:32], grads[32:]], axis=1)
    kept, given = jnp.where(first, grads, acts), jnp.where(first, acts, grads)
    kept_far = lax.ppermute(kept, AXES, PAIR_IN)
    cross_far = lax.ppermute(given, AXES, CROSS)
    given_far = lax.ppermute(given, "core", SWAP)

    def joined(mine, other):
        lanes = [[p[:, :half], p[:, half:]] for p in (mine, other)]
        as_grads = jnp.concatenate([jnp.concatenate(p, axis=0) for p in lanes], axis=1)
        as_acts = jnp.concatenate([other[:share], mine[:share], other[share:], mine[share:]], axis=0)
        return jnp.where(first, as_grads, as_acts)

    rows, rows_far = joined(kept, given_far), joined(kept_far, cross_far)
    low = jnp.where(first, zl // 2, zh) == 0
    rows = jnp.stack([jnp.where(low, rows, rows_far), jnp.where(low, rows_far, rows)])

    late = lax.optimization_barrier((given_far, basis_out, basis_in, eig_in, pair_order, length_bucket))
    basis_out_late, basis_in_late, eig_late, pair_order, length_bucket = late[1:]
    out_far = lax.ppermute(basis_out_late, "core", SWAP)
    in_far = lax.ppermute(basis_in_late, "core", SWAP)
    basis_in2 = jnp.where(
        first, jnp.concatenate([basis_in, in_far], axis=1), jnp.concatenate([in_far, basis_in], axis=1)
    )
    basis = jnp.where(first, jnp.concatenate([basis_out, out_far], axis=0), basis_in2)
    eig_far = lax.ppermute(eig_late, "core", SWAP)
    eig_in2 = jnp.where(first, jnp.concatenate([eig_in, eig_far]), jnp.concatenate([eig_far, eig_in]))
    place = lax.broadcasted_iota(jnp.int32, (tokens, 1), 0)
    token = lax.broadcasted_iota(jnp.int32, (1, tokens), 1)
    parity = jnp.where(place % 2 == 0, 1.0, -1.0)
    sign = jnp.sum(jnp.where(pair_order[:, None] == token, parity, 0.0), axis=0)
    weights = sign / jnp.sqrt((1.0 + length_bucket.astype(F32)) * tokens)
    weights = jnp.where(first, weights, 1.0)

    rows, basis, basis_in2, eig_in2, weights = lax.optimization_barrier(
        (rows, basis, basis_in2, eig_in2, weights)
    )
    rows = exchange(copies(rows, 8), EIGHT_IN)
    ordered = rows[:, :, :block].reshape(tokens, -1)
    paired = rows.reshape(4, 2, 2, 64, -1).swapaxes(1, 2)[:, :, :, :block].reshape(tokens, -1)
    part = dot(basis, jnp.where(first, paired, ordered), ((0,), (1,))).astype(BF)
    part = exchange(part.reshape(8, -1, tokens), EIGHT_MID)
    part, rows = lax.optimization_barrier((part, rows))
    total = jnp.sum(part.astype(F32), axis=0)
    total_far = lax.ppermute(total.astype(BF), AXES, PAIR_MID)
    slab0, slab1 = (
        rows[:, :, block + k * extra : block + (k + 1) * extra].swapaxes(0, 1).reshape(n * extra, -1)
        for k in range(2)
    )
    rot = ((total + total_far.astype(F32)) * weights).astype(BF)
    rot, slab0, slab1 = lax.optimization_barrier((rot, slab0, slab1))
    rot = exchange(copies(rot, 8), EIGHT_MID).reshape(-1, tokens)
    rot, slab0 = lax.optimization_barrier((rot, slab0))
    rot_far = lax.ppermute(rot, "core", SWAP)
    slab = jnp.where(first, lax.ppermute(slab0, "core", SWAP), slab1)

    middle = dot(rot, rot_far, ((1,), (1,)))
    down, across = jnp.where(first, eig_out, eig_in2), jnp.where(first, eig_in2, eig_out)
    scaled = (middle / (down[:, None] * across[None, :] + DAMPING)).astype(BF)
    left = jnp.where(first, dot(slab, scaled, ((1,), (0,))), dot(slab, scaled, ((1,), (1,))))

    left = lax.all_to_all(left.reshape(n, -1, left.shape[1]), ("x", "zl"), 0, 0, tiled=True)
    left = jnp.sum(left, axis=0).astype(BF)
    left = lax.all_to_all(copies(left, n), ("x", "zl"), 0, 0, tiled=True)
    left = left.reshape(-1, left.shape[2])
    final = dot(left, basis_in2, ((1,), (1,)))
    final = exchange(final.reshape(n, -1, final.shape[1]), COL_ALL[0] + COL_ALL[1])
    return jnp.sum(final, axis=0)


def solution(mesh):
    fine = Mesh(mesh.devices.reshape(SIZES), AXES)
    row, col = AXES[:2], AXES[2:]
    return jax.shard_map(
        shards,
        mesh=fine,
        in_specs=(P(row, col), P(col, row), P(col, row), P(row, col), P(row), P(col), P(), P()),
        out_specs=P(col, row),
        check_vma=False,
    )
```

time: 155 us -> 147 us (0.948)
  blocking collectives: 75.1 us -> 86 us
  waiting for transfers between devices: 16.3 us -> 7.14 us
  starting transfers between devices: 48.9 us -> 42.8 us
  other arithmetic: 5.95 us -> 4.06 us
    all_to_all x2 -> x4, blocking collectives: 35.6 us -> 64.9 us  [exchange(): lax.all_to_all(parts, AXES, 0, 0, axis_index_groups=groups, tiled=True)]
    all_to_all x1 -> x0, blocking collectives: 19.1 us -> none  [shards(): lax.all_to_all(final.reshape(n, -1, final.shape[1]), ('y', 'zh'), 0, 0, t...]
    all_to_all x1 -> x0, waiting for transfers between devices: 7.66 us -> none  [exchange(): lax.all_to_all(parts, AXES, 0, 0, axis_index_groups=groups, tiled=True)]
    ppermute x5 -> x7, waiting for transfers between devices: 5.27 us -> 0.14 us  [the longest x1 0.13 us: shards(): rot_far = lax.ppermute(rot, 'core', SWAP)]
    all_to_all x1 -> x0, starting transfers between devices: 4.86 us -> none  [exchange(): lax.all_to_all(parts, AXES, 0, 0, axis_index_groups=groups, tiled=True)]
    ppermute x1, waiting for transfers between devices: 3.37 us -> 6.65 us  [shards(): total_far = lax.ppermute(total.astype(BF), AXES, PAIR_MID)]
    ppermute x1, starting transfers between devices: 4.29 us -> 2.17 us  [shards(): total_far = lax.ppermute(total.astype(BF), AXES, PAIR_MID)]
    ppermute x5 -> x7, starting transfers between devices: 37.8 us -> 38.7 us  [the longest x1 13.8 us: shards(): rot_far = lax.ppermute(rot, 'core', SWAP)]
  transfers between devices with their start and end apart: 8 -> 9, of which waited for: 4 -> 3; matrix products, arithmetic and copies ran while one was open for 5% -> 2% of each run, Pallas kernels for 0% -> 0%
where the time goes in v4:
time: 147 us; the launch traced here: 145 us
  blocking collectives  86 us (59%)
  starting transfers between devices  42.8 us (29%)
  waiting for transfers between devices  7.14 us (5%)
  other arithmetic  4.06 us (3%)
  local copies, waits for them, and re-layouts  2.29 us (2%)
  matrix products  2.25 us (2%)
    all_to_all x4, blocking collectives, exchange(): lax.all_to_all(parts, AXES, 0, 0, axis_index_groups=groups, tiled=True)  64.9 us
    ppermute x1, starting transfers between devices, shards(): rot_far = lax.ppermute(rot, 'core', SWAP)  13.8 us
    all_to_all x1, blocking collectives, shards(): left = lax.all_to_all(copies(left, n), ('x', 'zl'), 0, 0, tiled=True)  10.7 us
    all_to_all x1, blocking collectives, shards(): lax.all_to_all(left.reshape(n, -1, left.shape[1]), ('x', 'zl'), 0, 0, til...  10.4 us
    ppermute x1, starting transfers between devices, shards(): given_far = lax.ppermute(given, 'core', SWAP)  8.78 us
    ppermute x1, starting transfers between devices, shards(): kept_far = lax.ppermute(kept, AXES, PAIR_IN)  7.25 us
    ppermute x1, waiting for transfers between devices, shards(): total_far = lax.ppermute(total.astype(BF), AXES, PAIR_MID)  6.65 us
  transfers between devices with their start and end apart: 9, of which 3 were waited for; matrix products, arithmetic and copies ran while one was open for 2% of the time, Pallas kernels for 0%

profile of v4, /device:TPU:1, one launch (start us, length us, event | category | flops | bytes accessed | tf_op | source)
XLA Modules:
  0.0 145.0 jit_solution(16022280693725516064)
XLA Ops:
  0.0 0.8 fusion.14
  0.8 0.7 slice.72
  1.5 0.8 broadcast_select_fusion.3
  2.3 8.8 %collective-permute-start = (bf16[32,512]{1,0:T(8,128)(2,1)S(1)}, bf16[32,512]{1,0:T(8,128)(2,1)S(1)}, u32[]{:S(2)}, u32[]{:S(2)}) collective-permute-start(bf16[32,512]{1,0:T(8,128)(2,1)S(1)} %get-tuple-element.43), channel_id=1, source_target_pairs={{0,1},{1,0},{2,3},{3,2},{4,5},{5,4},{6,7},{7,6},{8,9},{9,8},{10,11... | collective-permute-start | bytes 98312 | tf_op jit(solution)/shard_map/ppermute | solution.py:58
  11.1 1.9 %collective-permute-start.2 = (bf16[32,512]{1,0:T(8,128)(2,1)S(1)}, bf16[32,512]{1,0:T(8,128)(2,1)S(1)}, u32[]{:S(2)}, u32[]{:S(2)}) collective-permute-start(bf16[32,512]{1,0:T(8,128)(2,1)S(1)} %get-tuple-element.43), channel_id=1, source_target_pairs={{0,3},{2,1},{4,7},{6,5},{8,11},{10,9},{12,15},{14,13},{16,19},{18,... | collective-permute-start | bytes 98312 | tf_op jit(solution)/shard_map/ppermute | solution.py:57
  13.0 7.3 %collective-permute-start.1 = (bf16[32,512]{1,0:T(8,128)(2,1)S(1)}, bf16[32,512]{1,0:T(8,128)(2,1)S(1)}, u32[]{:S(2)}, u32[]{:S(2)}) collective-permute-start(bf16[32,512]{1,0:T(8,128)(2,1)S(1)} %get-tuple-element.44), channel_id=1, source_target_pairs={{0,64},{64,0},{2,66},{66,2},{4,68},{68,4},{6,70},{70,6},{8,72},{72... | collective-permute-start | bytes 98312 | tf_op jit(solution)/shard_map/ppermute | solution.py:56
  20.4 2.7 %collective-permute-start.3 = (bf16[256,512]{1,0:T(8,128)(2,1)}, bf16[256,512]{1,0:T(8,128)(2,1)S(1)}, u32[]{:S(2)}, u32[]{:S(2)}) collective-permute-start(bf16[256,512]{1,0:T(8,128)(2,1)} %param.10), channel_id=1, source_target_pairs={{0,1},{1,0},{2,3},{3,2},{4,5},{5,4},{6,7},{7,6},{8,9},{9,8},{10,11... | collective-permute-start | bytes 786440 | tf_op jit(solution)/shard_map/ppermute | solution.py:72
  23.0 1.9 %collective-permute-start.4 = (bf16[512,256]{1,0:T(8,128)(2,1)}, bf16[512,256]{1,0:T(8,128)(2,1)S(1)}, u32[]{:S(2)}, u32[]{:S(2)}) collective-permute-start(bf16[512,256]{1,0:T(8,128)(2,1)} %param.11), channel_id=1, source_target_pairs={{0,1},{1,0},{2,3},{3,2},{4,5},{5,4},{6,7},{7,6},{8,9},{9,8},{10,11... | collective-permute-start | bytes 786440 | tf_op jit(solution)/shard_map/ppermute | solution.py:73
  25.0 2.4 %collective-permute-start.5 = (f32[256]{0:T(256)}, f32[256]{0:T(256)S(1)}, u32[]{:S(2)}, u32[]{:S(2)}) collective-permute-start(f32[256]{0:T(256)} %param.13), channel_id=1, source_target_pairs={{0,1},{1,0},{2,3},{3,2},{4,5},{5,4},{6,7},{7,6},{8,9},{9,8},{10,11... | collective-permute-start | bytes 3080 | tf_op jit(solution)/shard_map/ppermute | solution.py:78
  27.5 1.1 select_reduce_fusion
  28.6 0.7 multiply_select_fusion
  29.6 0.2 maximum_select_fusion.1
  30.0 24.4 %all_to_all.30 = bf16[8,2,64,512]{3,2,1,0:T(8,128)(2,1)S(1)} all-to-all(bf16[8,2,64,512]{3,2,1,0:T(8,128)(2,1)S(1)} %broadcast_in_dim.48), channel_id=1, replica_groups={{0,32,128,160,256,288,384,416},{2,34,130,162,258,290,386,418},{4,36,132..., dimensions={0} | all-to-all | bytes 2097152 | tf_op jit(solution)/shard_map/all_to_all | solution.py:37
  54.6 0.2 bitcast_select_fusion
  54.8 0.8 convolution_convert_fusion
  55.6 14.5 %all_to_all.31 = bf16[8,64,896]{2,1,0:T(8,128)(2,1)S(1)} all-to-all(bf16[8,64,896]{2,1,0:T(8,128)(2,1)S(1)} %bitcast.49), channel_id=1, replica_groups={{0,4,8,12,16,20,24,28},{2,6,10,14,18,22,26,30},{32,36,40,44,48,52,56,60..., dimensions={0} | all-to-all | bytes 1835008 | tf_op jit(solution)/shard_map/all_to_all | solution.py:37
  70.1 0.1 convert_reduce_fusion
  70.2 2.2 %collective-permute-start.6 = (bf16[64,896]{1,0:T(8,128)(2,1)S(1)}, bf16[64,896]{1,0:T(8,128)(2,1)S(1)}, u32[]{:S(2)}, u32[]{:S(2)}) collective-permute-start(bf16[64,896]{1,0:T(8,128)(2,1)S(1)} %convert_element_type.33), channel_id=1, source_target_pairs={{0,2},{2,0},{4,6},{6,4},{8,10},{10,8},{12,14},{14,12},{16,18},{18,... | collective-permute-start | bytes 344072 | tf_op jit(solution)/shard_map/ppermute | solution.py:97
  72.5 6.6 %collective-permute-done.6 = bf16[64,896]{1,0:T(8,128)(2,1)S(1)} collective-permute-done((bf16[64,896]{1,0:T(8,128)(2,1)S(1)}, bf16[64,896]{1,0:T(8,128)(2,1)S(1)}, u32[]{:S(2)}, u32[]{:S(2)}) %collective-permute-start.6) | collective-permute-done | bytes 114720 | tf_op jit(solution)/shard_map/ppermute | solution.py:97
  79.4 12.2 %all_to_all.32 = bf16[8,64,896]{2,1,0:T(8,128)(2,1)S(1)} all-to-all(bf16[8,64,896]{2,1,0:T(8,128)(2,1)S(1)} %broadcast_in_dim.49), channel_id=1, replica_groups={{0,4,8,12,16,20,24,28},{2,6,10,14,18,22,26,30},{32,36,40,44,48,52,56,60..., dimensions={0} | all-to-all | bytes 1835008 | tf_op jit(solution)/shard_map/all_to_all | solution.py:37
  91.5 13.8 %collective-permute-start.8 = (bf16[512,896]{1,0:T(8,128)(2,1)S(1)}, bf16[512,896]{1,0:T(8,128)(2,1)S(1)}, u32[]{:S(2)}, u32[]{:S(2)}) collective-permute-start(bf16[512,896]{1,0:T(8,128)(2,1)S(1)} %bitcast.47), channel_id=1, source_target_pairs={{0,1},{1,0},{2,3},{3,2},{4,5},{5,4},{6,7},{7,6},{8,9},{9,8},{10,11... | collective-permute-start | bytes 2752520 | tf_op jit(solution)/shard_map/ppermute | solution.py:106
  105.3 1.9 %collective-permute-start.7 = (bf16[64,512]{1,0:T(8,128)(2,1)S(1)}, bf16[64,512]{1,0:T(8,128)(2,1)S(1)}, u32[]{:S(2)}, u32[]{:S(2)}) collective-permute-start(bf16[64,512]{1,0:T(8,128)(2,1)S(1)} %reshape.276), channel_id=1, source_target_pairs={{0,1},{1,0},{2,3},{3,2},{4,5},{5,4},{6,7},{7,6},{8,9},{9,8},{10,11... | collective-permute-start | bytes 196616 | tf_op jit(solution)/shard_map/ppermute | solution.py:107
  107.2 0.1 collective-permute-done.8
  107.4 0.7 fusion
  108.1 0.3 collective-permute-done.7
  108.5 0.3 fusion.4
  108.7 0.2 convolution_select_fusion
  109.0 10.4 %all_to_all.33 = f32[16,4,512]{2,1,0:T(4,128)S(1)} all-to-all(f32[16,4,512]{2,1,0:T(4,128)S(1)} %reshape.279), channel_id=1, replica_groups=mesh['x'=4,'zl'=4,'y'=8,'zh'=2,'core'=2] {'x','zl'}, dimensions={0} | all-to-all | bytes 262144 | tf_op jit(solution)/shard_map/all_to_all | solution.py:114
  119.4 10.7 %all_to_all.34 = bf16[16,4,512]{2,1,0:T(4,128)(2,1)S(1)} all-to-all(bf16[16,4,512]{2,1,0:T(4,128)(2,1)S(1)} %broadcast_in_dim.50), channel_id=1, replica_groups=mesh['x'=4,'zl'=4,'y'=8,'zh'=2,'core'=2] {'x','zl'}, dimensions={0} | all-to-all | bytes 131072 | tf_op jit(solution)/shard_map/all_to_all | solution.py:116
  130.1 0.3 fusion.1
  130.5 13.9 %all_to_all.35 = f32[16,4,512]{2,1,0:T(4,128)S(1)} all-to-all(f32[16,4,512]{2,1,0:T(4,128)S(1)} %copy.23), channel_id=1, replica_groups={{0,4,8,12,16,20,24,28,2,6,10,14,18,22,26,30},{32,36,40,44,48,52,56,60,3..., dimensions={0} | all-to-all | bytes 262144 | tf_op jit(solution)/shard_map/all_to_all | solution.py:37
  144.4 0.6 reduce_sum.39
  (52 shorter events, 1.1 us)
Async XLA Ops:
  0.0 29.5 %copy-start.3 = (f32[256]{0:T(256)S(1)}, f32[256]{0:T(256)}, u32[]{:S(2)}) copy-start(f32[256]{0:T(256)} %param.13) | copy-start | bytes 3076
  0.0 29.6 %copy-start = (bf16[256,512]{1,0:T(8,128)(2,1)S(1)}, bf16[256,512]{1,0:T(8,128)(2,1)}, u32[]{:S(2)}) copy-start(bf16[256,512]{1,0:T(8,128)(2,1)} %param.10) | copy-start | bytes 786436
  0.0 29.6 %copy-start.1 = (bf16[512,256]{1,0:T(8,128)(2,1)S(1)}, bf16[512,256]{1,0:T(8,128)(2,1)}, u32[]{:S(2)}) copy-start(bf16[512,256]{1,0:T(8,128)(2,1)} %param.11) | copy-start | bytes 786436
  2.3 18.1 %collective-permute-start = (bf16[32,512]{1,0:T(8,128)(2,1)S(1)}, bf16[32,512]{1,0:T(8,128)(2,1)S(1)}, u32[]{:S(2)}, u32[]{:S(2)}) collective-permute-start(bf16[32,512]{1,0:T(8,128)(2,1)S(1)} %get-tuple-element.43), channel_id=1, source_target_pairs={{0,1},{1,0},{2,3},{3,2},{4,5},{5,4},{6,7},{7,6},{8,9},{9,8},{10,11... | collective-permute-start | bytes 98312 | tf_op jit(solution)/shard_map/ppermute | solution.py:58
  11.1 16.4 %collective-permute-start.2 = (bf16[32,512]{1,0:T(8,128)(2,1)S(1)}, bf16[32,512]{1,0:T(8,128)(2,1)S(1)}, u32[]{:S(2)}, u32[]{:S(2)}) collective-permute-start(bf16[32,512]{1,0:T(8,128)(2,1)S(1)} %get-tuple-element.43), channel_id=1, source_target_pairs={{0,3},{2,1},{4,7},{6,5},{8,11},{10,9},{12,15},{14,13},{16,19},{18,... | collective-permute-start | bytes 98312 | tf_op jit(solution)/shard_map/ppermute | solution.py:57
  13.0 14.4 %collective-permute-start.1 = (bf16[32,512]{1,0:T(8,128)(2,1)S(1)}, bf16[32,512]{1,0:T(8,128)(2,1)S(1)}, u32[]{:S(2)}, u32[]{:S(2)}) collective-permute-start(bf16[32,512]{1,0:T(8,128)(2,1)S(1)} %get-tuple-element.44), channel_id=1, source_target_pairs={{0,64},{64,0},{2,66},{66,2},{4,68},{68,4},{6,70},{70,6},{8,72},{72... | collective-permute-start | bytes 98312 | tf_op jit(solution)/shard_map/ppermute | solution.py:56
  20.4 9.2 %collective-permute-start.3 = (bf16[256,512]{1,0:T(8,128)(2,1)}, bf16[256,512]{1,0:T(8,128)(2,1)S(1)}, u32[]{:S(2)}, u32[]{:S(2)}) collective-permute-start(bf16[256,512]{1,0:T(8,128)(2,1)} %param.10), channel_id=1, source_target_pairs={{0,1},{1,0},{2,3},{3,2},{4,5},{5,4},{6,7},{7,6},{8,9},{9,8},{10,11... | collective-permute-start | bytes 786440 | tf_op jit(solution)/shard_map/ppermute | solution.py:72
  23.0 6.5 %collective-permute-start.4 = (bf16[512,256]{1,0:T(8,128)(2,1)}, bf16[512,256]{1,0:T(8,128)(2,1)S(1)}, u32[]{:S(2)}, u32[]{:S(2)}) collective-permute-start(bf16[512,256]{1,0:T(8,128)(2,1)} %param.11), channel_id=1, source_target_pairs={{0,1},{1,0},{2,3},{3,2},{4,5},{5,4},{6,7},{7,6},{8,9},{9,8},{10,11... | collective-permute-start | bytes 786440 | tf_op jit(solution)/shard_map/ppermute | solution.py:73
  25.0 4.6 %collective-permute-start.5 = (f32[256]{0:T(256)}, f32[256]{0:T(256)S(1)}, u32[]{:S(2)}, u32[]{:S(2)}) collective-permute-start(f32[256]{0:T(256)} %param.13), channel_id=1, source_target_pairs={{0,1},{1,0},{2,3},{3,2},{4,5},{5,4},{6,7},{7,6},{8,9},{9,8},{10,11... | collective-permute-start | bytes 3080 | tf_op jit(solution)/shard_map/ppermute | solution.py:78
  70.2 9.0 %collective-permute-start.6 = (bf16[64,896]{1,0:T(8,128)(2,1)S(1)}, bf16[64,896]{1,0:T(8,128)(2,1)S(1)}, u32[]{:S(2)}, u32[]{:S(2)}) collective-permute-start(bf16[64,896]{1,0:T(8,128)(2,1)S(1)} %convert_element_type.33), channel_id=1, source_target_pairs={{0,2},{2,0},{4,6},{6,4},{8,10},{10,8},{12,14},{14,12},{16,18},{18,... | collective-permute-start | bytes 344072 | tf_op jit(solution)/shard_map/ppermute | solution.py:97
  79.3 26.0 %copy-start.2 = (f32[512]{0:T(512)S(1)}, f32[512]{0:T(512)}, u32[]{:S(2)}) copy-start(f32[512]{0:T(512)} %param.12) | copy-start | bytes 6148
  91.5 15.9 %collective-permute-start.8 = (bf16[512,896]{1,0:T(8,128)(2,1)S(1)}, bf16[512,896]{1,0:T(8,128)(2,1)S(1)}, u32[]{:S(2)}, u32[]{:S(2)}) collective-permute-start(bf16[512,896]{1,0:T(8,128)(2,1)S(1)} %bitcast.47), channel_id=1, source_target_pairs={{0,1},{1,0},{2,3},{3,2},{4,5},{5,4},{6,7},{7,6},{8,9},{9,8},{10,11... | collective-permute-start | bytes 2752520 | tf_op jit(solution)/shard_map/ppermute | solution.py:106
  105.3 3.1 %collective-permute-start.7 = (bf16[64,512]{1,0:T(8,128)(2,1)S(1)}, bf16[64,512]{1,0:T(8,128)(2,1)S(1)}, u32[]{:S(2)}, u32[]{:S(2)}) collective-permute-start(bf16[64,512]{1,0:T(8,128)(2,1)S(1)} %reshape.276), channel_id=1, source_target_pairs={{0,1},{1,0},{2,3},{3,2},{4,5},{5,4},{6,7},{7,6},{8,9},{9,8},{10,11... | collective-permute-start | bytes 196616 | tf_op jit(solution)/shard_map/ppermute | solution.py:107

commit v5 on v4

--- a/solution.py
+++ b/solution.py
@@ -41,6 +41,14 @@
     return jnp.broadcast_to(block[None], (n, *block.shape))
 
 
+def three(value):
+    out = []
+    for _ in range(3):
+        out.append(lax.reduce_precision(value, 8, 7))
+        value = value - out[-1]
+    return [v.astype(BF) for v in out]
+
+
 def shards(out_grads, inputs, basis_out, basis_in, eig_out, eig_in, pair_order, length_bucket):
     tokens, share, block = pair_order.shape[0], inputs.shape[0], out_grads.shape[0]
     half = basis_in.shape[1]
@@ -67,26 +75,16 @@
     low = jnp.where(first, zl // 2, zh) == 0
     rows = jnp.stack([jnp.where(low, rows, rows_far), jnp.where(low, rows_far, rows)])
 
-    late = lax.optimization_barrier((given_far, basis_out, basis_in, eig_in, pair_order, length_bucket))
-    basis_out_late, basis_in_late, eig_late, pair_order, length_bucket = late[1:]
-    out_far = lax.ppermute(basis_out_late, "core", SWAP)
-    in_far = lax.ppermute(basis_in_late, "core", SWAP)
+    late = lax.optimization_barrier((given_far, basis_out, basis_in, eig_in))
+    out_far = lax.ppermute(late[1], "core", SWAP)
+    packed = jnp.concatenate([late[2], jnp.stack(three(late[3])), jnp.zeros((13, half), BF)], axis=0)
+    in_far, eig_far = jnp.split(lax.ppermute(packed, "core", SWAP), [basis_in.shape[0]])
     basis_in2 = jnp.where(
         first, jnp.concatenate([basis_in, in_far], axis=1), jnp.concatenate([in_far, basis_in], axis=1)
     )
     basis = jnp.where(first, jnp.concatenate([basis_out, out_far], axis=0), basis_in2)
-    eig_far = lax.ppermute(eig_late, "core", SWAP)
-    eig_in2 = jnp.where(first, jnp.concatenate([eig_in, eig_far]), jnp.concatenate([eig_far, eig_in]))
-    place = lax.broadcasted_iota(jnp.int32, (tokens, 1), 0)
-    token = lax.broadcasted_iota(jnp.int32, (1, tokens), 1)
-    parity = jnp.where(place % 2 == 0, 1.0, -1.0)
-    sign = jnp.sum(jnp.where(pair_order[:, None] == token, parity, 0.0), axis=0)
-    weights = sign / jnp.sqrt((1.0 + length_bucket.astype(F32)) * tokens)
-    weights = jnp.where(first, weights, 1.0)
-
-    rows, basis, basis_in2, eig_in2, weights = lax.optimization_barrier(
-        (rows, basis, basis_in2, eig_in2, weights)
-    )
+    parity = jnp.where(jnp.arange(tokens) % 2 == 0, 1.0, -1.0)
+    rows, basis, basis_in2, eig_far, parity = lax.optimization_barrier((rows, basis, basis_in2, eig_far, parity))
     rows = exchange(copies(rows, 8), EIGHT_IN)
     ordered = rows[:, :, :block].reshape(tokens, -1)
     paired = rows.reshape(4, 2, 2, 64, -1).swapaxes(1, 2)[:, :, :, :block].reshape(tokens, -1)
@@ -99,8 +97,17 @@
         rows[:, :, block + k * extra : block + (k + 1) * extra].swapaxes(0, 1).reshape(n * extra, -1)
         for k in range(2)
     )
+
+    late = lax.optimization_barrier((part, pair_order, length_bucket, eig_far))
+    _, pair_order, length_bucket, eig_far = late
+    token = lax.broadcasted_iota(jnp.int32, (1, tokens), 1)
+    sign = jnp.sum(jnp.where(pair_order[:, None] == token, parity[:, None], 0.0), axis=0)
+    weights = sign / jnp.sqrt((1.0 + length_bucket.astype(F32)) * tokens)
+    weights = jnp.where(first, weights, 1.0)
+    eig_far = jnp.sum(eig_far.astype(F32), axis=0)
+    eig_in2 = jnp.where(first, jnp.concatenate([eig_in, eig_far]), jnp.concatenate([eig_far, eig_in]))
     rot = ((total + total_far.astype(F32)) * weights).astype(BF)
-    rot, slab0, slab1 = lax.optimization_barrier((rot, slab0, slab1))
+    rot, slab0, slab1, eig_in2 = lax.optimization_barrier((rot, slab0, slab1, eig_in2))
     rot = exchange(copies(rot, 8), EIGHT_MID).reshape(-1, tokens)
     rot, slab0 = lax.optimization_barrier((rot, slab0))
     rot_far = lax.ppermute(rot, "core", SWAP)

time: 147 us -> 150 us (1.020)
  blocking collectives: 86 us -> 90.1 us
  local copies, waits for them, and re-layouts: 2.29 us -> 3.86 us
    ppermute x1, starting transfers between devices: 1.92 us -> 7.2 us  [shards(): cross_far = lax.ppermute(given, AXES, CROSS)]
    all_to_all x4, blocking collectives: 64.9 us -> 68.4 us  [exchange(): lax.all_to_all(parts, AXES, 0, 0, axis_index_groups=groups, tiled=True)]
    ppermute x1, starting transfers between devices: 7.25 us -> 4.19 us  [shards(): kept_far = lax.ppermute(kept, AXES, PAIR_IN)]
    ppermute x3 -> x2, starting transfers between devices: 7.02 us -> 4.46 us  [the longest x1 2.44 us: shards(): lax.ppermute(packed, 'core', SWAP)]
    ppermute x1, starting transfers between devices: 8.78 us -> 6.57 us  [shards(): given_far = lax.ppermute(given, 'core', SWAP)]
    ppermute x1, waiting for transfers between devices: 6.65 us -> 4.85 us  [shards(): total_far = lax.ppermute(total.astype(BF), AXES, PAIR_MID)]
  transfers between devices with their start and end apart: 9 -> 8, of which waited for: 3 -> 4; matrix products, arithmetic and copies ran while one was open for 2% -> 2% of each run, Pallas kernels for 0% -> 0%
where the time goes in v5:
time: 150 us; the launch traced here: 148 us
  blocking collectives  90.1 us (60%)
  starting transfers between devices  41.4 us (28%)
  waiting for transfers between devices  6.15 us (4%)
  local copies, waits for them, and re-layouts  3.86 us (3%)
  other arithmetic  3.38 us (2%)
  matrix products  2.25 us (2%)
    all_to_all x4, blocking collectives, exchange(): lax.all_to_all(parts, AXES, 0, 0, axis_index_groups=groups, tiled=True)  68.4 us
    ppermute x1, starting transfers between devices, shards(): rot_far = lax.ppermute(rot, 'core', SWAP)  14.9 us
    all_to_all x1, blocking collectives, shards(): lax.all_to_all(left.reshape(n, -1, left.shape[1]), ('x', 'zl'), 0, 0, til...  11 us
    all_to_all x1, blocking collectives, shards(): left = lax.all_to_all(copies(left, n), ('x', 'zl'), 0, 0, tiled=True)  10.7 us
    ppermute x1, starting transfers between devices, shards(): cross_far = lax.ppermute(given, AXES, CROSS)  7.2 us
    ppermute x1, starting transfers between devices, shards(): given_far = lax.ppermute(given, 'core', SWAP)  6.57 us
    ppermute x1, waiting for transfers between devices, shards(): total_far = lax.ppermute(total.astype(BF), AXES, PAIR_MID)  4.85 us
    ppermute x1, starting transfers between devices, shards(): kept_far = lax.ppermute(kept, AXES, PAIR_IN)  4.19 us
  transfers between devices with their start and end apart: 8, of which 4 were waited for; matrix products, arithmetic and copies ran while one was open for 2% of the time, Pallas kernels for 0%

profile of v5, /device:TPU:1, one launch (start us, length us, event | category | flops | bytes accessed | tf_op | source)
XLA Modules:
  0.0 147.7 jit_solution(13542645149786696234)
XLA Ops:
  0.0 0.7 slice.72
  0.7 0.7 fusion.16
  1.4 0.8 broadcast_select_fusion.3
  2.2 7.2 %collective-permute-start.2 = (bf16[32,512]{1,0:T(8,128)(2,1)S(1)}, bf16[32,512]{1,0:T(8,128)(2,1)S(1)}, u32[]{:S(2)}, u32[]{:S(2)}) collective-permute-start(bf16[32,512]{1,0:T(8,128)(2,1)S(1)} %get-tuple-element.47), channel_id=1, source_target_pairs={{0,3},{2,1},{4,7},{6,5},{8,11},{10,9},{12,15},{14,13},{16,19},{18,... | collective-permute-start | bytes 98312 | tf_op jit(solution)/shard_map/ppermute | solution.py:65
  9.4 6.6 %collective-permute-start = (bf16[32,512]{1,0:T(8,128)(2,1)S(1)}, bf16[32,512]{1,0:T(8,128)(2,1)S(1)}, u32[]{:S(2)}, u32[]{:S(2)}) collective-permute-start(bf16[32,512]{1,0:T(8,128)(2,1)S(1)} %get-tuple-element.47), channel_id=1, source_target_pairs={{0,1},{1,0},{2,3},{3,2},{4,5},{5,4},{6,7},{7,6},{8,9},{9,8},{10,11... | collective-permute-start | bytes 98312 | tf_op jit(solution)/shard_map/ppermute | solution.py:66
  16.0 4.2 %collective-permute-start.1 = (bf16[32,512]{1,0:T(8,128)(2,1)S(1)}, bf16[32,512]{1,0:T(8,128)(2,1)S(1)}, u32[]{:S(2)}, u32[]{:S(2)}) collective-permute-start(bf16[32,512]{1,0:T(8,128)(2,1)S(1)} %get-tuple-element.48), channel_id=1, source_target_pairs={{0,64},{64,0},{2,66},{66,2},{4,68},{68,4},{6,70},{70,6},{8,72},{72... | collective-permute-start | bytes 98312 | tf_op jit(solution)/shard_map/ppermute | solution.py:64
  20.3 0.7 fusion.11
  21.0 2.0 %collective-permute-start.3 = (bf16[256,512]{1,0:T(8,128)(2,1)}, bf16[256,512]{1,0:T(8,128)(2,1)S(1)}, u32[]{:S(2)}, u32[]{:S(2)}) collective-permute-start(bf16[256,512]{1,0:T(8,128)(2,1)} %param.10), channel_id=1, source_target_pairs={{0,1},{1,0},{2,3},{3,2},{4,5},{5,4},{6,7},{7,6},{8,9},{9,8},{10,11... | collective-permute-start | bytes 786440 | tf_op jit(solution)/shard_map/ppermute | solution.py:79
  23.0 1.1 concatenate.139
  24.2 2.4 %collective-permute-start.4 = (bf16[528,256]{1,0:T(8,128)(2,1)S(1)}, bf16[528,256]{1,0:T(8,128)(2,1)S(1)}, u32[]{:S(2)}, u32[]{:S(2)}) collective-permute-start(bf16[528,256]{1,0:T(8,128)(2,1)S(1)} %concatenate.139), channel_id=1, source_target_pairs={{0,1},{1,0},{2,3},{3,2},{4,5},{5,4},{6,7},{7,6},{8,9},{9,8},{10,11... | collective-permute-start | bytes 811016 | tf_op jit(solution)/shard_map/ppermute | solution.py:81
  27.0 0.8 collective-permute-done.4
  27.9 0.2 maximum_select_fusion.1
  28.1 0.4 copy-done.2
  28.6 24.4 %all_to_all.30 = bf16[8,2,64,512]{3,2,1,0:T(8,128)(2,1)S(1)} all-to-all(bf16[8,2,64,512]{3,2,1,0:T(8,128)(2,1)S(1)} %broadcast_in_dim.51), channel_id=1, replica_groups={{0,32,128,160,256,288,384,416},{2,34,130,162,258,290,386,418},{4,36,132..., dimensions={0} | all-to-all | bytes 2097152 | tf_op jit(solution)/shard_map/all_to_all | solution.py:37
  53.2 0.2 bitcast_select_fusion
  53.5 0.8 convolution_convert_fusion
  54.2 14.6 %all_to_all.31 = bf16[8,64,896]{2,1,0:T(8,128)(2,1)S(1)} all-to-all(bf16[8,64,896]{2,1,0:T(8,128)(2,1)S(1)} %bitcast.49), channel_id=1, replica_groups={{0,4,8,12,16,20,24,28},{2,6,10,14,18,22,26,30},{32,36,40,44,48,52,56,60..., dimensions={0} | all-to-all | bytes 1835008 | tf_op jit(solution)/shard_map/all_to_all | solution.py:37
  69.0 2.2 %collective-permute-start.5 = (bf16[64,896]{1,0:T(8,128)(2,1)S(1)}, bf16[64,896]{1,0:T(8,128)(2,1)S(1)}, u32[]{:S(2)}, u32[]{:S(2)}) collective-permute-start(bf16[64,896]{1,0:T(8,128)(2,1)S(1)} %convert_element_type.47), channel_id=1, source_target_pairs={{0,2},{2,0},{4,6},{6,4},{8,10},{10,8},{12,14},{14,12},{16,18},{18,... | collective-permute-start | bytes 344072 | tf_op jit(solution)/shard_map/ppermute | solution.py:95
  71.2 0.4 select_reduce_fusion
  71.9 4.9 %collective-permute-done.5 = bf16[64,896]{1,0:T(8,128)(2,1)S(1)} collective-permute-done((bf16[64,896]{1,0:T(8,128)(2,1)S(1)}, bf16[64,896]{1,0:T(8,128)(2,1)S(1)}, u32[]{:S(2)}, u32[]{:S(2)}) %collective-permute-start.5) | collective-permute-done | bytes 114720 | tf_op jit(solution)/shard_map/ppermute | solution.py:95
  76.9 12.2 %all_to_all.32 = bf16[8,64,896]{2,1,0:T(8,128)(2,1)S(1)} all-to-all(bf16[8,64,896]{2,1,0:T(8,128)(2,1)S(1)} %broadcast_in_dim.54), channel_id=1, replica_groups={{0,4,8,12,16,20,24,28},{2,6,10,14,18,22,26,30},{32,36,40,44,48,52,56,60..., dimensions={0} | all-to-all | bytes 1835008 | tf_op jit(solution)/shard_map/all_to_all | solution.py:37
  89.0 14.9 %collective-permute-start.7 = (bf16[512,896]{1,0:T(8,128)(2,1)S(1)}, bf16[512,896]{1,0:T(8,128)(2,1)S(1)}, u32[]{:S(2)}, u32[]{:S(2)}) collective-permute-start(bf16[512,896]{1,0:T(8,128)(2,1)S(1)} %bitcast.47), channel_id=1, source_target_pairs={{0,1},{1,0},{2,3},{3,2},{4,5},{5,4},{6,7},{7,6},{8,9},{9,8},{10,11... | collective-permute-start | bytes 2752520 | tf_op jit(solution)/shard_map/ppermute | solution.py:113
  103.9 1.9 %collective-permute-start.6 = (bf16[64,512]{1,0:T(8,128)(2,1)S(1)}, bf16[64,512]{1,0:T(8,128)(2,1)S(1)}, u32[]{:S(2)}, u32[]{:S(2)}) collective-permute-start(bf16[64,512]{1,0:T(8,128)(2,1)S(1)} %reshape.258), channel_id=1, source_target_pairs={{0,1},{1,0},{2,3},{3,2},{4,5},{5,4},{6,7},{7,6},{8,9},{9,8},{10,11... | collective-permute-start | bytes 196616 | tf_op jit(solution)/shard_map/ppermute | solution.py:114
  106.0 0.7 fusion
  106.7 0.3 collective-permute-done.6
  107.1 0.3 fusion.4
  107.4 0.2 convolution_select_fusion
  107.6 11.0 %all_to_all.33 = f32[16,4,512]{2,1,0:T(4,128)S(1)} all-to-all(f32[16,4,512]{2,1,0:T(4,128)S(1)} %reshape.261), channel_id=1, replica_groups=mesh['x'=4,'zl'=4,'y'=8,'zh'=2,'core'=2] {'x','zl'}, dimensions={0} | all-to-all | bytes 262144 | tf_op jit(solution)/shard_map/all_to_all | solution.py:121
  118.7 10.7 %all_to_all.34 = bf16[16,4,512]{2,1,0:T(4,128)(2,1)S(1)} all-to-all(bf16[16,4,512]{2,1,0:T(4,128)(2,1)S(1)} %broadcast_in_dim.55), channel_id=1, replica_groups=mesh['x'=4,'zl'=4,'y'=8,'zh'=2,'core'=2] {'x','zl'}, dimensions={0} | all-to-all | bytes 131072 | tf_op jit(solution)/shard_map/all_to_all | solution.py:123
  129.4 0.3 fusion.1
  129.8 17.3 %all_to_all.35 = f32[16,4,512]{2,1,0:T(4,128)S(1)} all-to-all(f32[16,4,512]{2,1,0:T(4,128)S(1)} %copy.23), channel_id=1, replica_groups={{0,4,8,12,16,20,24,28,2,6,10,14,18,22,26,30},{32,36,40,44,48,52,56,60,3..., dimensions={0} | all-to-all | bytes 262144 | tf_op jit(solution)/shard_map/all_to_all | solution.py:37
  147.0 0.6 reduce_sum.49
  (66 shorter events, 1.4 us)
Async XLA Ops:
  2.2 24.5 %collective-permute-start.2 = (bf16[32,512]{1,0:T(8,128)(2,1)S(1)}, bf16[32,512]{1,0:T(8,128)(2,1)S(1)}, u32[]{:S(2)}, u32[]{:S(2)}) collective-permute-start(bf16[32,512]{1,0:T(8,128)(2,1)S(1)} %get-tuple-element.47), channel_id=1, source_target_pairs={{0,3},{2,1},{4,7},{6,5},{8,11},{10,9},{12,15},{14,13},{16,19},{18,... | collective-permute-start | bytes 98312 | tf_op jit(solution)/shard_map/ppermute | solution.py:65
  9.4 10.9 %collective-permute-start = (bf16[32,512]{1,0:T(8,128)(2,1)S(1)}, bf16[32,512]{1,0:T(8,128)(2,1)S(1)}, u32[]{:S(2)}, u32[]{:S(2)}) collective-permute-start(bf16[32,512]{1,0:T(8,128)(2,1)S(1)} %get-tuple-element.47), channel_id=1, source_target_pairs={{0,1},{1,0},{2,3},{3,2},{4,5},{5,4},{6,7},{7,6},{8,9},{9,8},{10,11... | collective-permute-start | bytes 98312 | tf_op jit(solution)/shard_map/ppermute | solution.py:66
  16.0 10.7 %collective-permute-start.1 = (bf16[32,512]{1,0:T(8,128)(2,1)S(1)}, bf16[32,512]{1,0:T(8,128)(2,1)S(1)}, u32[]{:S(2)}, u32[]{:S(2)}) collective-permute-start(bf16[32,512]{1,0:T(8,128)(2,1)S(1)} %get-tuple-element.48), channel_id=1, source_target_pairs={{0,64},{64,0},{2,66},{66,2},{4,68},{68,4},{6,70},{70,6},{8,72},{72... | collective-permute-start | bytes 98312 | tf_op jit(solution)/shard_map/ppermute | solution.py:64
  21.0 6.8 %collective-permute-start.3 = (bf16[256,512]{1,0:T(8,128)(2,1)}, bf16[256,512]{1,0:T(8,128)(2,1)S(1)}, u32[]{:S(2)}, u32[]{:S(2)}) collective-permute-start(bf16[256,512]{1,0:T(8,128)(2,1)} %param.10), channel_id=1, source_target_pairs={{0,1},{1,0},{2,3},{3,2},{4,5},{5,4},{6,7},{7,6},{8,9},{9,8},{10,11... | collective-permute-start | bytes 786440 | tf_op jit(solution)/shard_map/ppermute | solution.py:79
  24.2 3.7 %copy-start = (bf16[512,256]{1,0:T(8,128)(2,1)S(1)}, bf16[512,256]{1,0:T(8,128)(2,1)}, u32[]{:S(2)}) copy-start(bf16[512,256]{1,0:T(8,128)(2,1)} %param.11) | copy-start | bytes 786436
  24.2 3.7 %copy-start.1 = (bf16[256,512]{1,0:T(8,128)(2,1)S(1)}, bf16[256,512]{1,0:T(8,128)(2,1)}, u32[]{:S(2)}) copy-start(bf16[256,512]{1,0:T(8,128)(2,1)} %param.10) | copy-start | bytes 786436
  24.2 3.6 %collective-permute-start.4 = (bf16[528,256]{1,0:T(8,128)(2,1)S(1)}, bf16[528,256]{1,0:T(8,128)(2,1)S(1)}, u32[]{:S(2)}, u32[]{:S(2)}) collective-permute-start(bf16[528,256]{1,0:T(8,128)(2,1)S(1)} %concatenate.139), channel_id=1, source_target_pairs={{0,1},{1,0},{2,3},{3,2},{4,5},{5,4},{6,7},{7,6},{8,9},{9,8},{10,11... | collective-permute-start | bytes 811016 | tf_op jit(solution)/shard_map/ppermute | solution.py:81
  27.8 0.7 copy-start.2
  68.8 2.4 %copy-start.3 = (s32[896]{0:T(1024)S(1)}, s32[896]{0:T(1024)}, u32[]{:S(2)}) copy-start(s32[896]{0:T(1024)} %param.14) | copy-start | bytes 10756
  68.8 2.8 %copy-start.4 = (s32[896]{0:T(1024)S(1)}, s32[896]{0:T(1024)}, u32[]{:S(2)}) copy-start(s32[896]{0:T(1024)} %param.15) | copy-start | bytes 10756
  68.8 2.9 %slice-start = ((bf16[528,256]{1,0:T(8,128)(2,1)}), bf16[16,256]{1,0:T(8,128)(2,1)S(1)}, s32[]{:S(2)}) async-start(bf16[528,256]{1,0:T(8,128)(2,1)} %copy-done.2), calls=%async_computation.6 | async-start | bytes 16384 | tf_op jit(solution)/shard_map/split | solution.py:81
  68.9 2.9 %copy-start.5 = (f32[256]{0:T(256)S(1)}, f32[256]{0:T(256)}, u32[]{:S(2)}) copy-start(f32[256]{0:T(256)} %param.13) | copy-start | bytes 3076
  69.0 7.7 %collective-permute-start.5 = (bf16[64,896]{1,0:T(8,128)(2,1)S(1)}, bf16[64,896]{1,0:T(8,128)(2,1)S(1)}, u32[]{:S(2)}, u32[]{:S(2)}) collective-permute-start(bf16[64,896]{1,0:T(8,128)(2,1)S(1)} %convert_element_type.47), channel_id=1, source_target_pairs={{0,2},{2,0},{4,6},{6,4},{8,10},{10,8},{12,14},{14,12},{16,18},{18,... | collective-permute-start | bytes 344072 | tf_op jit(solution)/shard_map/ppermute | solution.py:95
  76.9 27.0 %copy-start.6 = (f32[512]{0:T(512)S(1)}, f32[512]{0:T(512)}, u32[]{:S(2)}) copy-start(f32[512]{0:T(512)} %param.12) | copy-start | bytes 6148
  89.0 16.9 %collective-permute-start.7 = (bf16[512,896]{1,0:T(8,128)(2,1)S(1)}, bf16[512,896]{1,0:T(8,128)(2,1)S(1)}, u32[]{:S(2)}, u32[]{:S(2)}) collective-permute-start(bf16[512,896]{1,0:T(8,128)(2,1)S(1)} %bitcast.47), channel_id=1, source_target_pairs={{0,1},{1,0},{2,3},{3,2},{4,5},{5,4},{6,7},{7,6},{8,9},{9,8},{10,11... | collective-permute-start | bytes 2752520 | tf_op jit(solution)/shard_map/ppermute | solution.py:113
  103.9 3.1 %collective-permute-start.6 = (bf16[64,512]{1,0:T(8,128)(2,1)S(1)}, bf16[64,512]{1,0:T(8,128)(2,1)S(1)}, u32[]{:S(2)}, u32[]{:S(2)}) collective-permute-start(bf16[64,512]{1,0:T(8,128)(2,1)S(1)} %reshape.258), channel_id=1, source_target_pairs={{0,1},{1,0},{2,3},{3,2},{4,5},{5,4},{6,7},{7,6},{8,9},{9,8},{10,11... | collective-permute-start | bytes 196616 | tf_op jit(solution)/shard_map/ppermute | solution.py:114

commit v6 on v5

v6 whole, which is shorter than its diff:
```python
import jax
import jax.numpy as jnp
import numpy as np
from jax import lax
from jax.sharding import Mesh, PartitionSpec as P

DAMPING = 0.1
AXES = ("x", "zl", "y", "zh", "core")
SIZES = (4, 4, 8, 2, 2)
BF = jnp.bfloat16
F32 = jnp.float32
SWAP = [(0, 1), (1, 0)]

INDEX = np.arange(512).reshape(4, 2, 2, 8, 2, 2)


def lists(order, size):
    return INDEX.transpose(order).reshape(2, -1, size).tolist()


ROW_PAIR, ROW_EIGHT = lists((5, 0, 2, 3, 4, 1), 2), lists((5, 1, 3, 4, 0, 2), 8)
COL_PAIR, COL_EIGHT = lists((5, 0, 1, 2, 3, 4), 2), lists((5, 0, 1, 2, 4, 3), 8)
COL_ALL = lists((5, 0, 1, 2, 4, 3), 16)
EIGHT_IN = ROW_EIGHT[0] + COL_EIGHT[1]
EIGHT_MID = COL_EIGHT[0] + ROW_EIGHT[1]
PAIR_IN = [(g[i], g[1 - i]) for g in ROW_PAIR[0] + COL_PAIR[1] for i in range(2)]
PAIR_MID = [(g[i], g[1 - i]) for g in COL_PAIR[0] + ROW_PAIR[1] for i in range(2)]


def dot(a, b, contract):
    return lax.dot_general(a, b, (contract, ((), ())), preferred_element_type=F32)


def exchange(parts, groups):
    return lax.all_to_all(parts, AXES, 0, 0, axis_index_groups=groups, tiled=True)


def copies(block, n):
    return jnp.broadcast_to(block[None], (n, *block.shape))


def wide(tall_one):
    rows = tall_one.shape[0] // 2
    return jnp.concatenate([tall_one[:rows], tall_one[rows:]], axis=1)


def tall(wide_one):
    lanes = wide_one.shape[1] // 2
    return jnp.concatenate([wide_one[:, :lanes], wide_one[:, lanes:]], axis=0)


def three(value):
    out = []
    for _ in range(3):
        out.append(lax.reduce_precision(value, 8, 7))
        value = value - out[-1]
    return [v.astype(BF) for v in out]


def shards(out_grads, inputs, basis_out, basis_in, eig_out, eig_in, pair_order, length_bucket):
    tokens, share, block = pair_order.shape[0], inputs.shape[0], out_grads.shape[0]
    half = basis_in.shape[1]
    extra = 32 - share
    n = 16
    first = lax.axis_index("core") == 0
    zh, zl = lax.axis_index("zh"), lax.axis_index("zl")

    acts = jnp.concatenate([inputs, basis_out[:extra]], axis=0)
    grads = jnp.pad(out_grads, ((0, 64 - block), (0, 0)))
    grads = jnp.concatenate([grads[:32], grads[32:]], axis=1)
    kept = jnp.where(first, grads, acts)
    far = jnp.where(
        first, jnp.concatenate([acts, wide(basis_in)], axis=0), jnp.concatenate([grads, basis_out], axis=0)
    )
    far = lax.ppermute(far, "core", SWAP)
    far, basis_far = far[:32], far[32:]
    lanes = [[p[:, :half], p[:, half:]] for p in (kept, far)]
    as_grads = jnp.concatenate([jnp.concatenate(p, axis=0) for p in lanes], axis=1)
    as_acts = jnp.concatenate([far[:share], kept[:share], far[share:], kept[share:]], axis=0)
    rows = jnp.where(first, as_grads, as_acts)

    rows_far = lax.ppermute(rows, AXES, PAIR_IN)
    basis = jnp.where(
        first,
        jnp.concatenate([basis_out, basis_far], axis=0),
        jnp.concatenate([tall(basis_far), basis_in], axis=1),
    )
    low = jnp.where(first, zl // 2, zh) == 0
    rows = jnp.stack([jnp.where(low, rows, rows_far), jnp.where(low, rows_far, rows)])
    parity = jnp.where(jnp.arange(tokens) % 2 == 0, 1.0, -1.0)
    rows, basis, parity = lax.optimization_barrier((rows, basis, parity))
    rows = exchange(copies(rows, 8), EIGHT_IN)
    ordered = rows[:, :, :block].reshape(tokens, -1)
    paired = rows.reshape(4, 2, 2, 64, -1).swapaxes(1, 2)[:, :, :, :block].reshape(tokens, -1)
    part = dot(basis, jnp.where(first, paired, ordered), ((0,), (1,))).astype(BF)
    part = exchange(part.reshape(8, -1, tokens), EIGHT_MID)
    total = jnp.sum(part.astype(F32), axis=0)

    sent, *late = lax.optimization_barrier((total.astype(BF), pair_order, length_bucket))
    pair_order, length_bucket = late
    total_far = lax.ppermute(sent, AXES, PAIR_MID)
    token = lax.broadcasted_iota(jnp.int32, (1, tokens), 1)
    sign = jnp.sum(jnp.where(pair_order[:, None] == token, parity[:, None], 0.0), axis=0)
    weights = sign / jnp.sqrt((1.0 + length_bucket.astype(F32)) * tokens)
    weights = jnp.where(first, weights, 1.0)
    weights, rows, in_late, eig_late = lax.optimization_barrier((weights, rows, basis_in, eig_in))
    slab0, slab1 = (
        rows[:, :, block + k * extra : block + (k + 1) * extra].swapaxes(0, 1).reshape(n * extra, -1)
        for k in range(2)
    )
    eig3 = jnp.concatenate([*three(eig_late), jnp.zeros((half,), BF)]).reshape(2, 2 * half)
    packed = jnp.concatenate([slab0, wide(in_late), jnp.pad(eig3, ((0, 14), (0, 0)))], axis=0)
    rot = ((total + total_far.astype(F32)) * weights).astype(BF)
    rot, packed, slab1 = lax.optimization_barrier((rot, packed, slab1))
    rot = exchange(copies(rot, 8), EIGHT_MID).reshape(-1, tokens)
    rot, packed = lax.optimization_barrier((rot, packed))
    rot_far = lax.ppermute(rot, "core", SWAP)
    far = lax.ppermute(packed, "core", SWAP)
    slab = jnp.where(first, far[: slab1.shape[0]], slab1)
    eig_far = far[-16:-14].astype(F32).reshape(4, half)
    eig_far = eig_far[0] + eig_far[1] + eig_far[2]
    eig_in2 = jnp.where(first, jnp.concatenate([eig_in, eig_far]), jnp.concatenate([eig_far, eig_in]))
    in_far = tall(far[slab1.shape[0] : -16])
    basis_in2 = jnp.where(
        first, jnp.concatenate([basis_in, in_far], axis=1), jnp.concatenate([in_far, basis_in], axis=1)
    )

    middle = dot(rot, rot_far, ((1,), (1,)))
    down, across = jnp.where(first, eig_out, eig_in2), jnp.where(first, eig_in2, eig_out)
    scaled = (middle / (down[:, None] * across[None, :] + DAMPING)).astype(BF)
    left = jnp.where(first, dot(slab, scaled, ((1,), (0,))), dot(slab, scaled, ((1,), (1,))))

    left, basis_in2 = lax.optimization_barrier((left, basis_in2))
    left = lax.all_to_all(left.reshape(n, -1, left.shape[1]), ("x", "zl"), 0, 0, tiled=True)
    left = jnp.sum(left, axis=0).astype(BF)
    left = lax.all_to_all(copies(left, n), ("x", "zl"), 0, 0, tiled=True)
    left = left.reshape(-1, left.shape[2])
    final = dot(left, basis_in2, ((1,), (1,)))
    final = exchange(final.reshape(n, -1, final.shape[1]), COL_ALL[0] + COL_ALL[1])
    return jnp.sum(final, axis=0)


def solution(mesh):
    fine = Mesh(mesh.devices.reshape(SIZES), AXES)
    row, col = AXES[:2], AXES[2:]
    return jax.shard_map(
        shards,
        mesh=fine,
        in_specs=(P(row, col), P(col, row), P(col, row), P(row, col), P(row), P(col), P(), P()),
        out_specs=P(col, row),
        check_vma=False,
    )
```

time: 150 us -> 146 us (0.973)
  starting transfers between devices: 41.4 us -> 33.9 us
  waiting for transfers between devices: 6.15 us -> 10.4 us
    ppermute x1, starting transfers between devices: 14.9 us -> 1.92 us  [shards(): rot_far = lax.ppermute(rot, 'core', SWAP)]
    ppermute x7 -> x4, starting transfers between devices: 26.5 us -> 32 us  [the longest x1 14 us: shards(): far = lax.ppermute(packed, 'core', SWAP)]
    ppermute x7 -> x4, waiting for transfers between devices: 6.03 us -> 8.22 us  [the longest x1 3.7 us: shards(): total_far = lax.ppermute(sent, AXES, PAIR_MID)]
    ppermute x1, waiting for transfers between devices: 0.13 us -> 2.2 us  [shards(): rot_far = lax.ppermute(rot, 'core', SWAP)]
  transfers between devices with their start and end apart: 8 -> 5, of which waited for: 4 -> 4; matrix products, arithmetic and copies ran while one was open for 2% -> 0% of each run, Pallas kernels for 0% -> 0%
where the time goes in v6:
time: 146 us; the launch traced here: 143 us
  blocking collectives  89.4 us (61%)
  starting transfers between devices  33.9 us (23%)
  waiting for transfers between devices  10.4 us (7%)
  local copies, waits for them, and re-layouts  3.84 us (3%)
  other arithmetic  2.99 us (2%)
  matrix products  2.26 us (2%)
    all_to_all x4, blocking collectives, exchange(): lax.all_to_all(parts, AXES, 0, 0, axis_index_groups=groups, tiled=True)  67 us
    ppermute x1, starting transfers between devices, shards(): far = lax.ppermute(packed, 'core', SWAP)  14 us
    all_to_all x1, blocking collectives, shards(): lax.all_to_all(left.reshape(n, -1, left.shape[1]), ('x', 'zl'), 0, 0, til...  11.7 us
    all_to_all x1, blocking collectives, shards(): left = lax.all_to_all(copies(left, n), ('x', 'zl'), 0, 0, tiled=True)  10.7 us
    ppermute x1, starting transfers between devices, shards(): far = lax.ppermute(far, 'core', SWAP)  8.79 us
    ppermute x1, starting transfers between devices, shards(): rows_far = lax.ppermute(rows, AXES, PAIR_IN)  5.26 us
    ppermute x1, starting transfers between devices, shards(): total_far = lax.ppermute(sent, AXES, PAIR_MID)  3.93 us
    ppermute x1, waiting for transfers between devices, shards(): total_far = lax.ppermute(sent, AXES, PAIR_MID)  3.7 us
  transfers between devices with their start and end apart: 5, of which 4 were waited for; matrix products, arithmetic and copies ran while one was open for 0% of the time, Pallas kernels for 0%

profile of v6, /device:TPU:1, one launch (start us, length us, event | category | flops | bytes accessed | tf_op | source)
XLA Modules:
  0.0 143.2 jit_solution(8469723306640600856)
XLA Ops:
  0.0 0.7 fusion.22
  0.7 1.0 fusion.20
  1.7 0.7 slice.100
  2.4 1.1 maximum_select_fusion
  3.5 8.8 %collective-permute-start = (bf16[288,512]{1,0:T(8,128)(2,1)S(1)}, bf16[288,512]{1,0:T(8,128)(2,1)S(1)}, u32[]{:S(2)}, u32[]{:S(2)}) collective-permute-start(bf16[288,512]{1,0:T(8,128)(2,1)S(1)} %maximum_select_fusion), channel_id=1, source_target_pairs={{0,1},{1,0},{2,3},{3,2},{4,5},{5,4},{6,7},{7,6},{8,9},{9,8},{10,11... | collective-permute-start | bytes 884744 | tf_op jit(solution)/shard_map/ppermute | solution.py:75
  12.4 1.1 collective-permute-done
  13.6 5.3 %collective-permute-start.1 = (bf16[64,512]{1,0:T(8,128)(2,1)S(1)}, bf16[64,512]{1,0:T(8,128)(2,1)S(1)}, u32[]{:S(2)}, u32[]{:S(2)}) collective-permute-start(bf16[64,512]{1,0:T(8,128)(2,1)S(1)} %maximum_select_fusion.1), channel_id=1, source_target_pairs={{0,64},{64,0},{2,66},{66,2},{4,68},{68,4},{6,70},{70,6},{8,72},{72... | collective-permute-start | bytes 196616 | tf_op jit(solution)/shard_map/ppermute | solution.py:82
  18.9 0.1 fusion.2
  19.1 3.4 %collective-permute-done.1 = bf16[64,512]{1,0:T(8,128)(2,1)S(1)} collective-permute-done((bf16[64,512]{1,0:T(8,128)(2,1)S(1)}, bf16[64,512]{1,0:T(8,128)(2,1)S(1)}, u32[]{:S(2)}, u32[]{:S(2)}) %collective-permute-start.1) | collective-permute-done | bytes 65568 | tf_op jit(solution)/shard_map/ppermute | solution.py:82
  22.6 22.4 %all_to_all.30 = bf16[8,2,64,512]{3,2,1,0:T(8,128)(2,1)S(1)} all-to-all(bf16[8,2,64,512]{3,2,1,0:T(8,128)(2,1)S(1)} %broadcast_in_dim.50), channel_id=1, replica_groups={{0,32,128,160,256,288,384,416},{2,34,130,162,258,290,386,418},{4,36,132..., dimensions={0} | all-to-all | bytes 2097152 | tf_op jit(solution)/shard_map/all_to_all | solution.py:35
  45.3 0.2 bitcast_select_fusion
  45.5 0.8 convolution_convert_fusion
  46.3 14.6 %all_to_all.31 = bf16[8,64,896]{2,1,0:T(8,128)(2,1)S(1)} all-to-all(bf16[8,64,896]{2,1,0:T(8,128)(2,1)S(1)} %bitcast.31), channel_id=1, replica_groups={{0,4,8,12,16,20,24,28},{2,6,10,14,18,22,26,30},{32,36,40,44,48,52,56,60..., dimensions={0} | all-to-all | bytes 1835008 | tf_op jit(solution)/shard_map/all_to_all | solution.py:35
  60.9 0.1 convert_reduce_fusion
  61.0 0.5 copy-done.3
  61.6 0.4 select_reduce_fusion
  62.3 3.9 %collective-permute-start.2 = (bf16[64,896]{1,0:T(8,128)(2,1)S(1)}, bf16[64,896]{1,0:T(8,128)(2,1)S(1)}, u32[]{:S(2)}, u32[]{:S(2)}) collective-permute-start(bf16[64,896]{1,0:T(8,128)(2,1)S(1)} %convert_element_type.44), channel_id=1, source_target_pairs={{0,2},{2,0},{4,6},{6,4},{8,10},{10,8},{12,14},{14,12},{16,18},{18,... | collective-permute-start | bytes 344072 | tf_op jit(solution)/shard_map/ppermute | solution.py:101
  66.2 3.7 %collective-permute-done.2 = bf16[64,896]{1,0:T(8,128)(2,1)S(1)} collective-permute-done((bf16[64,896]{1,0:T(8,128)(2,1)S(1)}, bf16[64,896]{1,0:T(8,128)(2,1)S(1)}, u32[]{:S(2)}, u32[]{:S(2)}) %collective-permute-start.2) | collective-permute-done | bytes 114720 | tf_op jit(solution)/shard_map/ppermute | solution.py:101
  70.0 0.1 broadcast_in_dim.54
  70.1 12.2 %all_to_all.32 = bf16[8,64,896]{2,1,0:T(8,128)(2,1)S(1)} all-to-all(bf16[8,64,896]{2,1,0:T(8,128)(2,1)S(1)} %broadcast_in_dim.54), channel_id=1, replica_groups={{0,4,8,12,16,20,24,28},{2,6,10,14,18,22,26,30},{32,36,40,44,48,52,56,60..., dimensions={0} | all-to-all | bytes 1835008 | tf_op jit(solution)/shard_map/all_to_all | solution.py:35
  82.3 14.0 %collective-permute-start.3 = (bf16[336,512]{1,0:T(8,128)(2,1)S(1)}, bf16[336,512]{1,0:T(8,128)(2,1)S(1)}, u32[]{:S(2)}, u32[]{:S(2)}) collective-permute-start(bf16[336,512]{1,0:T(8,128)(2,1)S(1)} %fusion.6), channel_id=1, source_target_pairs={{0,1},{1,0},{2,3},{3,2},{4,5},{5,4},{6,7},{7,6},{8,9},{9,8},{10,11... | collective-permute-start | bytes 1032200 | tf_op jit(solution)/shard_map/ppermute | solution.py:118
  96.3 1.9 %collective-permute-start.4 = (bf16[512,896]{1,0:T(8,128)(2,1)S(1)}, bf16[512,896]{1,0:T(8,128)(2,1)S(1)}, u32[]{:S(2)}, u32[]{:S(2)}) collective-permute-start(bf16[512,896]{1,0:T(8,128)(2,1)S(1)} %bitcast.29), channel_id=1, source_target_pairs={{0,1},{1,0},{2,3},{3,2},{4,5},{5,4},{6,7},{7,6},{8,9},{9,8},{10,11... | collective-permute-start | bytes 2752520 | tf_op jit(solution)/shard_map/ppermute | solution.py:117
  98.3 0.1 fusion.3
  98.5 2.2 %collective-permute-done.4 = bf16[512,896]{1,0:T(8,128)(2,1)S(1)} collective-permute-done((bf16[512,896]{1,0:T(8,128)(2,1)S(1)}, bf16[512,896]{1,0:T(8,128)(2,1)S(1)}, u32[]{:S(2)}, u32[]{:S(2)}) %collective-permute-start.4) | collective-permute-done | bytes 917536 | tf_op jit(solution)/shard_map/ppermute | solution.py:117
  100.7 0.7 fusion
  101.4 0.3 fusion.8
  101.7 0.2 convolution_select_fusion
  102.0 11.7 %all_to_all.33 = f32[16,4,512]{2,1,0:T(4,128)S(1)} all-to-all(f32[16,4,512]{2,1,0:T(4,128)S(1)} %reshape.59), channel_id=1, replica_groups=mesh['x'=4,'zl'=4,'y'=8,'zh'=2,'core'=2] {'x','zl'}, dimensions={0} | all-to-all | bytes 262144 | tf_op jit(solution)/shard_map/all_to_all | solution.py:134
  113.7 10.7 %all_to_all.34 = bf16[16,4,512]{2,1,0:T(4,128)(2,1)S(1)} all-to-all(bf16[16,4,512]{2,1,0:T(4,128)(2,1)S(1)} %broadcast_in_dim.55), channel_id=1, replica_groups=mesh['x'=4,'zl'=4,'y'=8,'zh'=2,'core'=2] {'x','zl'}, dimensions={0} | all-to-all | bytes 131072 | tf_op jit(solution)/shard_map/all_to_all | solution.py:136
  124.4 0.3 fusion.4
  124.8 17.9 %all_to_all.35 = f32[16,4,512]{2,1,0:T(4,128)S(1)} all-to-all(f32[16,4,512]{2,1,0:T(4,128)S(1)} %copy.23), channel_id=1, replica_groups={{0,4,8,12,16,20,24,28,2,6,10,14,18,22,26,30},{32,36,40,44,48,52,56,60,3..., dimensions={0} | all-to-all | bytes 262144 | tf_op jit(solution)/shard_map/all_to_all | solution.py:35
  142.6 0.6 reduce_sum.39
  (53 shorter events, 1.0 us)
Async XLA Ops:
  0.0 12.3 %copy-start.2 = (bf16[28,512]{1,0:T(8,128)(2,1)S(1)}, bf16[28,512]{1,0:T(8,128)(2,1)}, u32[]{:S(2)}) copy-start(bf16[28,512]{1,0:T(8,128)(2,1)} %param.9) | copy-start | bytes 86020
  2.4 16.5 %copy-start = (bf16[512,256]{1,0:T(8,128)(2,1)S(1)}, bf16[512,256]{1,0:T(8,128)(2,1)}, u32[]{:S(2)}) copy-start(bf16[512,256]{1,0:T(8,128)(2,1)} %param.11) | copy-start | bytes 786436
  2.4 16.5 %copy-start.1 = (bf16[256,512]{1,0:T(8,128)(2,1)S(1)}, bf16[256,512]{1,0:T(8,128)(2,1)}, u32[]{:S(2)}) copy-start(bf16[256,512]{1,0:T(8,128)(2,1)} %param.10) | copy-start | bytes 786436
  3.5 10.0 %collective-permute-start = (bf16[288,512]{1,0:T(8,128)(2,1)S(1)}, bf16[288,512]{1,0:T(8,128)(2,1)S(1)}, u32[]{:S(2)}, u32[]{:S(2)}) collective-permute-start(bf16[288,512]{1,0:T(8,128)(2,1)S(1)} %maximum_select_fusion), channel_id=1, source_target_pairs={{0,1},{1,0},{2,3},{3,2},{4,5},{5,4},{6,7},{7,6},{8,9},{9,8},{10,11... | collective-permute-start | bytes 884744 | tf_op jit(solution)/shard_map/ppermute | solution.py:75
  13.6 8.9 %collective-permute-start.1 = (bf16[64,512]{1,0:T(8,128)(2,1)S(1)}, bf16[64,512]{1,0:T(8,128)(2,1)S(1)}, u32[]{:S(2)}, u32[]{:S(2)}) collective-permute-start(bf16[64,512]{1,0:T(8,128)(2,1)S(1)} %maximum_select_fusion.1), channel_id=1, source_target_pairs={{0,64},{64,0},{2,66},{66,2},{4,68},{68,4},{6,70},{70,6},{8,72},{72... | collective-permute-start | bytes 196616 | tf_op jit(solution)/shard_map/ppermute | solution.py:82
  60.9 0.7 copy-start.3
  60.9 1.1 copy-start.4
  60.9 1.3 copy-start.5
  62.3 7.7 %collective-permute-start.2 = (bf16[64,896]{1,0:T(8,128)(2,1)S(1)}, bf16[64,896]{1,0:T(8,128)(2,1)S(1)}, u32[]{:S(2)}, u32[]{:S(2)}) collective-permute-start(bf16[64,896]{1,0:T(8,128)(2,1)S(1)} %convert_element_type.44), channel_id=1, source_target_pairs={{0,2},{2,0},{4,6},{6,4},{8,10},{10,8},{12,14},{14,12},{16,18},{18,... | collective-permute-start | bytes 344072 | tf_op jit(solution)/shard_map/ppermute | solution.py:101
  82.3 16.2 %copy-start.6 = (f32[512]{0:T(512)S(1)}, f32[512]{0:T(512)}, u32[]{:S(2)}) copy-start(f32[512]{0:T(512)} %param.12) | copy-start | bytes 6148
  82.3 16.0 %collective-permute-start.3 = (bf16[336,512]{1,0:T(8,128)(2,1)S(1)}, bf16[336,512]{1,0:T(8,128)(2,1)S(1)}, u32[]{:S(2)}, u32[]{:S(2)}) collective-permute-start(bf16[336,512]{1,0:T(8,128)(2,1)S(1)} %fusion.6), channel_id=1, source_target_pairs={{0,1},{1,0},{2,3},{3,2},{4,5},{5,4},{6,7},{7,6},{8,9},{9,8},{10,11... | collective-permute-start | bytes 1032200 | tf_op jit(solution)/shard_map/ppermute | solution.py:118
  96.3 4.4 %collective-permute-start.4 = (bf16[512,896]{1,0:T(8,128)(2,1)S(1)}, bf16[512,896]{1,0:T(8,128)(2,1)S(1)}, u32[]{:S(2)}, u32[]{:S(2)}) collective-permute-start(bf16[512,896]{1,0:T(8,128)(2,1)S(1)} %bitcast.29), channel_id=1, source_target_pairs={{0,1},{1,0},{2,3},{3,2},{4,5},{5,4},{6,7},{7,6},{8,9},{9,8},{10,11... | collective-permute-start | bytes 2752520 | tf_op jit(solution)/shard_map/ppermute | solution.py:117

commit v7 on v6

--- a/solution.py
+++ b/solution.py
@@ -85,37 +85,39 @@
         jnp.concatenate([basis_out, basis_far], axis=0),
         jnp.concatenate([tall(basis_far), basis_in], axis=1),
     )
+    late = lax.optimization_barrier((rows, basis_in, eig_in, pair_order, length_bucket))
+    _, in_late, eig_late, pair_order, length_bucket = late
+    parity = jnp.where(jnp.arange(tokens) % 2 == 0, 1.0, -1.0)
+    token = lax.broadcasted_iota(jnp.int32, (1, tokens), 1)
+    sign = jnp.sum(jnp.where(pair_order[:, None] == token, parity[:, None], 0.0), axis=0)
+    weights = sign / jnp.sqrt((1.0 + length_bucket.astype(F32)) * tokens)
+    weights = jnp.where(first, weights, 1.0)
+    eig3 = jnp.concatenate([*three(eig_late), jnp.zeros((half,), BF)]).reshape(2, 2 * half)
+    later = jnp.concatenate([wide(in_late), jnp.pad(eig3, ((0, 14), (0, 0)))], axis=0)
     low = jnp.where(first, zl // 2, zh) == 0
     rows = jnp.stack([jnp.where(low, rows, rows_far), jnp.where(low, rows_far, rows)])
-    parity = jnp.where(jnp.arange(tokens) % 2 == 0, 1.0, -1.0)
-    rows, basis, parity = lax.optimization_barrier((rows, basis, parity))
+    rows, basis, weights, later = lax.optimization_barrier((rows, basis, weights, later))
     rows = exchange(copies(rows, 8), EIGHT_IN)
     ordered = rows[:, :, :block].reshape(tokens, -1)
     paired = rows.reshape(4, 2, 2, 64, -1).swapaxes(1, 2)[:, :, :, :block].reshape(tokens, -1)
     part = dot(basis, jnp.where(first, paired, ordered), ((0,), (1,))).astype(BF)
     part = exchange(part.reshape(8, -1, tokens), EIGHT_MID)
+    part, rows = lax.optimization_barrier((part, rows))
     total = jnp.sum(part.astype(F32), axis=0)
 
-    sent, *late = lax.optimization_barrier((total.astype(BF), pair_order, length_bucket))
-    pair_order, length_bucket = late
-    total_far = lax.ppermute(sent, AXES, PAIR_MID)
-    token = lax.broadcasted_iota(jnp.int32, (1, tokens), 1)
-    sign = jnp.sum(jnp.where(pair_order[:, None] == token, parity[:, None], 0.0), axis=0)
-    weights = sign / jnp.sqrt((1.0 + length_bucket.astype(F32)) * tokens)
-    weights = jnp.where(first, weights, 1.0)
-    weights, rows, in_late, eig_late = lax.optimization_barrier((weights, rows, basis_in, eig_in))
+    total_far = lax.ppermute(total.astype(BF), AXES, PAIR_MID)
     slab0, slab1 = (
         rows[:, :, block + k * extra : block + (k + 1) * extra].swapaxes(0, 1).reshape(n * extra, -1)
         for k in range(2)
     )
-    eig3 = jnp.concatenate([*three(eig_late), jnp.zeros((half,), BF)]).reshape(2, 2 * half)
-    packed = jnp.concatenate([slab0, wide(in_late), jnp.pad(eig3, ((0, 14), (0, 0)))], axis=0)
+    packed = jnp.concatenate([slab0, later], axis=0)
     rot = ((total + total_far.astype(F32)) * weights).astype(BF)
     rot, packed, slab1 = lax.optimization_barrier((rot, packed, slab1))
     rot = exchange(copies(rot, 8), EIGHT_MID).reshape(-1, tokens)
     rot, packed = lax.optimization_barrier((rot, packed))
     rot_far = lax.ppermute(rot, "core", SWAP)
     far = lax.ppermute(packed, "core", SWAP)
+    rot_far, far = lax.optimization_barrier((rot_far, far))
     slab = jnp.where(first, far[: slab1.shape[0]], slab1)
     eig_far = far[-16:-14].astype(F32).reshape(4, half)
     eig_far = eig_far[0] + eig_far[1] + eig_far[2]

time: 146 us -> 144 us (0.986)
    ppermute x1, starting transfers between devices: 14 us -> 1.92 us  [shards(): far = lax.ppermute(packed, 'core', SWAP)]
    ppermute x1, starting transfers between devices: 1.92 us -> 13.9 us  [shards(): rot_far = lax.ppermute(rot, 'core', SWAP)]
    ppermute x1, waiting for transfers between devices: 2.2 us -> 0.01 us  [shards(): rot_far = lax.ppermute(rot, 'core', SWAP)]
    ppermute x1, waiting for transfers between devices: 0.01 us -> 1.62 us  [shards(): far = lax.ppermute(packed, 'core', SWAP)]
  transfers between devices with their start and end apart: 5 -> 5, of which waited for: 4 -> 4; matrix products, arithmetic and copies ran while one was open for 0% -> 1% of each run, Pallas kernels for 0% -> 0%
where the time goes in v7:
time: 144 us; the launch traced here: 141 us
  blocking collectives  89.4 us (62%)
  starting transfers between devices  33.8 us (23%)
  waiting for transfers between devices  9.07 us (6%)
  local copies, waits for them, and re-layouts  3.35 us (2%)
  other arithmetic  2.95 us (2%)
  matrix products  2.25 us (2%)
    all_to_all x4, blocking collectives, exchange(): lax.all_to_all(parts, AXES, 0, 0, axis_index_groups=groups, tiled=True)  67 us
    ppermute x1, starting transfers between devices, shards(): rot_far = lax.ppermute(rot, 'core', SWAP)  13.9 us
    all_to_all x1, blocking collectives, shards(): lax.all_to_all(left.reshape(n, -1, left.shape[1]), ('x', 'zl'), 0, 0, til...  11.7 us
    all_to_all x1, blocking collectives, shards(): left = lax.all_to_all(copies(left, n), ('x', 'zl'), 0, 0, tiled=True)  10.7 us
    ppermute x1, starting transfers between devices, shards(): far = lax.ppermute(far, 'core', SWAP)  8.79 us
    ppermute x1, starting transfers between devices, shards(): rows_far = lax.ppermute(rows, AXES, PAIR_IN)  5.26 us
    ppermute x1, starting transfers between devices, shards(): total_far = lax.ppermute(total.astype(BF), AXES, PAIR_MID)  3.93 us
    ppermute x1, waiting for transfers between devices, shards(): total_far = lax.ppermute(total.astype(BF), AXES, PAIR_MID)  3.52 us
  transfers between devices with their start and end apart: 5, of which 4 were waited for; matrix products, arithmetic and copies ran while one was open for 1% of the time, Pallas kernels for 0%

profile of v7, /device:TPU:1, one launch (start us, length us, event | category | flops | bytes accessed | tf_op | source)
XLA Modules:
  0.0 141.3 jit_solution(9516492921557256774)
XLA Ops:
  0.0 0.7 slice.100
  0.7 0.8 fusion.22
  1.5 1.0 fusion.20
  2.5 1.1 maximum_select_fusion
  3.6 8.8 %collective-permute-start = (bf16[288,512]{1,0:T(8,128)(2,1)S(1)}, bf16[288,512]{1,0:T(8,128)(2,1)S(1)}, u32[]{:S(2)}, u32[]{:S(2)}) collective-permute-start(bf16[288,512]{1,0:T(8,128)(2,1)S(1)} %maximum_select_fusion), channel_id=1, source_target_pairs={{0,1},{1,0},{2,3},{3,2},{4,5},{5,4},{6,7},{7,6},{8,9},{9,8},{10,11... | collective-permute-start | bytes 884744 | tf_op jit(solution)/shard_map/ppermute | solution.py:75
  12.5 1.1 collective-permute-done
  13.6 5.3 %collective-permute-start.1 = (bf16[64,512]{1,0:T(8,128)(2,1)S(1)}, bf16[64,512]{1,0:T(8,128)(2,1)S(1)}, u32[]{:S(2)}, u32[]{:S(2)}) collective-permute-start(bf16[64,512]{1,0:T(8,128)(2,1)S(1)} %maximum_select_fusion.1), channel_id=1, source_target_pairs={{0,64},{64,0},{2,66},{66,2},{4,68},{68,4},{6,70},{70,6},{8,72},{72... | collective-permute-start | bytes 196616 | tf_op jit(solution)/shard_map/ppermute | solution.py:82
  19.0 0.4 select_reduce_fusion
  19.5 0.1 fusion.2
  19.7 2.9 %collective-permute-done.1 = bf16[64,512]{1,0:T(8,128)(2,1)S(1)} collective-permute-done((bf16[64,512]{1,0:T(8,128)(2,1)S(1)}, bf16[64,512]{1,0:T(8,128)(2,1)S(1)}, u32[]{:S(2)}, u32[]{:S(2)}) %collective-permute-start.1) | collective-permute-done | bytes 65568 | tf_op jit(solution)/shard_map/ppermute | solution.py:82
  22.6 0.1 broadcast_in_dim.53
  22.7 22.4 %all_to_all.30 = bf16[8,2,64,512]{3,2,1,0:T(8,128)(2,1)S(1)} all-to-all(bf16[8,2,64,512]{3,2,1,0:T(8,128)(2,1)S(1)} %broadcast_in_dim.53), channel_id=1, replica_groups={{0,32,128,160,256,288,384,416},{2,34,130,162,258,290,386,418},{4,36,132..., dimensions={0} | all-to-all | bytes 2097152 | tf_op jit(solution)/shard_map/all_to_all | solution.py:35
  45.4 0.2 bitcast_select_fusion
  45.6 0.8 convolution_convert_fusion
  46.3 14.6 %all_to_all.31 = bf16[8,64,896]{2,1,0:T(8,128)(2,1)S(1)} all-to-all(bf16[8,64,896]{2,1,0:T(8,128)(2,1)S(1)} %bitcast.31), channel_id=1, replica_groups={{0,4,8,12,16,20,24,28},{2,6,10,14,18,22,26,30},{32,36,40,44,48,52,56,60..., dimensions={0} | all-to-all | bytes 1835008 | tf_op jit(solution)/shard_map/all_to_all | solution.py:35
  60.9 0.1 convert_reduce_fusion
  61.0 3.9 %collective-permute-start.2 = (bf16[64,896]{1,0:T(8,128)(2,1)S(1)}, bf16[64,896]{1,0:T(8,128)(2,1)S(1)}, u32[]{:S(2)}, u32[]{:S(2)}) collective-permute-start(bf16[64,896]{1,0:T(8,128)(2,1)S(1)} %convert_element_type.48), channel_id=1, source_target_pairs={{0,2},{2,0},{4,6},{6,4},{8,10},{10,8},{12,14},{14,12},{16,18},{18,... | collective-permute-start | bytes 344072 | tf_op jit(solution)/shard_map/ppermute | solution.py:108
  65.2 3.5 %collective-permute-done.2 = bf16[64,896]{1,0:T(8,128)(2,1)S(1)} collective-permute-done((bf16[64,896]{1,0:T(8,128)(2,1)S(1)}, bf16[64,896]{1,0:T(8,128)(2,1)S(1)}, u32[]{:S(2)}, u32[]{:S(2)}) %collective-permute-start.2) | collective-permute-done | bytes 114720 | tf_op jit(solution)/shard_map/ppermute | solution.py:108
  68.7 0.1 broadcast_in_dim.54
  68.9 12.2 %all_to_all.32 = bf16[8,64,896]{2,1,0:T(8,128)(2,1)S(1)} all-to-all(bf16[8,64,896]{2,1,0:T(8,128)(2,1)S(1)} %broadcast_in_dim.54), channel_id=1, replica_groups={{0,4,8,12,16,20,24,28},{2,6,10,14,18,22,26,30},{32,36,40,44,48,52,56,60..., dimensions={0} | all-to-all | bytes 1835008 | tf_op jit(solution)/shard_map/all_to_all | solution.py:35
  81.0 13.9 %collective-permute-start.3 = (bf16[512,896]{1,0:T(8,128)(2,1)S(1)}, bf16[512,896]{1,0:T(8,128)(2,1)S(1)}, u32[]{:S(2)}, u32[]{:S(2)}) collective-permute-start(bf16[512,896]{1,0:T(8,128)(2,1)S(1)} %bitcast.29), channel_id=1, source_target_pairs={{0,1},{1,0},{2,3},{3,2},{4,5},{5,4},{6,7},{7,6},{8,9},{9,8},{10,11... | collective-permute-start | bytes 2752520 | tf_op jit(solution)/shard_map/ppermute | solution.py:118
  95.0 1.9 %collective-permute-start.4 = (bf16[336,512]{1,0:T(8,128)(2,1)S(1)}, bf16[336,512]{1,0:T(8,128)(2,1)S(1)}, u32[]{:S(2)}, u32[]{:S(2)}) collective-permute-start(bf16[336,512]{1,0:T(8,128)(2,1)S(1)} %pad_maximum_fusion.2), channel_id=1, source_target_pairs={{0,1},{1,0},{2,3},{3,2},{4,5},{5,4},{6,7},{7,6},{8,9},{9,8},{10,11... | collective-permute-start | bytes 1032200 | tf_op jit(solution)/shard_map/ppermute | solution.py:119
  96.9 1.6 %collective-permute-done.4 = bf16[336,512]{1,0:T(8,128)(2,1)S(1)} collective-permute-done((bf16[336,512]{1,0:T(8,128)(2,1)S(1)}, bf16[336,512]{1,0:T(8,128)(2,1)S(1)}, u32[]{:S(2)}, u32[]{:S(2)}) %collective-permute-start.4) | collective-permute-done | bytes 344096 | tf_op jit(solution)/shard_map/ppermute | solution.py:119
  98.6 0.7 fusion
  99.3 0.2 fusion.8
  99.5 0.3 convolution_select_fusion
  99.8 0.1 fusion.3
  100.0 11.7 %all_to_all.33 = f32[16,4,512]{2,1,0:T(4,128)S(1)} all-to-all(f32[16,4,512]{2,1,0:T(4,128)S(1)} %reshape.69), channel_id=1, replica_groups=mesh['x'=4,'zl'=4,'y'=8,'zh'=2,'core'=2] {'x','zl'}, dimensions={0} | all-to-all | bytes 262144 | tf_op jit(solution)/shard_map/all_to_all | solution.py:136
  111.7 10.7 %all_to_all.34 = bf16[16,4,512]{2,1,0:T(4,128)(2,1)S(1)} all-to-all(bf16[16,4,512]{2,1,0:T(4,128)(2,1)S(1)} %broadcast_in_dim.55), channel_id=1, replica_groups=mesh['x'=4,'zl'=4,'y'=8,'zh'=2,'core'=2] {'x','zl'}, dimensions={0} | all-to-all | bytes 131072 | tf_op jit(solution)/shard_map/all_to_all | solution.py:138
  122.4 0.3 fusion.4
  122.8 17.8 %all_to_all.35 = f32[16,4,512]{2,1,0:T(4,128)S(1)} all-to-all(f32[16,4,512]{2,1,0:T(4,128)S(1)} %copy.23), channel_id=1, replica_groups={{0,4,8,12,16,20,24,28,2,6,10,14,18,22,26,30},{32,36,40,44,48,52,56,60,3..., dimensions={0} | all-to-all | bytes 262144 | tf_op jit(solution)/shard_map/all_to_all | solution.py:35
  140.6 0.6 reduce_sum.39
  (54 shorter events, 1.0 us)
Async XLA Ops:
  0.0 12.4 %copy-start.2 = (bf16[28,512]{1,0:T(8,128)(2,1)S(1)}, bf16[28,512]{1,0:T(8,128)(2,1)}, u32[]{:S(2)}) copy-start(bf16[28,512]{1,0:T(8,128)(2,1)} %param.9) | copy-start | bytes 86020
  0.0 18.9 %copy-start.5 = (f32[256]{0:T(256)S(1)}, f32[256]{0:T(256)}, u32[]{:S(2)}) copy-start(f32[256]{0:T(256)} %param.13) | copy-start | bytes 3076
  0.7 18.2 %copy-start = (bf16[512,256]{1,0:T(8,128)(2,1)S(1)}, bf16[512,256]{1,0:T(8,128)(2,1)}, u32[]{:S(2)}) copy-start(bf16[512,256]{1,0:T(8,128)(2,1)} %param.11) | copy-start | bytes 786436
  2.5 16.5 %copy-start.3 = (s32[896]{0:T(1024)S(1)}, s32[896]{0:T(1024)}, u32[]{:S(2)}) copy-start(s32[896]{0:T(1024)} %param.14) | copy-start | bytes 10756
  2.5 16.9 %copy-start.4 = (s32[896]{0:T(1024)S(1)}, s32[896]{0:T(1024)}, u32[]{:S(2)}) copy-start(s32[896]{0:T(1024)} %param.15) | copy-start | bytes 10756
  3.6 10.0 %collective-permute-start = (bf16[288,512]{1,0:T(8,128)(2,1)S(1)}, bf16[288,512]{1,0:T(8,128)(2,1)S(1)}, u32[]{:S(2)}, u32[]{:S(2)}) collective-permute-start(bf16[288,512]{1,0:T(8,128)(2,1)S(1)} %maximum_select_fusion), channel_id=1, source_target_pairs={{0,1},{1,0},{2,3},{3,2},{4,5},{5,4},{6,7},{7,6},{8,9},{9,8},{10,11... | collective-permute-start | bytes 884744 | tf_op jit(solution)/shard_map/ppermute | solution.py:75
  12.4 7.1 %copy-start.1 = (bf16[256,512]{1,0:T(8,128)(2,1)S(1)}, bf16[256,512]{1,0:T(8,128)(2,1)}, u32[]{:S(2)}) copy-start(bf16[256,512]{1,0:T(8,128)(2,1)} %param.10) | copy-start | bytes 786436
  13.6 8.9 %collective-permute-start.1 = (bf16[64,512]{1,0:T(8,128)(2,1)S(1)}, bf16[64,512]{1,0:T(8,128)(2,1)S(1)}, u32[]{:S(2)}, u32[]{:S(2)}) collective-permute-start(bf16[64,512]{1,0:T(8,128)(2,1)S(1)} %maximum_select_fusion.1), channel_id=1, source_target_pairs={{0,64},{64,0},{2,66},{66,2},{4,68},{68,4},{6,70},{70,6},{8,72},{72... | collective-permute-start | bytes 196616 | tf_op jit(solution)/shard_map/ppermute | solution.py:82
  61.0 7.7 %collective-permute-start.2 = (bf16[64,896]{1,0:T(8,128)(2,1)S(1)}, bf16[64,896]{1,0:T(8,128)(2,1)S(1)}, u32[]{:S(2)}, u32[]{:S(2)}) collective-permute-start(bf16[64,896]{1,0:T(8,128)(2,1)S(1)} %convert_element_type.48), channel_id=1, source_target_pairs={{0,2},{2,0},{4,6},{6,4},{8,10},{10,8},{12,14},{14,12},{16,18},{18,... | collective-permute-start | bytes 344072 | tf_op jit(solution)/shard_map/ppermute | solution.py:108
  68.9 29.7 %copy-start.6 = (f32[512]{0:T(512)S(1)}, f32[512]{0:T(512)}, u32[]{:S(2)}) copy-start(f32[512]{0:T(512)} %param.12) | copy-start | bytes 6148
  81.0 17.5 %collective-permute-start.3 = (bf16[512,896]{1,0:T(8,128)(2,1)S(1)}, bf16[512,896]{1,0:T(8,128)(2,1)S(1)}, u32[]{:S(2)}, u32[]{:S(2)}) collective-permute-start(bf16[512,896]{1,0:T(8,128)(2,1)S(1)} %bitcast.29), channel_id=1, source_target_pairs={{0,1},{1,0},{2,3},{3,2},{4,5},{5,4},{6,7},{7,6},{8,9},{9,8},{10,11... | collective-permute-start | bytes 2752520 | tf_op jit(solution)/shard_map/ppermute | solution.py:118
  95.0 3.5 %collective-permute-start.4 = (bf16[336,512]{1,0:T(8,128)(2,1)S(1)}, bf16[336,512]{1,0:T(8,128)(2,1)S(1)}, u32[]{:S(2)}, u32[]{:S(2)}) collective-permute-start(bf16[336,512]{1,0:T(8,128)(2,1)S(1)} %pad_maximum_fusion.2), channel_id=1, source_target_pairs={{0,1},{1,0},{2,3},{3,2},{4,5},{5,4},{6,7},{7,6},{8,9},{9,8},{10,11... | collective-permute-start | bytes 1032200 | tf_op jit(solution)/shard_map/ppermute | solution.py:119

commit v8 on v7

--- a/solution.py
+++ b/solution.py
@@ -23,8 +23,8 @@
 COL_ALL = lists((5, 0, 1, 2, 4, 3), 16)
 EIGHT_IN = ROW_EIGHT[0] + COL_EIGHT[1]
 EIGHT_MID = COL_EIGHT[0] + ROW_EIGHT[1]
-PAIR_IN = [(g[i], g[1 - i]) for g in ROW_PAIR[0] + COL_PAIR[1] for i in range(2)]
-PAIR_MID = [(g[i], g[1 - i]) for g in COL_PAIR[0] + ROW_PAIR[1] for i in range(2)]
+PAIR_IN = ROW_PAIR[0] + COL_PAIR[1]
+PAIR_MID = COL_PAIR[0] + ROW_PAIR[1]
 
 
 def dot(a, b, contract):
@@ -33,6 +33,10 @@
 
 def exchange(parts, groups):
     return lax.all_to_all(parts, AXES, 0, 0, axis_index_groups=groups, tiled=True)
+
+
+def both(block, groups):
+    return lax.all_gather(block, AXES, axis_index_groups=groups)
 
 
 def copies(block, n):
@@ -79,24 +83,22 @@
     as_acts = jnp.concatenate([far[:share], kept[:share], far[share:], kept[share:]], axis=0)
     rows = jnp.where(first, as_grads, as_acts)
 
-    rows_far = lax.ppermute(rows, AXES, PAIR_IN)
+    rows = both(rows, PAIR_IN)
     basis = jnp.where(
         first,
         jnp.concatenate([basis_out, basis_far], axis=0),
         jnp.concatenate([tall(basis_far), basis_in], axis=1),
     )
-    late = lax.optimization_barrier((rows, basis_in, eig_in, pair_order, length_bucket))
-    _, in_late, eig_late, pair_order, length_bucket = late
+
     parity = jnp.where(jnp.arange(tokens) % 2 == 0, 1.0, -1.0)
     token = lax.broadcasted_iota(jnp.int32, (1, tokens), 1)
     sign = jnp.sum(jnp.where(pair_order[:, None] == token, parity[:, None], 0.0), axis=0)
     weights = sign / jnp.sqrt((1.0 + length_bucket.astype(F32)) * tokens)
     weights = jnp.where(first, weights, 1.0)
-    eig3 = jnp.concatenate([*three(eig_late), jnp.zeros((half,), BF)]).reshape(2, 2 * half)
-    later = jnp.concatenate([wide(in_late), jnp.pad(eig3, ((0, 14), (0, 0)))], axis=0)
-    low = jnp.where(first, zl // 2, zh) == 0
-    rows = jnp.stack([jnp.where(low, rows, rows_far), jnp.where(low, rows_far, rows)])
-    rows, basis, weights, later = lax.optimization_barrier((rows, basis, weights, later))
+    eig3 = jnp.concatenate([*three(eig_in), jnp.zeros((half,), BF)]).reshape(2, 2 * half)
+    later = jnp.concatenate([wide(basis_in), jnp.pad(eig3, ((0, 14), (0, 0)))], axis=0)
+    low = jnp.where(first, zh, zl // 2) == 0
+    rows, basis, weights, later, low = lax.optimization_barrier((rows, basis, weights, later, low))
     rows = exchange(copies(rows, 8), EIGHT_IN)
     ordered = rows[:, :, :block].reshape(tokens, -1)
     paired = rows.reshape(4, 2, 2, 64, -1).swapaxes(1, 2)[:, :, :, :block].reshape(tokens, -1)
@@ -105,7 +107,8 @@
     part, rows = lax.optimization_barrier((part, rows))
     total = jnp.sum(part.astype(F32), axis=0)
 
-    total_far = lax.ppermute(total.astype(BF), AXES, PAIR_MID)
+    totals = both(total.astype(BF), PAIR_MID)
+    total_far = jnp.where(low, totals[1], totals[0])
     slab0, slab1 = (
         rows[:, :, block + k * extra : block + (k + 1) * extra].swapaxes(0, 1).reshape(n * extra, -1)
         for k in range(2)

time: 144 us -> 142 us (0.986)
  blocking collectives: 89.4 us -> 103 us
  starting transfers between devices: 33.8 us -> 24.5 us
  waiting for transfers between devices: 9.07 us -> 2.1 us
    all_gather x0 -> x2, blocking collectives: none -> 14.1 us  [both(): return lax.all_gather(block, AXES, axis_index_groups=groups)]
    ppermute x2 -> x0, starting transfers between devices: 9.19 us -> none  [the longest x1 5.26 us: shards(): rows_far = lax.ppermute(rows, AXES, PAIR_IN)]
    ppermute x2 -> x0, waiting for transfers between devices: 6.38 us -> none  [the longest x1 3.52 us: shards(): total_far = lax.ppermute(total.astype(BF), AXES, PAIR_MID)]
  transfers between devices with their start and end apart: 5 -> 3, of which waited for: 4 -> 2; matrix products, arithmetic and copies ran while one was open for 1% -> 0% of each run, Pallas kernels for 0% -> 0%
where the time goes in v8:
time: 142 us; the launch traced here: 139 us
  blocking collectives  103 us (73%)
  starting transfers between devices  24.5 us (17%)
  local copies, waits for them, and re-layouts  3.32 us (2%)
  other arithmetic  2.96 us (2%)
  matrix products  2.25 us (2%)
  waiting for transfers between devices  2.1 us (1%)
    all_to_all x4, blocking collectives, exchange(): lax.all_to_all(parts, AXES, 0, 0, axis_index_groups=groups, tiled=True)  66.8 us
    all_gather x2, blocking collectives, both(): return lax.all_gather(block, AXES, axis_index_groups=groups)  14.1 us
    ppermute x1, starting transfers between devices, shards(): rot_far = lax.ppermute(rot, 'core', SWAP)  13.8 us
    all_to_all x1, blocking collectives, shards(): lax.all_to_all(left.reshape(n, -1, left.shape[1]), ('x', 'zl'), 0, 0, til...  11.8 us
    all_to_all x1, blocking collectives, shards(): left = lax.all_to_all(copies(left, n), ('x', 'zl'), 0, 0, tiled=True)  10.7 us
    ppermute x1, starting transfers between devices, shards(): far = lax.ppermute(far, 'core', SWAP)  8.79 us
  transfers between devices with their start and end apart: 3, of which 2 were waited for; matrix products, arithmetic and copies ran while one was open for 0% of the time, Pallas kernels for 0%

profile of v8, /device:TPU:1, one launch (start us, length us, event | category | flops | bytes accessed | tf_op | source)
XLA Modules:
  0.0 139.0 jit_solution(10285589824236807118)
XLA Ops:
  0.0 0.7 slice.102
  0.7 0.7 fusion.23
  1.4 1.0 fusion.21
  2.5 1.1 maximum_select_fusion
  3.5 8.8 %collective-permute-start = (bf16[288,512]{1,0:T(8,128)(2,1)S(1)}, bf16[288,512]{1,0:T(8,128)(2,1)S(1)}, u32[]{:S(2)}, u32[]{:S(2)}) collective-permute-start(bf16[288,512]{1,0:T(8,128)(2,1)S(1)} %maximum_select_fusion), channel_id=1, source_target_pairs={{0,1},{1,0},{2,3},{3,2},{4,5},{5,4},{6,7},{7,6},{8,9},{9,8},{10,11... | collective-permute-start | bytes 884744 | tf_op jit(solution)/shard_map/ppermute | solution.py:79
  12.5 0.4 select_reduce_fusion
  13.0 0.5 collective-permute-done
  13.6 7.7 %all_gather.8 = bf16[2,64,512]{2,1,0:T(8,128)(2,1)S(1)} all-gather(bf16[1,64,512]{2,1,0:T(8,128)(2,1)S(1)} %maximum_select_fusion.1), channel_id=1, replica_groups={{0,64},{2,66},{4,68},{6,70},{8,72},{10,74},{12,76},{14,78},{16,80},{18,..., dimensions={0}, use_global_device_ids=true | all-gather | bytes 196608 | tf_op jit(solution)/shard_map/all_gather | solution.py:39
  21.3 0.1 fusion.2
  21.5 0.1 broadcast_in_dim.53
  21.6 22.4 %all_to_all.30 = bf16[8,2,64,512]{3,2,1,0:T(8,128)(2,1)S(1)} all-to-all(bf16[8,2,64,512]{3,2,1,0:T(8,128)(2,1)S(1)} %broadcast_in_dim.53), channel_id=1, replica_groups={{0,32,128,160,256,288,384,416},{2,34,130,162,258,290,386,418},{4,36,132..., dimensions={0} | all-to-all | bytes 2097152 | tf_op jit(solution)/shard_map/all_to_all | solution.py:35
  44.1 0.1 slice.143
  44.2 0.2 bitcast_select_fusion
  44.5 0.8 convolution_convert_fusion
  45.2 14.6 %all_to_all.31 = bf16[8,64,896]{2,1,0:T(8,128)(2,1)S(1)} all-to-all(bf16[8,64,896]{2,1,0:T(8,128)(2,1)S(1)} %bitcast.38), channel_id=1, replica_groups={{0,4,8,12,16,20,24,28},{2,6,10,14,18,22,26,30},{32,36,40,44,48,52,56,60..., dimensions={0} | all-to-all | bytes 1835008 | tf_op jit(solution)/shard_map/all_to_all | solution.py:35
  59.8 0.1 convert_reduce_fusion
  59.9 6.4 %all-gather = bf16[128,896]{1,0:T(8,128)(2,1)S(1)} all-gather(bf16[64,896]{1,0:T(8,128)(2,1)S(1)} %convert_element_type.61), channel_id=2, replica_groups={{0,2},{4,6},{8,10},{12,14},{16,18},{20,22},{24,26},{28,30},{32,34},{36,..., dimensions={0}, use_global_device_ids=true | all-gather | bytes 344064 | tf_op jit(solution)/shard_map/all_gather | solution.py:39
  66.6 0.1 broadcast_in_dim.54
  66.8 12.2 %all_to_all.32 = bf16[8,64,896]{2,1,0:T(8,128)(2,1)S(1)} all-to-all(bf16[8,64,896]{2,1,0:T(8,128)(2,1)S(1)} %broadcast_in_dim.54), channel_id=1, replica_groups={{0,4,8,12,16,20,24,28},{2,6,10,14,18,22,26,30},{32,36,40,44,48,52,56,60..., dimensions={0} | all-to-all | bytes 1835008 | tf_op jit(solution)/shard_map/all_to_all | solution.py:35
  78.9 13.8 %collective-permute-start.1 = (bf16[512,896]{1,0:T(8,128)(2,1)S(1)}, bf16[512,896]{1,0:T(8,128)(2,1)S(1)}, u32[]{:S(2)}, u32[]{:S(2)}) collective-permute-start(bf16[512,896]{1,0:T(8,128)(2,1)S(1)} %bitcast.36), channel_id=1, source_target_pairs={{0,1},{1,0},{2,3},{3,2},{4,5},{5,4},{6,7},{7,6},{8,9},{9,8},{10,11... | collective-permute-start | bytes 2752520 | tf_op jit(solution)/shard_map/ppermute | solution.py:121
  92.7 1.9 %collective-permute-start.2 = (bf16[336,512]{1,0:T(8,128)(2,1)S(1)}, bf16[336,512]{1,0:T(8,128)(2,1)S(1)}, u32[]{:S(2)}, u32[]{:S(2)}) collective-permute-start(bf16[336,512]{1,0:T(8,128)(2,1)S(1)} %pad_maximum_fusion.2), channel_id=1, source_target_pairs={{0,1},{1,0},{2,3},{3,2},{4,5},{5,4},{6,7},{7,6},{8,9},{9,8},{10,11... | collective-permute-start | bytes 1032200 | tf_op jit(solution)/shard_map/ppermute | solution.py:122
  94.6 1.6 %collective-permute-done.2 = bf16[336,512]{1,0:T(8,128)(2,1)S(1)} collective-permute-done((bf16[336,512]{1,0:T(8,128)(2,1)S(1)}, bf16[336,512]{1,0:T(8,128)(2,1)S(1)}, u32[]{:S(2)}, u32[]{:S(2)}) %collective-permute-start.2) | collective-permute-done | bytes 344096 | tf_op jit(solution)/shard_map/ppermute | solution.py:122
  96.4 0.7 fusion
  97.1 0.2 fusion.10
  97.3 0.3 convolution_select_fusion
  97.6 0.1 fusion.3
  97.8 11.8 %all_to_all.33 = f32[16,4,512]{2,1,0:T(4,128)S(1)} all-to-all(f32[16,4,512]{2,1,0:T(4,128)S(1)} %reshape.162), channel_id=1, replica_groups=mesh['x'=4,'zl'=4,'y'=8,'zh'=2,'core'=2] {'x','zl'}, dimensions={0} | all-to-all | bytes 262144 | tf_op jit(solution)/shard_map/all_to_all | solution.py:139
  109.6 10.7 %all_to_all.34 = bf16[16,4,512]{2,1,0:T(4,128)(2,1)S(1)} all-to-all(bf16[16,4,512]{2,1,0:T(4,128)(2,1)S(1)} %broadcast_in_dim.55), channel_id=1, replica_groups=mesh['x'=4,'zl'=4,'y'=8,'zh'=2,'core'=2] {'x','zl'}, dimensions={0} | all-to-all | bytes 131072 | tf_op jit(solution)/shard_map/all_to_all | solution.py:141
  120.3 0.3 fusion.4
  120.6 0.1 copy.23
  120.7 17.7 %all_to_all.35 = f32[16,4,512]{2,1,0:T(4,128)S(1)} all-to-all(f32[16,4,512]{2,1,0:T(4,128)S(1)} %copy.23), channel_id=1, replica_groups={{0,4,8,12,16,20,24,28,2,6,10,14,18,22,26,30},{32,36,40,44,48,52,56,60,3..., dimensions={0} | all-to-all | bytes 262144 | tf_op jit(solution)/shard_map/all_to_all | solution.py:35
  138.4 0.6 reduce_sum.39
  (52 shorter events, 0.8 us)
Async XLA Ops:
  0.0 12.3 %copy-start.2 = (bf16[28,512]{1,0:T(8,128)(2,1)S(1)}, bf16[28,512]{1,0:T(8,128)(2,1)}, u32[]{:S(2)}) copy-start(bf16[28,512]{1,0:T(8,128)(2,1)} %param.9) | copy-start | bytes 86020
  0.0 12.4 %copy-start.5 = (f32[256]{0:T(256)S(1)}, f32[256]{0:T(256)}, u32[]{:S(2)}) copy-start(f32[256]{0:T(256)} %param.13) | copy-start | bytes 3076
  1.4 11.1 %copy-start.3 = (s32[896]{0:T(1024)S(1)}, s32[896]{0:T(1024)}, u32[]{:S(2)}) copy-start(s32[896]{0:T(1024)} %param.14) | copy-start | bytes 10756
  1.4 11.5 %copy-start.4 = (s32[896]{0:T(1024)S(1)}, s32[896]{0:T(1024)}, u32[]{:S(2)}) copy-start(s32[896]{0:T(1024)} %param.15) | copy-start | bytes 10756
  3.5 10.0 %collective-permute-start = (bf16[288,512]{1,0:T(8,128)(2,1)S(1)}, bf16[288,512]{1,0:T(8,128)(2,1)S(1)}, u32[]{:S(2)}, u32[]{:S(2)}) collective-permute-start(bf16[288,512]{1,0:T(8,128)(2,1)S(1)} %maximum_select_fusion), channel_id=1, source_target_pairs={{0,1},{1,0},{2,3},{3,2},{4,5},{5,4},{6,7},{7,6},{8,9},{9,8},{10,11... | collective-permute-start | bytes 884744 | tf_op jit(solution)/shard_map/ppermute | solution.py:79
  12.5 8.8 %copy-start = (bf16[512,256]{1,0:T(8,128)(2,1)S(1)}, bf16[512,256]{1,0:T(8,128)(2,1)}, u32[]{:S(2)}) copy-start(bf16[512,256]{1,0:T(8,128)(2,1)} %param.11) | copy-start | bytes 786436
  12.5 8.8 %copy-start.1 = (bf16[256,512]{1,0:T(8,128)(2,1)S(1)}, bf16[256,512]{1,0:T(8,128)(2,1)}, u32[]{:S(2)}) copy-start(bf16[256,512]{1,0:T(8,128)(2,1)} %param.10) | copy-start | bytes 786436
  66.7 29.6 %copy-start.6 = (f32[512]{0:T(512)S(1)}, f32[512]{0:T(512)}, u32[]{:S(2)}) copy-start(f32[512]{0:T(512)} %param.12) | copy-start | bytes 6148
  78.9 17.4 %collective-permute-start.1 = (bf16[512,896]{1,0:T(8,128)(2,1)S(1)}, bf16[512,896]{1,0:T(8,128)(2,1)S(1)}, u32[]{:S(2)}, u32[]{:S(2)}) collective-permute-start(bf16[512,896]{1,0:T(8,128)(2,1)S(1)} %bitcast.36), channel_id=1, source_target_pairs={{0,1},{1,0},{2,3},{3,2},{4,5},{5,4},{6,7},{7,6},{8,9},{9,8},{10,11... | collective-permute-start | bytes 2752520 | tf_op jit(solution)/shard_map/ppermute | solution.py:121
  92.7 3.5 %collective-permute-start.2 = (bf16[336,512]{1,0:T(8,128)(2,1)S(1)}, bf16[336,512]{1,0:T(8,128)(2,1)S(1)}, u32[]{:S(2)}, u32[]{:S(2)}) collective-permute-start(bf16[336,512]{1,0:T(8,128)(2,1)S(1)} %pad_maximum_fusion.2), channel_id=1, source_target_pairs={{0,1},{1,0},{2,3},{3,2},{4,5},{5,4},{6,7},{7,6},{8,9},{9,8},{10,11... | collective-permute-start | bytes 1032200 | tf_op jit(solution)/shard_map/ppermute | solution.py:122

commit v9 on v8

--- a/solution.py
+++ b/solution.py
@@ -21,10 +21,10 @@
 ROW_PAIR, ROW_EIGHT = lists((5, 0, 2, 3, 4, 1), 2), lists((5, 1, 3, 4, 0, 2), 8)
 COL_PAIR, COL_EIGHT = lists((5, 0, 1, 2, 3, 4), 2), lists((5, 0, 1, 2, 4, 3), 8)
 COL_ALL = lists((5, 0, 1, 2, 4, 3), 16)
-EIGHT_IN = ROW_EIGHT[0] + COL_EIGHT[1]
-EIGHT_MID = COL_EIGHT[0] + ROW_EIGHT[1]
-PAIR_IN = ROW_PAIR[0] + COL_PAIR[1]
-PAIR_MID = COL_PAIR[0] + ROW_PAIR[1]
+EIGHT_IN = COL_EIGHT[0] + ROW_EIGHT[1]
+EIGHT_MID = ROW_EIGHT[0] + [[g[3 * p % 8] for p in range(8)] for g in COL_EIGHT[1]]
+PAIR_IN = COL_PAIR[0] + ROW_PAIR[1]
+PAIR_MID = ROW_PAIR[0] + COL_PAIR[1]
 
 
 def dot(a, b, contract):
@@ -67,42 +67,44 @@
     extra = 32 - share
     n = 16
     first = lax.axis_index("core") == 0
+    out_side = lax.axis_index("core") == 1
     zh, zl = lax.axis_index("zh"), lax.axis_index("zl")
 
     acts = jnp.concatenate([inputs, basis_out[:extra]], axis=0)
     grads = jnp.pad(out_grads, ((0, 64 - block), (0, 0)))
     grads = jnp.concatenate([grads[:32], grads[32:]], axis=1)
-    kept = jnp.where(first, grads, acts)
+    kept = jnp.where(out_side, grads, acts)
     far = jnp.where(
-        first, jnp.concatenate([acts, wide(basis_in)], axis=0), jnp.concatenate([grads, basis_out], axis=0)
+        out_side, jnp.concatenate([acts, wide(basis_in)], axis=0), jnp.concatenate([grads, basis_out], axis=0)
     )
-    far = lax.ppermute(far, "core", SWAP)
+    far = lax.all_gather(far, "core")
+    far = jnp.where(first, far[1], far[0])
     far, basis_far = far[:32], far[32:]
     lanes = [[p[:, :half], p[:, half:]] for p in (kept, far)]
     as_grads = jnp.concatenate([jnp.concatenate(p, axis=0) for p in lanes], axis=1)
-    as_acts = jnp.concatenate([far[:share], kept[:share], far[share:], kept[share:]], axis=0)
-    rows = jnp.where(first, as_grads, as_acts)
+    as_acts = jnp.concatenate([kept[:share], far[:share], kept[share:], far[share:]], axis=0)
+    rows = jnp.where(out_side, as_grads, as_acts)
 
     rows = both(rows, PAIR_IN)
     basis = jnp.where(
-        first,
+        out_side,
         jnp.concatenate([basis_out, basis_far], axis=0),
-        jnp.concatenate([tall(basis_far), basis_in], axis=1),
+        jnp.concatenate([basis_in, tall(basis_far)], axis=1),
     )
 
     parity = jnp.where(jnp.arange(tokens) % 2 == 0, 1.0, -1.0)
     token = lax.broadcasted_iota(jnp.int32, (1, tokens), 1)
     sign = jnp.sum(jnp.where(pair_order[:, None] == token, parity[:, None], 0.0), axis=0)
     weights = sign / jnp.sqrt((1.0 + length_bucket.astype(F32)) * tokens)
-    weights = jnp.where(first, weights, 1.0)
+    weights = jnp.where(out_side, weights, 1.0)
     eig3 = jnp.concatenate([*three(eig_in), jnp.zeros((half,), BF)]).reshape(2, 2 * half)
     later = jnp.concatenate([wide(basis_in), jnp.pad(eig3, ((0, 14), (0, 0)))], axis=0)
-    low = jnp.where(first, zh, zl // 2) == 0
+    low = jnp.where(out_side, zh, zl // 2) == 0
     rows, basis, weights, later, low = lax.optimization_barrier((rows, basis, weights, later, low))
     rows = exchange(copies(rows, 8), EIGHT_IN)
     ordered = rows[:, :, :block].reshape(tokens, -1)
     paired = rows.reshape(4, 2, 2, 64, -1).swapaxes(1, 2)[:, :, :, :block].reshape(tokens, -1)
-    part = dot(basis, jnp.where(first, paired, ordered), ((0,), (1,))).astype(BF)
+    part = dot(basis, jnp.where(out_side, paired, ordered), ((0,), (1,))).astype(BF)
     part = exchange(part.reshape(8, -1, tokens), EIGHT_MID)
     part, rows = lax.optimization_barrier((part, rows))
     total = jnp.sum(part.astype(F32), axis=0)
@@ -113,32 +115,32 @@
         rows[:, :, block + k * extra : block + (k + 1) * extra].swapaxes(0, 1).reshape(n * extra, -1)
         for k in range(2)
     )
-    packed = jnp.concatenate([slab0, later], axis=0)
+    packed = jnp.concatenate([slab1, later], axis=0)
     rot = ((total + total_far.astype(F32)) * weights).astype(BF)
-    rot, packed, slab1 = lax.optimization_barrier((rot, packed, slab1))
+    rot, packed, slab0 = lax.optimization_barrier((rot, packed, slab0))
     rot = exchange(copies(rot, 8), EIGHT_MID).reshape(-1, tokens)
     rot, packed = lax.optimization_barrier((rot, packed))
     rot_far = lax.ppermute(rot, "core", SWAP)
     far = lax.ppermute(packed, "core", SWAP)
     rot_far, far = lax.optimization_barrier((rot_far, far))
-    slab = jnp.where(first, far[: slab1.shape[0]], slab1)
+    slab = jnp.where(out_side, far[: slab0.shape[0]], slab0)
     eig_far = far[-16:-14].astype(F32).reshape(4, half)
     eig_far = eig_far[0] + eig_far[1] + eig_far[2]
     eig_in2 = jnp.where(first, jnp.concatenate([eig_in, eig_far]), jnp.concatenate([eig_far, eig_in]))
-    in_far = tall(far[slab1.shape[0] : -16])
+    in_far = tall(far[slab0.shape[0] : -16])
     basis_in2 = jnp.where(
         first, jnp.concatenate([basis_in, in_far], axis=1), jnp.concatenate([in_far, basis_in], axis=1)
     )
 
     middle = dot(rot, rot_far, ((1,), (1,)))
-    down, across = jnp.where(first, eig_out, eig_in2), jnp.where(first, eig_in2, eig_out)
+    down, across = jnp.where(out_side, eig_out, eig_in2), jnp.where(out_side, eig_in2, eig_out)
     scaled = (middle / (down[:, None] * across[None, :] + DAMPING)).astype(BF)
-    left = jnp.where(first, dot(slab, scaled, ((1,), (0,))), dot(slab, scaled, ((1,), (1,))))
+    left = jnp.where(out_side, dot(slab, scaled, ((1,), (0,))), dot(slab, scaled, ((1,), (1,))))
 
     left, basis_in2 = lax.optimization_barrier((left, basis_in2))
-    left = lax.all_to_all(left.reshape(n, -1, left.shape[1]), ("x", "zl"), 0, 0, tiled=True)
-    left = jnp.sum(left, axis=0).astype(BF)
-    left = lax.all_to_all(copies(left, n), ("x", "zl"), 0, 0, tiled=True)
+    left = exchange(left.reshape(8, -1, left.shape[1]), ROW_EIGHT[0] + ROW_EIGHT[1])
+    left = both(jnp.sum(left, axis=0), ROW_PAIR[0] + ROW_PAIR[1])
+    left = exchange(copies((left[0] + left[1]).astype(BF), 8), ROW_EIGHT[0] + ROW_EIGHT[1])
     left = left.reshape(-1, left.shape[2])
     final = dot(left, basis_in2, ((1,), (1,)))
     final = exchange(final.reshape(n, -1, final.shape[1]), COL_ALL[0] + COL_ALL[1])

time: 142 us -> 140 us (0.986)
  the two profiles are of different devices: /device:TPU:1 before, /device:TPU:8 now
where the time goes in v9:
time: 140 us; the launch traced here: 139 us
  blocking collectives  125 us (89%)
  starting transfers between devices  4.32 us (3%)
  local copies, waits for them, and re-layouts  3.8 us (3%)
  other arithmetic  2.8 us (2%)
  matrix products  2.25 us (2%)
    all_to_all x6, blocking collectives, exchange(): lax.all_to_all(parts, AXES, 0, 0, axis_index_groups=groups, tiled=True)  96.2 us
    all_gather x3, blocking collectives, both(): return lax.all_gather(block, AXES, axis_index_groups=groups)  26.2 us
  transfers between devices with their start and end apart: 2, of which 1 were waited for; matrix products, arithmetic and copies ran while one was open for 0% of the time, Pallas kernels for 0%

profile of v9, /device:TPU:8, one launch (start us, length us, event | category | flops | bytes accessed | tf_op | source)
XLA Modules:
  0.0 139.5 jit_solution(16534235140483954094)
XLA Ops:
  0.0 0.8 fusion.23
  0.8 0.7 fusion.26
  1.5 0.8 maximum_select_fusion.2
  2.3 1.0 fusion.24
  3.4 2.2 %all_gather.18 = bf16[2,288,512]{2,1,0:T(8,128)(2,1)S(1)} all-gather(bf16[1,288,512]{2,1,0:T(8,128)(2,1)S(1)} %maximum_select_fusion), channel_id=1, replica_groups=mesh['x'=4,'zl'=4,'y'=8,'zh'=2,'core'=2] {'core'}, dimensions={0}, use_global_device_ids=true | all-gather | bytes 884736 | tf_op jit(solution)/shard_map/all_gather | solution.py:80
  5.9 0.5 copy-done.5
  6.5 12.1 %all_gather.19 = bf16[2,64,512]{2,1,0:T(8,128)(2,1)S(1)} all-gather(bf16[1,64,512]{2,1,0:T(8,128)(2,1)S(1)} %maximum_select_fusion.1), channel_id=1, replica_groups={{0,2},{4,6},{8,10},{12,14},{16,18},{20,22},{24,26},{28,30},{32,34},{36,..., dimensions={0}, use_global_device_ids=true | all-gather | bytes 196608 | tf_op jit(solution)/shard_map/all_gather | solution.py:39
  18.7 0.4 select_reduce_fusion
  19.1 0.1 fusion.2
  19.3 0.1 broadcast_in_dim.55
  19.4 25.2 %all_to_all.30 = bf16[8,2,64,512]{3,2,1,0:T(8,128)(2,1)S(1)} all-to-all(bf16[8,2,64,512]{3,2,1,0:T(8,128)(2,1)S(1)} %broadcast_in_dim.55), channel_id=1, replica_groups={{0,4,8,12,16,20,24,28},{2,6,10,14,18,22,26,30},{32,36,40,44,48,52,56,60..., dimensions={0} | all-to-all | bytes 2097152 | tf_op jit(solution)/shard_map/all_to_all | solution.py:35
  44.8 0.2 bitcast_select_fusion
  45.1 0.8 convolution_convert_fusion
  45.8 18.8 %all_to_all.31 = bf16[8,64,896]{2,1,0:T(8,128)(2,1)S(1)} all-to-all(bf16[8,64,896]{2,1,0:T(8,128)(2,1)S(1)} %bitcast.48), channel_id=1, replica_groups={{0,32,128,160,256,288,384,416},{2,34,130,162,258,290,386,418},{4,36,132..., dimensions={0} | all-to-all | bytes 1835008 | tf_op jit(solution)/shard_map/all_to_all | solution.py:35
  64.6 0.1 convert_reduce_fusion
  64.8 8.8 %all-gather = bf16[128,896]{1,0:T(8,128)(2,1)S(1)} all-gather(bf16[64,896]{1,0:T(8,128)(2,1)S(1)} %convert_element_type.58), channel_id=2, replica_groups={{0,64},{2,66},{4,68},{6,70},{8,72},{10,74},{12,76},{14,78},{16,80},{18,..., dimensions={0}, use_global_device_ids=true | all-gather | bytes 344064 | tf_op jit(solution)/shard_map/all_gather | solution.py:39
  73.8 0.1 broadcast_in_dim.56
  73.9 13.3 %all_to_all.32 = bf16[8,64,896]{2,1,0:T(8,128)(2,1)S(1)} all-to-all(bf16[8,64,896]{2,1,0:T(8,128)(2,1)S(1)} %broadcast_in_dim.56), channel_id=1, replica_groups={{0,32,128,160,256,288,384,416},{2,34,130,162,258,290,386,418},{4,36,132..., dimensions={0} | all-to-all | bytes 1835008 | tf_op jit(solution)/shard_map/all_to_all | solution.py:35
  87.2 1.9 %collective-permute-start = (bf16[512,896]{1,0:T(8,128)(2,1)S(1)}, bf16[512,896]{1,0:T(8,128)(2,1)S(1)}, u32[]{:S(2)}, u32[]{:S(2)}) collective-permute-start(bf16[512,896]{1,0:T(8,128)(2,1)S(1)} %bitcast.46), channel_id=1, source_target_pairs={{0,1},{1,0},{2,3},{3,2},{4,5},{5,4},{6,7},{7,6},{8,9},{9,8},{10,11... | collective-permute-start | bytes 2752520 | tf_op jit(solution)/shard_map/ppermute | solution.py:123
  89.2 2.4 %collective-permute-start.1 = (bf16[336,512]{1,0:T(8,128)(2,1)S(1)}, bf16[336,512]{1,0:T(8,128)(2,1)S(1)}, u32[]{:S(2)}, u32[]{:S(2)}) collective-permute-start(bf16[336,512]{1,0:T(8,128)(2,1)S(1)} %pad_maximum_fusion.2), channel_id=1, source_target_pairs={{0,1},{1,0},{2,3},{3,2},{4,5},{5,4},{6,7},{7,6},{8,9},{9,8},{10,11... | collective-permute-start | bytes 1032200 | tf_op jit(solution)/shard_map/ppermute | solution.py:124
  91.6 1.3 collective-permute-done.1
  92.9 0.7 fusion
  93.7 0.2 fusion.11
  93.9 0.3 convolution_select_fusion
  94.1 0.1 fusion.3
  94.3 9.2 %all_to_all.33 = f32[8,8,512]{2,1,0:T(8,128)S(1)} all-to-all(f32[8,8,512]{2,1,0:T(8,128)S(1)} %bitcast.49), channel_id=1, replica_groups={{0,32,128,160,256,288,384,416},{2,34,130,162,258,290,386,418},{4,36,132..., dimensions={0} | all-to-all | bytes 262144 | tf_op jit(solution)/shard_map/all_to_all | solution.py:35
  103.5 5.3 %all-gather.1 = f32[16,512]{1,0:T(8,128)S(1)} all-gather(f32[8,512]{1,0:T(8,128)S(1)} %reduce_sum.38), channel_id=3, replica_groups={{0,64},{2,66},{4,68},{6,70},{8,72},{10,74},{12,76},{14,78},{16,80},{18,..., dimensions={0}, use_global_device_ids=true | all-gather | bytes 49152 | tf_op jit(solution)/shard_map/all_gather | solution.py:39
  108.8 8.8 %all_to_all.34 = bf16[8,8,512]{2,1,0:T(8,128)(2,1)S(1)} all-to-all(bf16[8,8,512]{2,1,0:T(8,128)(2,1)S(1)} %broadcast_in_dim.58), channel_id=1, replica_groups={{0,32,128,160,256,288,384,416},{2,34,130,162,258,290,386,418},{4,36,132..., dimensions={0} | all-to-all | bytes 131072 | tf_op jit(solution)/shard_map/all_to_all | solution.py:35
  117.6 0.3 fusion.4
  117.9 0.1 copy.25
  118.0 20.9 %all_to_all.35 = f32[16,4,512]{2,1,0:T(4,128)S(1)} all-to-all(f32[16,4,512]{2,1,0:T(4,128)S(1)} %copy.25), channel_id=1, replica_groups={{0,4,8,12,16,20,24,28,2,6,10,14,18,22,26,30},{32,36,40,44,48,52,56,60,3..., dimensions={0} | all-to-all | bytes 262144 | tf_op jit(solution)/shard_map/all_to_all | solution.py:35
  138.9 0.6 reduce_sum.39
  (56 shorter events, 0.9 us)
Async XLA Ops:
  0.0 3.3 %copy-start.1 = (bf16[256,512]{1,0:T(8,128)(2,1)S(1)}, bf16[256,512]{1,0:T(8,128)(2,1)}, u32[]{:S(2)}) copy-start(bf16[256,512]{1,0:T(8,128)(2,1)} %param.10) | copy-start | bytes 786436
  0.0 3.3 %copy-start.2 = (bf16[28,512]{1,0:T(8,128)(2,1)S(1)}, bf16[28,512]{1,0:T(8,128)(2,1)}, u32[]{:S(2)}) copy-start(bf16[28,512]{1,0:T(8,128)(2,1)} %param.9) | copy-start | bytes 86020
  5.7 0.7 copy-start.5
  5.8 12.9 %copy-start.3 = (s32[896]{0:T(1024)S(1)}, s32[896]{0:T(1024)}, u32[]{:S(2)}) copy-start(s32[896]{0:T(1024)} %param.14) | copy-start | bytes 10756
  5.8 13.3 %copy-start.4 = (s32[896]{0:T(1024)S(1)}, s32[896]{0:T(1024)}, u32[]{:S(2)}) copy-start(s32[896]{0:T(1024)} %param.15) | copy-start | bytes 10756
  5.8 13.3 %copy-start = (bf16[512,256]{1,0:T(8,128)(2,1)S(1)}, bf16[512,256]{1,0:T(8,128)(2,1)}, u32[]{:S(2)}) copy-start(bf16[512,256]{1,0:T(8,128)(2,1)} %param.11) | copy-start | bytes 786436
  73.9 19.0 %copy-start.6 = (f32[512]{0:T(512)S(1)}, f32[512]{0:T(512)}, u32[]{:S(2)}) copy-start(f32[512]{0:T(512)} %param.12) | copy-start | bytes 6148
  87.2 5.6 %collective-permute-start = (bf16[512,896]{1,0:T(8,128)(2,1)S(1)}, bf16[512,896]{1,0:T(8,128)(2,1)S(1)}, u32[]{:S(2)}, u32[]{:S(2)}) collective-permute-start(bf16[512,896]{1,0:T(8,128)(2,1)S(1)} %bitcast.46), channel_id=1, source_target_pairs={{0,1},{1,0},{2,3},{3,2},{4,5},{5,4},{6,7},{7,6},{8,9},{9,8},{10,11... | collective-permute-start | bytes 2752520 | tf_op jit(solution)/shard_map/ppermute | solution.py:123
  89.2 3.7 %collective-permute-start.1 = (bf16[336,512]{1,0:T(8,128)(2,1)S(1)}, bf16[336,512]{1,0:T(8,128)(2,1)S(1)}, u32[]{:S(2)}, u32[]{:S(2)}) collective-permute-start(bf16[336,512]{1,0:T(8,128)(2,1)S(1)} %pad_maximum_fusion.2), channel_id=1, source_target_pairs={{0,1},{1,0},{2,3},{3,2},{4,5},{5,4},{6,7},{7,6},{8,9},{9,8},{10,11... | collective-permute-start | bytes 1032200 | tf_op jit(solution)/shard_map/ppermute | solution.py:124

commit v10 on v9

--- a/solution.py
+++ b/solution.py
@@ -19,6 +19,7 @@
 
 
 ROW_PAIR, ROW_EIGHT = lists((5, 0, 2, 3, 4, 1), 2), lists((5, 1, 3, 4, 0, 2), 8)
+NEAR_PAIR, NEAR_EIGHT = lists((5, 0, 1, 3, 4, 2), 2), lists((5, 2, 3, 4, 0, 1), 8)
 COL_PAIR, COL_EIGHT = lists((5, 0, 1, 2, 3, 4), 2), lists((5, 0, 1, 2, 4, 3), 8)
 COL_ALL = lists((5, 0, 1, 2, 4, 3), 16)
 EIGHT_IN = COL_EIGHT[0] + ROW_EIGHT[1]
@@ -138,9 +139,9 @@
     left = jnp.where(out_side, dot(slab, scaled, ((1,), (0,))), dot(slab, scaled, ((1,), (1,))))
 
     left, basis_in2 = lax.optimization_barrier((left, basis_in2))
-    left = exchange(left.reshape(8, -1, left.shape[1]), ROW_EIGHT[0] + ROW_EIGHT[1])
-    left = both(jnp.sum(left, axis=0), ROW_PAIR[0] + ROW_PAIR[1])
-    left = exchange(copies((left[0] + left[1]).astype(BF), 8), ROW_EIGHT[0] + ROW_EIGHT[1])
+    left = exchange(left.reshape(8, -1, left.shape[1]), NEAR_EIGHT[0] + NEAR_EIGHT[1])
+    left = both(jnp.sum(left, axis=0), NEAR_PAIR[0] + NEAR_PAIR[1])
+    left = exchange(copies((left[0] + left[1]).astype(BF), 8), NEAR_EIGHT[0] + NEAR_EIGHT[1])
     left = left.reshape(-1, left.shape[2])
     final = dot(left, basis_in2, ((1,), (1,)))
     final = exchange(final.reshape(n, -1, final.shape[1]), COL_ALL[0] + COL_ALL[1])

time: 140 us -> 144 us (1.029)
  blocking collectives: 125 us -> 129 us
    all_to_all x6, blocking collectives: 96.2 us -> 101 us  [exchange(): lax.all_to_all(parts, AXES, 0, 0, axis_index_groups=groups, tiled=True)]
where the time goes in v10:
time: 144 us
  blocking collectives  129 us (90%)
  starting transfers between devices  4.32 us (3%)
  local copies, waits for them, and re-layouts  3.81 us (3%)
  other arithmetic  2.8 us (2%)
  matrix products  2.25 us (2%)
    all_to_all x6, blocking collectives, exchange(): lax.all_to_all(parts, AXES, 0, 0, axis_index_groups=groups, tiled=True)  101 us
    all_gather x3, blocking collectives, both(): return lax.all_gather(block, AXES, axis_index_groups=groups)  25.3 us
  transfers between devices with their start and end apart: 2, of which 1 were waited for; matrix products, arithmetic and copies ran while one was open for 0% of the time, Pallas kernels for 0%

profile of v10, /device:TPU:8, one launch (start us, length us, event | category | flops | bytes accessed | tf_op | source)
XLA Modules:
  0.0 143.7 jit_solution(706278055420588391)
XLA Ops:
  0.0 0.8 fusion.23
  0.8 0.7 fusion.26
  1.5 0.8 maximum_select_fusion.2
  2.3 1.0 fusion.24
  3.4 2.2 %all_gather.18 = bf16[2,288,512]{2,1,0:T(8,128)(2,1)S(1)} all-gather(bf16[1,288,512]{2,1,0:T(8,128)(2,1)S(1)} %maximum_select_fusion), channel_id=1, replica_groups=mesh['x'=4,'zl'=4,'y'=8,'zh'=2,'core'=2] {'core'}, dimensions={0}, use_global_device_ids=true | all-gather | bytes 884736 | tf_op jit(solution)/shard_map/all_gather | solution.py:81
  5.9 0.5 copy-done.5
  6.5 12.1 %all_gather.19 = bf16[2,64,512]{2,1,0:T(8,128)(2,1)S(1)} all-gather(bf16[1,64,512]{2,1,0:T(8,128)(2,1)S(1)} %maximum_select_fusion.1), channel_id=1, replica_groups={{0,2},{4,6},{8,10},{12,14},{16,18},{20,22},{24,26},{28,30},{32,34},{36,..., dimensions={0}, use_global_device_ids=true | all-gather | bytes 196608 | tf_op jit(solution)/shard_map/all_gather | solution.py:40
  18.7 0.4 select_reduce_fusion
  19.1 0.1 fusion.2
  19.3 0.1 broadcast_in_dim.55
  19.4 25.2 %all_to_all.30 = bf16[8,2,64,512]{3,2,1,0:T(8,128)(2,1)S(1)} all-to-all(bf16[8,2,64,512]{3,2,1,0:T(8,128)(2,1)S(1)} %broadcast_in_dim.55), channel_id=1, replica_groups={{0,4,8,12,16,20,24,28},{2,6,10,14,18,22,26,30},{32,36,40,44,48,52,56,60..., dimensions={0} | all-to-all | bytes 2097152 | tf_op jit(solution)/shard_map/all_to_all | solution.py:36
  44.8 0.2 bitcast_select_fusion
  45.1 0.8 convolution_convert_fusion
  45.8 18.8 %all_to_all.31 = bf16[8,64,896]{2,1,0:T(8,128)(2,1)S(1)} all-to-all(bf16[8,64,896]{2,1,0:T(8,128)(2,1)S(1)} %bitcast.48), channel_id=1, replica_groups={{0,32,128,160,256,288,384,416},{2,34,130,162,258,290,386,418},{4,36,132..., dimensions={0} | all-to-all | bytes 1835008 | tf_op jit(solution)/shard_map/all_to_all | solution.py:36
  64.6 0.1 convert_reduce_fusion
  64.8 8.8 %all-gather = bf16[128,896]{1,0:T(8,128)(2,1)S(1)} all-gather(bf16[64,896]{1,0:T(8,128)(2,1)S(1)} %convert_element_type.58), channel_id=2, replica_groups={{0,64},{2,66},{4,68},{6,70},{8,72},{10,74},{12,76},{14,78},{16,80},{18,..., dimensions={0}, use_global_device_ids=true | all-gather | bytes 344064 | tf_op jit(solution)/shard_map/all_gather | solution.py:40
  73.8 0.1 broadcast_in_dim.56
  73.9 13.3 %all_to_all.32 = bf16[8,64,896]{2,1,0:T(8,128)(2,1)S(1)} all-to-all(bf16[8,64,896]{2,1,0:T(8,128)(2,1)S(1)} %broadcast_in_dim.56), channel_id=1, replica_groups={{0,32,128,160,256,288,384,416},{2,34,130,162,258,290,386,418},{4,36,132..., dimensions={0} | all-to-all | bytes 1835008 | tf_op jit(solution)/shard_map/all_to_all | solution.py:36
  87.2 1.9 %collective-permute-start = (bf16[512,896]{1,0:T(8,128)(2,1)S(1)}, bf16[512,896]{1,0:T(8,128)(2,1)S(1)}, u32[]{:S(2)}, u32[]{:S(2)}) collective-permute-start(bf16[512,896]{1,0:T(8,128)(2,1)S(1)} %bitcast.46), channel_id=1, source_target_pairs={{0,1},{1,0},{2,3},{3,2},{4,5},{5,4},{6,7},{7,6},{8,9},{9,8},{10,11... | collective-permute-start | bytes 2752520 | tf_op jit(solution)/shard_map/ppermute | solution.py:124
  89.2 2.4 %collective-permute-start.1 = (bf16[336,512]{1,0:T(8,128)(2,1)S(1)}, bf16[336,512]{1,0:T(8,128)(2,1)S(1)}, u32[]{:S(2)}, u32[]{:S(2)}) collective-permute-start(bf16[336,512]{1,0:T(8,128)(2,1)S(1)} %pad_maximum_fusion.2), channel_id=1, source_target_pairs={{0,1},{1,0},{2,3},{3,2},{4,5},{5,4},{6,7},{7,6},{8,9},{9,8},{10,11... | collective-permute-start | bytes 1032200 | tf_op jit(solution)/shard_map/ppermute | solution.py:125
  91.6 1.3 collective-permute-done.1
  92.9 0.7 fusion
  93.7 0.2 fusion.11
  93.9 0.3 convolution_select_fusion
  94.1 0.1 fusion.3
  94.3 13.3 %all_to_all.33 = f32[8,8,512]{2,1,0:T(8,128)S(1)} all-to-all(f32[8,8,512]{2,1,0:T(8,128)S(1)} %bitcast.49), channel_id=1, replica_groups={{0,64,128,192,256,320,384,448},{2,66,130,194,258,322,386,450},{4,68,132..., dimensions={0} | all-to-all | bytes 262144 | tf_op jit(solution)/shard_map/all_to_all | solution.py:36
  107.6 4.4 %all-gather.1 = f32[16,512]{1,0:T(8,128)S(1)} all-gather(f32[8,512]{1,0:T(8,128)S(1)} %reduce_sum.38), channel_id=3, replica_groups={{0,32},{2,34},{4,36},{6,38},{8,40},{10,42},{12,44},{14,46},{16,48},{18,..., dimensions={0}, use_global_device_ids=true | all-gather | bytes 49152 | tf_op jit(solution)/shard_map/all_gather | solution.py:40
  112.1 9.9 %all_to_all.34 = bf16[8,8,512]{2,1,0:T(8,128)(2,1)S(1)} all-to-all(bf16[8,8,512]{2,1,0:T(8,128)(2,1)S(1)} %broadcast_in_dim.58), channel_id=1, replica_groups={{0,64,128,192,256,320,384,448},{2,66,130,194,258,322,386,450},{4,68,132..., dimensions={0} | all-to-all | bytes 131072 | tf_op jit(solution)/shard_map/all_to_all | solution.py:36
  122.0 0.3 fusion.4
  122.2 0.1 copy.25
  122.3 20.7 %all_to_all.35 = f32[16,4,512]{2,1,0:T(4,128)S(1)} all-to-all(f32[16,4,512]{2,1,0:T(4,128)S(1)} %copy.25), channel_id=1, replica_groups={{0,4,8,12,16,20,24,28,2,6,10,14,18,22,26,30},{32,36,40,44,48,52,56,60,3..., dimensions={0} | all-to-all | bytes 262144 | tf_op jit(solution)/shard_map/all_to_all | solution.py:36
  143.1 0.6 reduce_sum.39
  (56 shorter events, 0.9 us)
Async XLA Ops:
  0.0 3.3 %copy-start.1 = (bf16[256,512]{1,0:T(8,128)(2,1)S(1)}, bf16[256,512]{1,0:T(8,128)(2,1)}, u32[]{:S(2)}) copy-start(bf16[256,512]{1,0:T(8,128)(2,1)} %param.10) | copy-start | bytes 786436
  0.0 3.3 %copy-start.2 = (bf16[28,512]{1,0:T(8,128)(2,1)S(1)}, bf16[28,512]{1,0:T(8,128)(2,1)}, u32[]{:S(2)}) copy-start(bf16[28,512]{1,0:T(8,128)(2,1)} %param.9) | copy-start | bytes 86020
  5.7 0.7 copy-start.5
  5.8 12.9 %copy-start.3 = (s32[896]{0:T(1024)S(1)}, s32[896]{0:T(1024)}, u32[]{:S(2)}) copy-start(s32[896]{0:T(1024)} %param.14) | copy-start | bytes 10756
  5.8 13.3 %copy-start.4 = (s32[896]{0:T(1024)S(1)}, s32[896]{0:T(1024)}, u32[]{:S(2)}) copy-start(s32[896]{0:T(1024)} %param.15) | copy-start | bytes 10756
  5.8 13.3 %copy-start = (bf16[512,256]{1,0:T(8,128)(2,1)S(1)}, bf16[512,256]{1,0:T(8,128)(2,1)}, u32[]{:S(2)}) copy-start(bf16[512,256]{1,0:T(8,128)(2,1)} %param.11) | copy-start | bytes 786436
  73.9 19.0 %copy-start.6 = (f32[512]{0:T(512)S(1)}, f32[512]{0:T(512)}, u32[]{:S(2)}) copy-start(f32[512]{0:T(512)} %param.12) | copy-start | bytes 6148
  87.2 5.6 %collective-permute-start = (bf16[512,896]{1,0:T(8,128)(2,1)S(1)}, bf16[512,896]{1,0:T(8,128)(2,1)S(1)}, u32[]{:S(2)}, u32[]{:S(2)}) collective-permute-start(bf16[512,896]{1,0:T(8,128)(2,1)S(1)} %bitcast.46), channel_id=1, source_target_pairs={{0,1},{1,0},{2,3},{3,2},{4,5},{5,4},{6,7},{7,6},{8,9},{9,8},{10,11... | collective-permute-start | bytes 2752520 | tf_op jit(solution)/shard_map/ppermute | solution.py:124
  89.2 3.7 %collective-permute-start.1 = (bf16[336,512]{1,0:T(8,128)(2,1)S(1)}, bf16[336,512]{1,0:T(8,128)(2,1)S(1)}, u32[]{:S(2)}, u32[]{:S(2)}) collective-permute-start(bf16[336,512]{1,0:T(8,128)(2,1)S(1)} %pad_maximum_fusion.2), channel_id=1, source_target_pairs={{0,1},{1,0},{2,3},{3,2},{4,5},{5,4},{6,7},{7,6},{8,9},{9,8},{10,11... | collective-permute-start | bytes 1032200 | tf_op jit(solution)/shard_map/ppermute | solution.py:125
